TPU v7x, 32 devices: a whole 2x2x4 slice. The times are simulated.
32 devices in a mesh: rcv: 8 (over z, y), hd: 4 (over x, core).
Axes of the slice: x: 2, y: 2, z: 4, core: 2. Of those that a mesh axis runs over, the one named last changes fastest.
Arguments:
- stream: bfloat16 [4096, 1024], P(('rcv', 'hd')), may hold values from -3 to 3
- queries: bfloat16 [4096, 1024], P(('rcv', 'hd')), may hold values from -9 to 9
- keys: bfloat16 [4096, 1024], P(('rcv', 'hd')), may hold values from -9 to 9
- values: bfloat16 [4096, 1024], P(('rcv', 'hd')), may hold values from -6 to 6
- out_proj: bfloat16 [1024, 1024], replicated, may hold values from -0.375 to 0.375
- norm_gain: float32 [1024], replicated, may hold values from 0.5 to 1.5
- expert_weights: bfloat16 [1024, 16, 3, 512], P(None, 'rcv'), may hold values from -0.1875 to 0.1875
- expert_ids: int32 [4096, 4], P(('rcv', 'hd')), may hold values from 0 to 15, as said below
- gate_weights: float32 [4096, 4], P(('rcv', 'hd')), may hold values from 0.1 to 1
- out_cotangent: bfloat16 [4096, 1024], P(('rcv', 'hd')), may hold values from -6 to 6
Outputs:
- block_out: bfloat16 [4096, 1024], P(('rcv', 'hd'))
- stream_grad: bfloat16 [4096, 1024], P(('rcv', 'hd'))
Inputs may be any that keep to these rules, and one draw needn't show every extreme that they name: `expert_ids`: each token names 4 different experts; its k-th id lies in k * 4 to (k + 1) * 4 - 1. Within each aligned block of 128 rows no expert is named more than 40 times, and in each of these 4 ranges one expert, the same for all blocks, is named exactly 40 times in every block.
All inputs are finite; a program needn't handle non-finite values.
Results may differ from a plain program's by a relative error of at most 0.015.
Values may be sent and summed in bfloat16 or wider, within the bound.
No kernel may reach another device: no remote copies, remote signals or barrier semaphores. Data moves between devices by JAX's collectives and lax.ppermute only.
A program may use at most 128 MiB of HBM per device.

v0:
```python
import math

import jax
import jax.numpy as jnp
from jax import lax
from jax.sharding import PartitionSpec as P

HS = 64


NORM_EPS = 1e-06


def silu_parts(pre_gate):
    sigmoid = 1.0 / (1.0 + jnp.exp(-pre_gate))
    return (pre_gate * sigmoid, sigmoid * (1.0 + pre_gate * (1.0 - sigmoid)))


def expert_pass(arrived_rows, arrived_cot, expert_weights):
    pre_pair = jnp.einsum(
        "jmd,djcf->jmcf", arrived_rows, expert_weights[:, :, :2], preferred_element_type=jnp.float32
    )
    activated, act_slope = silu_parts(pre_pair[:, :, 0])
    up_value = pre_pair[:, :, 1]
    hidden = (activated * up_value).astype(jnp.bfloat16)
    expert_outs = jnp.einsum(
        "jmf,djf->jmd", hidden, expert_weights[:, :, 2], preferred_element_type=jnp.float32
    ).astype(jnp.bfloat16)
    back_hidden = jnp.einsum(
        "jmd,djf->jmf", arrived_cot, expert_weights[:, :, 2], preferred_element_type=jnp.float32
    )
    hidden_grads = jnp.stack(
        [back_hidden * up_value * act_slope, back_hidden * activated], axis=2
    ).astype(jnp.bfloat16)
    expert_grads = jnp.einsum(
        "jmcf,djcf->jmd", hidden_grads, expert_weights[:, :, :2], preferred_element_type=jnp.float32
    ).astype(jnp.bfloat16)
    return (expert_outs, expert_grads)


def per_device(
    stream,
    queries,
    keys,
    values,
    out_proj,
    norm_gain,
    expert_weights,
    expert_ids,
    gate_weights,
    out_cotangent,
):
    row_count, feature_width = stream.shape
    groups = lax.axis_size("rcv")
    local_count = expert_weights.shape[1]
    experts = local_count * groups
    top_count = expert_ids.shape[1]
    capacity = (5 * row_count * top_count + 4 * experts - 1) // (4 * experts)
    score_scale = 1.0 / math.sqrt(HS)
    flat_ids = expert_ids.reshape(-1)
    onehot = (flat_ids[:, None] == jnp.arange(experts, dtype=jnp.int32)[None, :]).astype(jnp.int32)
    slot_index = jnp.sum((jnp.cumsum(onehot, axis=0) - onehot) * onehot, axis=1)
    owner_rank = flat_ids // local_count
    local_expert = flat_ids % local_count
    cell_index = (local_expert * groups + owner_rank) * capacity + slot_index
    cell_total = experts * capacity
    token_index = jnp.arange(row_count * top_count, dtype=jnp.int32) // top_count
    source = jnp.full((cell_total,), row_count, jnp.int32).at[cell_index].set(token_index)

    def pack_rows(row_data):
        padded = jnp.concatenate([row_data, jnp.zeros((1, feature_width), row_data.dtype)], axis=0)
        return jnp.take(padded, source, axis=0).reshape(
            local_count, groups, capacity, feature_width
        )

    query_all, key_all, value_all = (
        lax.all_to_all(queries, "hd", split_axis=1, concat_axis=0, tiled=True),
        lax.all_to_all(keys, "hd", split_axis=1, concat_axis=0, tiled=True),
        lax.all_to_all(values, "hd", split_axis=1, concat_axis=0, tiled=True),
    )
    length = query_all.shape[0]
    head_count = query_all.shape[1] // HS
    block_rows = math.gcd(length, 512)
    key_heads = key_all.reshape(length, head_count, HS)
    value_heads = value_all.reshape(length, head_count, HS)

    def one_block(row_start):
        query_block = lax.dynamic_slice_in_dim(query_all, row_start, block_rows, 0).reshape(
            block_rows, head_count, HS
        )
        scores = (
            jnp.einsum("qhd,khd->hqk", query_block, key_heads, preferred_element_type=jnp.float32)
            * score_scale
        )
        row_max = jnp.max(scores, axis=2, keepdims=True)
        raw_weights = jnp.exp(scores - row_max)
        row_total = jnp.sum(raw_weights, axis=2)
        mixed_heads = jnp.einsum(
            "hqk,khd->qhd",
            raw_weights.astype(jnp.bfloat16),
            value_heads,
            preferred_element_type=jnp.float32,
        )
        result = mixed_heads / jnp.transpose(row_total)[:, :, None]
        return result.astype(jnp.bfloat16).reshape(block_rows, head_count * HS)

    starts = jnp.arange(length // block_rows, dtype=jnp.int32) * block_rows
    head_result = lax.map(one_block, starts).reshape(length, head_count * HS)
    attended = lax.all_to_all(head_result, "hd", split_axis=0, concat_axis=1, tiled=True)
    projected = jnp.dot(attended, out_proj, preferred_element_type=jnp.float32)
    mix_stream = (stream.astype(jnp.float32) + projected).astype(jnp.bfloat16)
    stream_wide = mix_stream.astype(jnp.float32)
    inverse = lax.rsqrt(jnp.mean(stream_wide * stream_wide, axis=1, keepdims=True) + NORM_EPS)
    normed = (norm_gain * stream_wide * inverse).astype(jnp.bfloat16)
    arrived_rows, arrived_cot = (
        lax.all_to_all(pack_rows(normed), "rcv", split_axis=1, concat_axis=1, tiled=True),
        lax.all_to_all(pack_rows(out_cotangent), "rcv", split_axis=1, concat_axis=1, tiled=True),
    )
    expert_outs, expert_grads = expert_pass(
        arrived_rows.reshape(local_count, groups * capacity, feature_width),
        arrived_cot.reshape(local_count, groups * capacity, feature_width),
        expert_weights,
    )
    back_out, back_grad = (
        lax.all_to_all(
            expert_outs.reshape(local_count, groups, capacity, feature_width),
            "rcv",
            split_axis=1,
            concat_axis=1,
            tiled=True,
        ),
        lax.all_to_all(
            expert_grads.reshape(local_count, groups, capacity, feature_width),
            "rcv",
            split_axis=1,
            concat_axis=1,
            tiled=True,
        ),
    )
    picked_out = jnp.take(back_out.reshape(cell_total, feature_width), cell_index, axis=0).reshape(
        row_count, top_count, feature_width
    )
    picked_grad = jnp.take(
        back_grad.reshape(cell_total, feature_width), cell_index, axis=0
    ).reshape(row_count, top_count, feature_width)
    gate_column = gate_weights[:, :, None]
    block_out = (
        stream_wide + jnp.sum(gate_column * picked_out.astype(jnp.float32), axis=1)
    ).astype(jnp.bfloat16)
    normed_grad = jnp.sum(gate_column * picked_grad.astype(jnp.float32), axis=1)
    weighted = norm_gain * normed_grad
    scaled = stream_wide * inverse
    stream_grad = out_cotangent.astype(jnp.float32) + inverse * (
        weighted - scaled * jnp.mean(weighted * scaled, axis=1, keepdims=True)
    )
    return (block_out, stream_grad.astype(jnp.bfloat16))


def solution(mesh):
    placed = (
        P(("rcv", "hd"), None),
        P(("rcv", "hd"), None),
        P(("rcv", "hd"), None),
        P(("rcv", "hd"), None),
        P(),
        P(),
        P(None, "rcv", None, None),
        P(("rcv", "hd"), None),
        P(("rcv", "hd"), None),
        P(("rcv", "hd"), None),
    )
    return jax.shard_map(
        per_device,
        mesh=mesh,
        in_specs=placed,
        out_specs=(P(("rcv", "hd"), None), P(("rcv", "hd"), None)),
        check_vma=False,
    )
```

profile of v0, /device:TPU:0, one launch (start us, length us, event | category | flops | bytes accessed | tf_op | source)
XLA Modules:
  0.0 227.0 jit_solution(5658086145408563885)
XLA Ops:
  0.7 1.9 copy.35
  2.6 4.2 %all-to-all-start = ((bf16[128,4,256]{0,2,1:T(8,128)(2,1)}), bf16[128,4,256]{0,2,1:T(8,128)(2,1)S(1)}, u32[]{:S(2)}, u32[]{:S(2)}) async-start(bf16[128,4,256]{0,2,1:T(8,128)(2,1)} %bitcast), calls=%async_computation | async-start | bytes 524288 | tf_op jit(solution)/shard_map/all_to_all | solution.py:77
  12.9 3.4 %all-to-all-start.1 = ((bf16[128,4,256]{0,2,1:T(8,128)(2,1)}), bf16[128,4,256]{0,2,1:T(8,128)(2,1)S(1)}, u32[]{:S(2)}, u32[]{:S(2)}) async-start(bf16[128,4,256]{0,2,1:T(8,128)(2,1)} %bitcast.2), calls=%async_computation.1 | async-start | bytes 524288 | tf_op jit(solution)/shard_map/all_to_all | solution.py:78
  16.3 2.4 %scatter_custom_fusion = s32[640]{0:T(1024)S(1)} fusion(s32[512]{0:T(512)S(1)} %bitcast.116, s32[512]{0:T(512)S(1)} %add_select_fusion.2, s32[]{:T(128)} %constant.96.clone.1), kind=kCustom, calls=%fused_computation.88 | custom fusion | bytes 2564 | tf_op jit(solution)/shard_map/scatter | solution.py:68
  18.8 3.5 %all-to-all-done.1 = bf16[128,4,256]{0,2,1:T(8,128)(2,1)S(1)} async-done(((bf16[128,4,256]{0,2,1:T(8,128)(2,1)}), bf16[128,4,256]{0,2,1:T(8,128)(2,1)S(1)}, u32[]{:S(2)}, u32[]{:S(2)}) %all-to-all-start.1) | async-done | bytes 262176 | tf_op jit(solution)/shard_map/all_to_all | solution.py:78
  22.3 3.4 %all-to-all-start.2 = ((bf16[128,4,256]{0,2,1:T(8,128)(2,1)}), bf16[128,4,256]{0,2,1:T(8,128)(2,1)S(1)}, u32[]{:S(2)}, u32[]{:S(2)}) async-start(bf16[128,4,256]{0,2,1:T(8,128)(2,1)} %bitcast.4), calls=%async_computation.2 | async-start | bytes 524288 | tf_op jit(solution)/shard_map/all_to_all | solution.py:79
  25.7 3.5 %gather_fusion.2 = bf16[640,1024]{1,0:T(8,128)(2,1)} fusion(bf16[129,1024]{1,0:T(8,128)(2,1)S(1)} %concatenate.7, s32[1024]{0:T(1024)S(1)} %pad_clamp_fusion.1), kind=kCustom, calls=%fused_computation.2.clone | custom fusion | bytes 2624000 | tf_op jit(solution)/shard_map/jit(_take)/gather | solution.py:72
  29.9 1.8 all-to-all-done.2
  35.2 3.4 %all-to-all-start.3 = ((bf16[4,128,256]{1,2,0:T(8,128)(2,1)}), bf16[4,128,256]{1,2,0:T(8,128)(2,1)S(1)}, u32[]{:S(2)}, u32[]{:S(2)}) async-start(bf16[4,128,256]{1,2,0:T(8,128)(2,1)} %copy.42), calls=%async_computation.3 | async-start | bytes 524288 | tf_op jit(solution)/shard_map/all_to_all | solution.py:109
  38.6 6.0 %all-to-all-done.3 = bf16[4,128,256]{1,2,0:T(8,128)(2,1)S(1)} async-done(((bf16[4,128,256]{1,2,0:T(8,128)(2,1)}), bf16[4,128,256]{1,2,0:T(8,128)(2,1)S(1)}, u32[]{:S(2)}, u32[]{:S(2)}) %all-to-all-start.3) | async-done | bytes 262176 | tf_op jit(solution)/shard_map/all_to_all | solution.py:109
  46.1 3.5 %gather_fusion = bf16[640,1024]{1,0:T(8,128)(2,1)} fusion(bf16[129,1024]{1,0:T(8,128)(2,1)S(1)} %concatenate.6, s32[1024]{0:T(1024)S(1)} %pad_clamp_fusion.1), kind=kCustom, calls=%fused_computation.clone | custom fusion | bytes 2624000 | tf_op jit(solution)/shard_map/jit(_take)/gather | solution.py:72
  49.5 3.1 %broadcast_select_fusion.1 = (bf16[640,1024]{1,0:T(8,128)(2,1)S(1)}, bf16[640,1024]{1,0:T(8,128)(2,1)}) fusion(bf16[640,1024]{1,0:T(8,128)(2,1)} %gather_fusion, pred[640]{0:T(1024)(128)(4,1)S(1)} %compare_and_fusion, bf16[640,1024]{1,0:T(8,128)(2,1)} %gather_fusion.2), kind=kLoop, calls=%fused_computation.34 | loop fusion | flops 1310720 | bytes 5243520 | tf_op jit(solution)/shard_map/jit(_take)/select_n | solution.py:72
  53.8 6.5 %all-to-all-start.4 = ((bf16[2,8,40,1024]{3,2,0,1:T(8,128)(2,1)}), bf16[2,8,40,1024]{3,2,0,1:T(8,128)(2,1)S(1)}, u32[]{:S(2)}, u32[]{:S(2)}) async-start(bf16[2,8,40,1024]{3,2,0,1:T(8,128)(2,1)} %copy.48), calls=%async_computation.4 | async-start | bytes 2621440 | tf_op jit(solution)/shard_map/all_to_all | solution.py:116
  60.3 2.5 %copy.55 = bf16[2,8,40,1024]{3,2,0,1:T(8,128)(2,1)} copy(bf16[2,8,40,1024]{3,2,1,0:T(8,128)(2,1)} %bitcast.104) | data formatting | bytes 2621440 | tf_op jit(solution)/shard_map/reshape | solution.py:72
  62.8 28.7 %all-to-all-done.4 = bf16[2,8,40,1024]{3,2,0,1:T(8,128)(2,1)S(1)} async-done(((bf16[2,8,40,1024]{3,2,0,1:T(8,128)(2,1)}), bf16[2,8,40,1024]{3,2,0,1:T(8,128)(2,1)S(1)}, u32[]{:S(2)}, u32[]{:S(2)}) %all-to-all-start.4) | async-done | bytes 1310752 | tf_op jit(solution)/shard_map/all_to_all | solution.py:116
  91.5 4.4 %all-to-all-start.6 = ((bf16[2,8,40,1024]{3,2,0,1:T(8,128)(2,1)}), bf16[2,8,40,1024]{3,2,0,1:T(8,128)(2,1)}, u32[]{:S(2)}, u32[]{:S(2)}) async-start(bf16[2,8,40,1024]{3,2,0,1:T(8,128)(2,1)} %copy.55), calls=%async_computation.6 | async-start | bytes 2621440 | tf_op jit(solution)/shard_map/all_to_all | solution.py:117
  95.9 7.0 %slice.22 = bf16[1024,2,2,512]{3,1,2,0:T(2,128)(2,1)} slice(bf16[1024,2,3,512]{3,1,2,0:T(2,128)(2,1)} %param.20), slice={[0:1024], [0:2], [0:2], [0:512]} | slice | bytes 8388608 | tf_op jit(solution)/shard_map/slice | solution.py:21
  102.9 4.6 %slice.25 = bf16[1024,2,1,512]{3,1,2,0:T(2,128)(2,1)} slice(bf16[1024,2,3,512]{3,1,2,0:T(2,128)(2,1)} %param.20), slice={[0:1024], [0:2], [2:3], [0:512]} | slice | bytes 4194304 | tf_op jit(solution)/shard_map/slice | solution.py:27
  107.6 3.4 %fusion.2 = f32[2,320,2,512]{3,1,2,0:T(8,128)} fusion(bf16[2,320,1024,1]{2,1,3,0:T(8,128)(2,1)S(1)} %bitcast.109, bf16[1024,2,2,512]{3,1,2,0:T(2,128)(2,1)S(1)} %copy-done.4), kind=kOutput, calls=%fused_computation.7 | convolution fusion | flops 1342177280 | bytes 8126464 | tf_op jit(solution)/shard_map/jmd,djcf->jmcf/dot_general | solution.py:20
  111.0 15.9 %all-to-all-done.6 = bf16[2,8,40,1024]{3,2,0,1:T(8,128)(2,1)} async-done(((bf16[2,8,40,1024]{3,2,0,1:T(8,128)(2,1)}), bf16[2,8,40,1024]{3,2,0,1:T(8,128)(2,1)}, u32[]{:S(2)}, u32[]{:S(2)}) %all-to-all-start.6) | async-done | bytes 1310752 | tf_op jit(solution)/shard_map/all_to_all | solution.py:117
  128.9 3.2 %fusion.31 = (bf16[2,320,1,512]{3,1,0,2:T(8,128)(2,1)S(1)}, bf16[2,320,1,512]{3,1,0,2:T(8,128)(2,1)S(1)}) fusion(f32[2,320,2,512]{3,1,2,0:T(8,128)} %fusion.2, bf16[2,320,1024]{2,1,0:T(8,128)(2,1)S(1)} %bitcast.106, bf16[1024,2,1,512]{3,1,2,0:T(2,128)(2,1)S(1)} %copy-done.6), kind=kOutput, calls=%fused_computation.44 | convolution fusion | flops 675348480 | bytes 7340032 | tf_op jit(solution)/shard_map/jmd,djf->jmf/dot_general | solution.py:29
  135.0 3.6 %all-to-all-start.7 = ((bf16[2,8,40,1024]{3,2,0,1:T(8,128)(2,1)}), bf16[2,8,40,1024]{3,2,0,1:T(8,128)(2,1)S(1)}, u32[]{:S(2)}, u32[]{:S(2)}) async-start(bf16[2,8,40,1024]{3,2,0,1:T(8,128)(2,1)} %copy.58), calls=%async_computation.7 | async-start | bytes 2621440 | tf_op jit(solution)/shard_map/all_to_all | solution.py:132
  138.5 3.3 %fusion.14 = bf16[2,320,1024]{2,1,0:T(8,128)(2,1)S(1)} fusion(bf16[1024,2,1,512]{3,1,2,0:T(2,128)(2,1)} %slice.25, f32[2,320,2,512]{3,1,2,0:T(8,128)} %fusion.2), kind=kOutput, calls=%fused_computation.22 | convolution fusion | flops 673710080 | bytes 6029312 | tf_op jit(solution)/shard_map/jmf,djf->jmd/dot_general | solution.py:26
  143.1 26.9 %all-to-all-done.7 = bf16[2,8,40,1024]{3,2,0,1:T(8,128)(2,1)S(1)} async-done(((bf16[2,8,40,1024]{3,2,0,1:T(8,128)(2,1)}), bf16[2,8,40,1024]{3,2,0,1:T(8,128)(2,1)S(1)}, u32[]{:S(2)}, u32[]{:S(2)}) %all-to-all-start.7) | async-done | bytes 1310752 | tf_op jit(solution)/shard_map/all_to_all | solution.py:132
  171.0 4.5 %all-to-all-start.5 = ((bf16[2,8,40,1024]{3,2,0,1:T(8,128)(2,1)}), bf16[2,8,40,1024]{3,2,0,1:T(8,128)(2,1)}, u32[]{:S(2)}, u32[]{:S(2)}) async-start(bf16[2,8,40,1024]{3,2,0,1:T(8,128)(2,1)} %copy.53), calls=%async_computation.5 | async-start | bytes 2621440 | tf_op jit(solution)/shard_map/all_to_all | solution.py:125
  177.2 2.8 %gather_fusion.3 = bf16[512,1024]{1,0:T(8,128)(2,1)} fusion(bf16[640,1024]{1,0:T(8,128)(2,1)S(1)} %bitcast.103, s32[1024]{0:T(1024)S(1)} %pad_clamp_fusion), kind=kCustom, calls=%fused_computation.3.clone | custom fusion | bytes 2099200 | tf_op jit(solution)/shard_map/jit(_take)/gather | solution.py:143
  179.9 26.6 %all-to-all-done.5 = bf16[2,8,40,1024]{3,2,0,1:T(8,128)(2,1)} async-done(((bf16[2,8,40,1024]{3,2,0,1:T(8,128)(2,1)}), bf16[2,8,40,1024]{3,2,0,1:T(8,128)(2,1)}, u32[]{:S(2)}, u32[]{:S(2)}) %all-to-all-start.5) | async-done | bytes 1310752 | tf_op jit(solution)/shard_map/all_to_all | solution.py:125
  208.0 2.8 %gather_fusion.1 = bf16[512,1024]{1,0:T(8,128)(2,1)} fusion(bf16[640,1024]{1,0:T(8,128)(2,1)S(1)} %bitcast.102, s32[1024]{0:T(1024)S(1)} %pad_clamp_fusion), kind=kCustom, calls=%fused_computation.1.clone | custom fusion | bytes 2099200 | tf_op jit(solution)/shard_map/jit(_take)/gather | solution.py:140
  210.7 3.9 %select_convert_fusion.1 = (f32[512,1024]{1,0:T(8,128)}, f32[512,1024]{1,0:T(8,128)}) fusion(bf16[512,1024]{1,0:T(8,128)(2,1)} %gather_fusion.1, pred[512]{0:T(512)(128)(4,1)S(1)} %get-tuple-element.21, bf16[512,1024]{1,0:T(8,128)(2,1)} %gather_fusion.3), kind=kLoop, calls=%fused_computation.42 | loop fusion | flops 2097152 | bytes 6291968 | tf_op jit(solution)/shard_map/convert_element_type | solution.py:148
  214.6 2.8 %reshape.244 = f32[128,4,1024]{2,1,0:T(4,128)} reshape(f32[512,1024]{1,0:T(8,128)} %get-tuple-element.29) | data formatting | bytes 4194304 | tf_op jit(solution)/shard_map/convert_element_type | solution.py:148
  217.4 2.8 %reshape.245 = f32[128,4,1024]{2,1,0:T(4,128)} reshape(f32[512,1024]{1,0:T(8,128)} %get-tuple-element.30) | data formatting | bytes 4194304 | tf_op jit(solution)/shard_map/convert_element_type | solution.py:150
  220.3 5.5 %multiply_reduce_fusion.1 = (f32[128,1024]{1,0:T(8,128)S(1)}, f32[128,1024]{1,0:T(8,128)S(1)}) fusion(f32[128,4,1024]{2,1,0:T(4,128)} %reshape.245, f32[128,4]{1,0:T(8,128)S(1)} %copy.43, f32[128,4,1024]{2,1,0:T(4,128)} %reshape.244), kind=kLoop, calls=%fused_computation.16 | loop fusion | flops 1835008 | bytes 5244928 | tf_op jit(solution)/shard_map/reduce_sum | solution.py:150
  (76 shorter events, 24.3 us)
Async XLA Ops:
  0.6 44.0 %copy-start = (bf16[1024,1024]{1,0:T(8,128)(2,1)S(1)}, bf16[1024,1024]{1,0:T(8,128)(2,1)}, u32[]{:S(2)}) copy-start(bf16[1024,1024]{1,0:T(8,128)(2,1)} %param.18) | copy-start | bytes 6291460
  0.6 7.3 %copy-start.9 = (bf16[128,1024]{1,0:T(8,128)(2,1)S(1)}, bf16[128,1024]{1,0:T(8,128)(2,1)}, u32[]{:S(2)}) copy-start(bf16[128,1024]{1,0:T(8,128)(2,1)} %param.16) | copy-start | bytes 786436
  0.7 8.2 %copy-start.10 = (bf16[128,1024]{1,0:T(8,128)(2,1)S(1)}, bf16[128,1024]{1,0:T(8,128)(2,1)}, u32[]{:S(2)}) copy-start(bf16[128,1024]{1,0:T(8,128)(2,1)} %param.17) | copy-start | bytes 786436
  2.6 10.2 %all-to-all-start = ((bf16[128,4,256]{0,2,1:T(8,128)(2,1)}), bf16[128,4,256]{0,2,1:T(8,128)(2,1)S(1)}, u32[]{:S(2)}, u32[]{:S(2)}) async-start(bf16[128,4,256]{0,2,1:T(8,128)(2,1)} %bitcast), calls=%async_computation | async-start | bytes 524288 | tf_op jit(solution)/shard_map/all_to_all | solution.py:77
  6.8 18.9 %copy-start.7 = (bf16[128,1024]{1,0:T(8,128)(2,1)S(1)}, bf16[128,1024]{1,0:T(8,128)(2,1)}, u32[]{:S(2)}) copy-start(bf16[128,1024]{1,0:T(8,128)(2,1)} %param.23) | copy-start | bytes 786436
  12.9 9.4 %all-to-all-start.1 = ((bf16[128,4,256]{0,2,1:T(8,128)(2,1)}), bf16[128,4,256]{0,2,1:T(8,128)(2,1)S(1)}, u32[]{:S(2)}, u32[]{:S(2)}) async-start(bf16[128,4,256]{0,2,1:T(8,128)(2,1)} %bitcast.2), calls=%async_computation.1 | async-start | bytes 524288 | tf_op jit(solution)/shard_map/all_to_all | solution.py:78
  22.3 9.4 %all-to-all-start.2 = ((bf16[128,4,256]{0,2,1:T(8,128)(2,1)}), bf16[128,4,256]{0,2,1:T(8,128)(2,1)S(1)}, u32[]{:S(2)}, u32[]{:S(2)}) async-start(bf16[128,4,256]{0,2,1:T(8,128)(2,1)} %bitcast.4), calls=%async_computation.2 | async-start | bytes 524288 | tf_op jit(solution)/shard_map/all_to_all | solution.py:79
  34.3 10.2 %copy-start.11 = (bf16[128,1024]{1,0:T(8,128)(2,1)S(1)}, bf16[128,1024]{1,0:T(8,128)(2,1)}, u32[]{:S(2)}) copy-start(bf16[128,1024]{1,0:T(8,128)(2,1)} %param.14) | copy-start | bytes 786436
  35.2 9.4 %all-to-all-start.3 = ((bf16[4,128,256]{1,2,0:T(8,128)(2,1)}), bf16[4,128,256]{1,2,0:T(8,128)(2,1)S(1)}, u32[]{:S(2)}, u32[]{:S(2)}) async-start(bf16[4,128,256]{1,2,0:T(8,128)(2,1)} %copy.42), calls=%async_computation.3 | async-start | bytes 524288 | tf_op jit(solution)/shard_map/all_to_all | solution.py:109
  44.6 1.3 copy-start.12
  45.1 0.8 copy-start.1
  53.8 37.6 %all-to-all-start.4 = ((bf16[2,8,40,1024]{3,2,0,1:T(8,128)(2,1)}), bf16[2,8,40,1024]{3,2,0,1:T(8,128)(2,1)S(1)}, u32[]{:S(2)}, u32[]{:S(2)}) async-start(bf16[2,8,40,1024]{3,2,0,1:T(8,128)(2,1)} %copy.48), calls=%async_computation.4 | async-start | bytes 2621440 | tf_op jit(solution)/shard_map/all_to_all | solution.py:116
  91.5 35.4 %all-to-all-start.6 = ((bf16[2,8,40,1024]{3,2,0,1:T(8,128)(2,1)}), bf16[2,8,40,1024]{3,2,0,1:T(8,128)(2,1)}, u32[]{:S(2)}, u32[]{:S(2)}) async-start(bf16[2,8,40,1024]{3,2,0,1:T(8,128)(2,1)} %copy.55), calls=%async_computation.6 | async-start | bytes 2621440 | tf_op jit(solution)/shard_map/all_to_all | solution.py:117
  102.9 4.7 %copy-start.4 = (bf16[1024,2,2,512]{3,1,2,0:T(2,128)(2,1)S(1)}, bf16[1024,2,2,512]{3,1,2,0:T(2,128)(2,1)}, u32[]{:S(2)}) copy-start(bf16[1024,2,2,512]{3,1,2,0:T(2,128)(2,1)} %slice.22) | copy-start | bytes 12582916
  126.9 2.0 copy-start.6
  128.9 3.2 %copy-start.5 = (bf16[1024,2,2,512]{3,1,2,0:T(2,128)(2,1)S(1)}, bf16[1024,2,2,512]{3,1,2,0:T(2,128)(2,1)}, u32[]{:S(2)}) copy-start(bf16[1024,2,2,512]{3,1,2,0:T(2,128)(2,1)} %slice.22) | copy-start | bytes 12582916
  135.0 35.0 %all-to-all-start.7 = ((bf16[2,8,40,1024]{3,2,0,1:T(8,128)(2,1)}), bf16[2,8,40,1024]{3,2,0,1:T(8,128)(2,1)S(1)}, u32[]{:S(2)}, u32[]{:S(2)}) async-start(bf16[2,8,40,1024]{3,2,0,1:T(8,128)(2,1)} %copy.58), calls=%async_computation.7 | async-start | bytes 2621440 | tf_op jit(solution)/shard_map/all_to_all | solution.py:132
  143.1 32.5 %copy-start.13 = (f32[128,4]{0,1:T(4,128)S(1)}, f32[128,4]{0,1:T(4,128)}, u32[]{:S(2)}) copy-start(f32[128,4]{0,1:T(4,128)} %param.22) | copy-start | bytes 6148
  170.0 1.1 copy-start.3
  171.0 35.5 %all-to-all-start.5 = ((bf16[2,8,40,1024]{3,2,0,1:T(8,128)(2,1)}), bf16[2,8,40,1024]{3,2,0,1:T(8,128)(2,1)}, u32[]{:S(2)}, u32[]{:S(2)}) async-start(bf16[2,8,40,1024]{3,2,0,1:T(8,128)(2,1)} %copy.53), calls=%async_computation.5 | async-start | bytes 2621440 | tf_op jit(solution)/shard_map/all_to_all | solution.py:125
  220.3 5.5 %copy-start.2 = (f32[128,1024]{1,0:T(8,128)S(1)}, f32[128,1024]{1,0:T(8,128)}, u32[]{:S(2)}) copy-start(f32[128,1024]{1,0:T(8,128)} %copy-done.1) | copy-start | bytes 1572868
  220.3 5.7 %copy-start.8 = (bf16[128,1024]{1,0:T(8,128)(2,1)S(1)}, bf16[128,1024]{1,0:T(8,128)(2,1)}, u32[]{:S(2)}) copy-start(bf16[128,1024]{1,0:T(8,128)(2,1)} %param.23) | copy-start | bytes 786436
where the time goes:
time: 228 us; the launch traced here: 227 us
  waiting for transfers between devices  111 us (49%)
  local copies, waits for them, and re-layouts  52 us (23%)
  starting transfers between devices  33.4 us (15%)
  other arithmetic  15.8 us (7%)
  matrix products  13.7 us (6%)
    all_to_all x1, waiting for transfers between devices, per_device(): lax.all_to_all(pack_rows(normed), 'rcv', split_axis=1, concat_axis=1, til...  28.7 us
    all_to_all x1, waiting for transfers between devices, per_device(): lax.all_to_all(expert_grads.reshape(local_count, groups, capacity, featur...  26.9 us
    all_to_all x1, waiting for transfers between devices, per_device(): lax.all_to_all(expert_outs.reshape(local_count, groups, capacity, feature...  26.6 us
    all_to_all x1, waiting for transfers between devices, per_device(): lax.all_to_all(pack_rows(out_cotangent), 'rcv', split_axis=1, concat_axis...  15.9 us
    slice x1, local copies, waits for them, and re-layouts, expert_pass(): expert_weights[:, :, :2]  7.01 us
    gather x2, local copies, waits for them, and re-layouts, pack_rows(): jnp.take(padded, source, axis=0)  6.94 us
    unnamed x33, local copies, waits for them, and re-layouts  6.86 us
    all_to_all x1, starting transfers between devices, per_device(): lax.all_to_all(pack_rows(normed), 'rcv', split_axis=1, concat_axis=1, til...  6.45 us
  transfers between devices with their start and end apart: 8, of which 8 were waited for; matrix products, arithmetic and copies ran while one was open for 16% of the time, Pallas kernels for 0%

commit v1 on v0

v1 whole, which is shorter than its diff:
```python
import functools
import math

import jax
import jax.numpy as jnp
from jax import lax
from jax.experimental import pallas as pl
from jax.experimental.pallas import tpu as pltpu
from jax.sharding import PartitionSpec as P

HS = 64
LANES = 128
CHUNK = 32
NORM_EPS = 1e-06
VMEM_BYTES = 48 << 20
F32, BF16 = jnp.float32, jnp.bfloat16


def dot(a, b, contract=((1,), (0,))):
    return lax.dot_general(a, b, (contract, ((), ())), preferred_element_type=F32)


def params():
    return pltpu.CompilerParams(vmem_limit_bytes=VMEM_BYTES)


def vmem_specs(count):
    return [pl.BlockSpec(memory_space=pltpu.VMEM)] * count


def cost(flops, nbytes):
    return pl.CostEstimate(flops=int(flops), bytes_accessed=int(nbytes), transcendentals=0)


def split_kernel(w_ref, o_ref):
    for part in range(w_ref.shape[1]):
        by_expert = jnp.swapaxes(w_ref[:, part], 0, 1)
        for block in range(o_ref.shape[0]):
            for expert in range(by_expert.shape[0]):
                o_ref[block, expert, part] = by_expert[expert, block * CHUNK : (block + 1) * CHUNK]


def split_experts(expert_weights):
    depth, local, parts, hidden = expert_weights.shape
    rows = 4 * CHUNK
    return pl.pallas_call(
        split_kernel,
        grid=(depth // rows,),
        in_specs=[pl.BlockSpec((rows, parts, local, hidden), lambda i: (i, 0, 0, 0))],
        out_specs=pl.BlockSpec((4, local, parts, CHUNK, hidden), lambda i: (i, 0, 0, 0, 0)),
        out_shape=jax.ShapeDtypeStruct((depth // CHUNK, local, parts, CHUNK, hidden), BF16),
        compiler_params=params(),
        cost_estimate=cost(0, 4 * depth * local * parts * hidden),
        name="split_experts",
    )(jnp.transpose(expert_weights, (0, 2, 1, 3)))


def attention_kernel(count, q_ref, stream_ref, proj_ref, gain_ref, *refs):
    kv_refs, (mix_ref, normed_ref, attended) = refs[:count], refs[count:]
    rows, width = q_ref.shape
    first = lax.broadcasted_iota(jnp.int32, (rows, LANES), 1) < HS
    for pair in range(width // LANES):
        cols = slice(pair * LANES, (pair + 1) * LANES)
        query = q_ref[:, cols] * jnp.asarray(1.0 / math.sqrt(HS), BF16)
        zero = jnp.zeros_like(query)
        both = jnp.concatenate([jnp.where(first, query, zero), jnp.where(first, zero, query)], axis=0)
        keys = jnp.concatenate([r[:rows, cols] for r in kv_refs], axis=0)
        vals = jnp.concatenate([r[rows:, cols] for r in kv_refs], axis=0)
        scores = dot(both, keys, ((1,), (1,)))
        raw = jnp.exp(scores - jnp.max(scores, axis=1, keepdims=True))
        total = jnp.sum(raw, axis=1, keepdims=True)
        mixed = dot(raw.astype(BF16), vals) / total
        attended[:, cols] = jnp.where(first, mixed[:rows], mixed[rows:]).astype(BF16)
    mix = (stream_ref[...].astype(F32) + dot(attended[...], proj_ref[...])).astype(BF16)
    mix_ref[...] = mix
    wide = mix.astype(F32)
    inverse = lax.rsqrt(jnp.mean(wide * wide, axis=1, keepdims=True) + NORM_EPS)
    normed_ref[...] = (gain_ref[...] * wide * inverse).astype(BF16)


def attention(queries, stream, out_proj, norm_gain, kv_blocks):
    shape = jax.ShapeDtypeStruct(stream.shape, BF16)
    rows, width = stream.shape
    return pl.pallas_call(
        functools.partial(attention_kernel, len(kv_blocks)),
        in_specs=vmem_specs(4 + len(kv_blocks)),
        out_specs=vmem_specs(2),
        out_shape=(shape, shape),
        scratch_shapes=[pltpu.VMEM(stream.shape, BF16)],
        compiler_params=params(),
        cost_estimate=cost(8e9, 4e6),
        name="attention",
    )(queries, stream, out_proj, norm_gain[None, :], *kv_blocks)


def pick_rows(where_ref, meta_refs, experts, slots):
    choice, member = where_ref[0], where_ref[1]
    rows = meta_refs[0].shape[1]
    names, gates = [], []
    for ref in meta_refs:
        meta = ref[...].astype(F32)
        top = meta.shape[0] // 4
        line = lax.broadcasted_iota(jnp.int32, meta.shape, 0)
        names.append(jnp.sum(jnp.where(line == choice, meta, 0.0), axis=0, keepdims=True))
        gate = jnp.where((line >= top) & (lax.rem(line, top) == choice), meta, 0.0)
        gate = jnp.broadcast_to(jnp.sum(gate, axis=0, keepdims=True), (rows, rows))
        gates.append(jnp.transpose(gate)[:, :1])
    names = jnp.concatenate(names, axis=1)
    count = names.shape[1]
    named = names.astype(jnp.int32) - choice * experts
    lines = max(experts, 8)
    chosen = named == lax.broadcasted_iota(jnp.int32, (lines, count), 0)
    earlier = lax.broadcasted_iota(jnp.int32, (count, count), 0) < lax.broadcasted_iota(
        jnp.int32, (count, count), 1
    )
    ones = jnp.where(chosen, 1.0, 0.0).astype(BF16)
    rank = dot(ones, jnp.where(earlier, 1.0, 0.0).astype(BF16))
    own_rank = jnp.sum(jnp.where(chosen, rank, 0.0), axis=0, keepdims=True).astype(jnp.int32)

    def matrix(expert):
        target = jnp.where(named == expert, own_rank, -1)
        hit = target == lax.broadcasted_iota(jnp.int32, (slots, count), 0)
        return jnp.where(hit, 1.0, 0.0).astype(BF16)

    return matrix, gates


def weight_copies(where_ref, sets, buffer, sems, index):
    copies, base = [], 2
    for ahead in range(index):
        base += len(sets[ahead])
    for place, ref in enumerate(sets[index]):
        for block in range(ref.shape[0]):
            start = pl.multiple_of((where_ref[base + place] + block) * CHUNK, CHUNK)
            copies.append(
                pltpu.make_async_copy(
                    ref.at[block],
                    buffer.at[index % 2, :, :, pl.ds(start, CHUNK), :],
                    sems.at[index % 2, len(copies)],
                )
            )
    return copies


def for_each_set(where_ref, sets, buffer, sems, body):
    for copy in weight_copies(where_ref, sets, buffer, sems, 0):
        copy.start()
    for index in range(len(sets)):
        if index + 1 < len(sets):
            for copy in weight_copies(where_ref, sets, buffer, sems, index + 1):
                copy.start()
        for copy in weight_copies(where_ref, sets, buffer, sems, index):
            copy.wait()
        body(index, buffer.at[index % 2])


def take_refs(refs, counts):
    taken = []
    for count in counts:
        taken.append(refs[:count])
        refs = refs[count:]
    return taken


def group_sets(refs, set_sizes):
    return take_refs(refs, set_sizes)


def out_kernel(set_sizes, experts, slots, where_ref, *refs):
    x_refs, meta_refs, w_refs, out_refs, rest = take_refs(refs, (4, 4, sum(set_sizes), 4, 5))
    act_ref, slope_ref, total, buffer, sems = rest
    rows = x_refs[0].shape[0]
    local = buffer.shape[1]
    sets = len(set_sizes)
    matrix, gates = pick_rows(where_ref, meta_refs, experts, slots)
    arrived = jnp.concatenate([r[...] for r in x_refs], axis=0)

    def one_set(index, weights):
        owner = lax.rem(where_ref[1] + index, sets)
        for expert in range(local):
            pick = matrix(owner * local + expert)
            x = dot(pick, arrived).astype(BF16)
            gate = dot(x, weights[expert, 0])
            up = dot(x, weights[expert, 1])
            sigmoid = 1.0 / (1.0 + jnp.exp(-gate))
            active = gate * sigmoid
            act_ref[index, expert] = active
            slope_ref[index, expert] = up * (sigmoid * (1.0 + gate * (1.0 - sigmoid)))
            hidden = (active * up).astype(BF16)
            result = dot(hidden, weights[expert, 2], ((1,), (1,))).astype(BF16)
            back = dot(pick, result, ((0,), (0,)))
            if index == 0 and expert == 0:
                total[...] = back
            else:
                total[...] += back

    for_each_set(where_ref, group_sets(w_refs, set_sizes), buffer, sems, one_set)
    for block, ref in enumerate(out_refs):
        ref[...] = (gates[block] * total[block * rows : (block + 1) * rows]).astype(BF16)


def grad_kernel(set_sizes, experts, slots, where_ref, *refs):
    c_refs, meta_refs, (act_ref, slope_ref), w_refs, out_refs, rest = take_refs(
        refs, (4, 4, 2, sum(set_sizes), 4, 3)
    )
    total, buffer, sems = rest
    rows = c_refs[0].shape[0]
    local = buffer.shape[1]
    sets = len(set_sizes)
    matrix, gates = pick_rows(where_ref, meta_refs, experts, slots)
    arrived = jnp.concatenate([r[...] for r in c_refs], axis=0)

    def one_set(index, weights):
        owner = lax.rem(where_ref[1] + index, sets)
        for expert in range(local):
            pick = matrix(owner * local + expert)
            cot = dot(pick, arrived).astype(BF16)
            back_hidden = dot(cot, weights[expert, 2])
            gate = (back_hidden * slope_ref[index, expert]).astype(BF16)
            up = (back_hidden * act_ref[index, expert]).astype(BF16)
            result = dot(gate, weights[expert, 0], ((1,), (1,))) + dot(
                up, weights[expert, 1], ((1,), (1,))
            )
            back = dot(pick, result.astype(BF16), ((0,), (0,)))
            if index == 0 and expert == 0:
                total[...] = back
            else:
                total[...] += back

    for_each_set(where_ref, group_sets(w_refs, set_sizes), buffer, sems, one_set)
    for block, ref in enumerate(out_refs):
        ref[...] = (gates[block] * total[block * rows : (block + 1) * rows]).astype(BF16)


def expert_calls(where, x_blocks, cot_blocks, weight_sets, experts, slots, top):
    rows, width = x_blocks[0].shape
    _, local, parts, _, hidden = weight_sets[0][0].shape
    set_sizes = tuple(len(pieces) for pieces in weight_sets)
    flat = [piece for pieces in weight_sets for piece in pieces]
    most = max(sum(piece.shape[0] for piece in pieces) for pieces in weight_sets)
    block = jax.ShapeDtypeStruct((rows, width), BF16)
    kept = jax.ShapeDtypeStruct((len(weight_sets), local, slots, hidden), F32)
    smem = [pl.BlockSpec(memory_space=pltpu.SMEM)]
    hbm = [pl.BlockSpec(memory_space=pl.ANY)] * len(flat)
    meta = [
        pl.BlockSpec((4 * top, rows), lambda i: (rows // (4 * top), 0))
    ] * 4
    full = [pl.BlockSpec((rows, width), lambda i: (0, 0))] * 4
    whole_kept = [pl.BlockSpec(kept.shape, lambda i: (0, 0, 0, 0))] * 2
    scratch = [
        pltpu.VMEM((4 * rows, width), F32),
        pltpu.VMEM((2, local, parts, width, hidden), BF16),
        pltpu.SemaphoreType.DMA((2, most)),
    ]
    estimate = cost(6e9, 2 * len(weight_sets) * local * parts * width * hidden)
    *outs, active, slope = pl.pallas_call(
        functools.partial(out_kernel, set_sizes, experts, slots),
        grid=(1,),
        in_specs=smem + full + meta + hbm,
        out_specs=full + whole_kept,
        out_shape=[block] * 4 + [kept] * 2,
        scratch_shapes=scratch,
        compiler_params=params(),
        cost_estimate=estimate,
        name="expert_out",
    )(where, *x_blocks, *cot_blocks, *flat)
    grads = pl.pallas_call(
        functools.partial(grad_kernel, set_sizes, experts, slots),
        grid=(1,),
        in_specs=smem + full + meta + whole_kept + hbm,
        out_specs=full,
        out_shape=[block] * 4,
        scratch_shapes=scratch,
        compiler_params=params(),
        cost_estimate=estimate,
        name="expert_grad",
    )(where, *cot_blocks, *cot_blocks, active, slope, *flat)
    return outs, grads


def finish_kernel(mix_ref, cot_ref, gain_ref, o0, o1, o2, g0, g1, g2, out_ref, grad_ref):
    wide = mix_ref[...].astype(F32)
    inverse = lax.rsqrt(jnp.mean(wide * wide, axis=1, keepdims=True) + NORM_EPS)
    out_ref[...] = (
        wide + (o0[...].astype(F32) + o1[...].astype(F32) + o2[...].astype(F32))
    ).astype(BF16)
    weighted = gain_ref[...] * (g0[...].astype(F32) + g1[...].astype(F32) + g2[...].astype(F32))
    scaled = wide * inverse
    grad_ref[...] = (
        cot_ref[...].astype(F32)
        + inverse * (weighted - scaled * jnp.mean(weighted * scaled, axis=1, keepdims=True))
    ).astype(BF16)


def finish(mix, cot, norm_gain, outs, grads):
    shape = jax.ShapeDtypeStruct(mix.shape, BF16)
    return pl.pallas_call(
        finish_kernel,
        in_specs=vmem_specs(9),
        out_specs=vmem_specs(2),
        out_shape=(shape, shape),
        compiler_params=params(),
        cost_estimate=cost(0, 9 * mix.size * 2),
        name="finish",
    )(mix, cot, norm_gain[None, :], *outs, *grads)


class Moves:
    def __init__(self, groups, heads, top):
        self.shape = (top, groups // top, heads // 2, 2)

    def send(self, array, target):
        top, members, chips, cores = self.shape
        pairs = []
        for index in range(math.prod(self.shape)):
            core = index % cores
            chip = index // cores % chips
            member = index // (cores * chips) % members
            choice = index // (cores * chips * members)
            k, m, h, c = target(choice, member, chip, core)
            pairs.append((index, ((k * members + m) * chips + h) * cores + c))
        return lax.ppermute(array, ("rcv", "hd"), pairs)

    def other_core(self, array):
        return self.send(array, lambda k, m, h, c: (k, m, h, 1 - c))

    def next_chip(self, array, step):
        return self.send(array, lambda k, m, h, c: (k, m, (h + step) % self.shape[2], c))

    def other_member(self, array):
        return self.send(array, lambda k, m, h, c: (k, 1 - m, h, c))

    def partner(self, array):
        return self.send(array, lambda k, m, h, c: (k ^ 1, m, h, c))

    def mirror(self, array):
        return self.send(array, lambda k, m, h, c: (3 - k, m, h, c))


def gather_choices(moves, block):
    across = moves.mirror(block)
    beside = moves.partner(block)
    return [block, beside, across, moves.partner(across)]


def scatter_choices(moves, blocks):
    own, beside, across, far = blocks
    merged = (across.astype(F32) + moves.partner(far).astype(F32)).astype(BF16)
    return [own, moves.partner(beside), moves.mirror(merged)]


def gather_sequence(moves, block):
    gathered = [block] + [moves.next_chip(block, step) for step in range(1, moves.shape[2])]
    return gathered + [moves.other_core(each) for each in gathered]


def other_weights(moves, weights, chip, core):
    _, members, chips, _ = moves.shape
    total = weights.shape[0]
    if members == 1:
        return []
    if (members, chips) != (2, 2) or total % 16 != 0:
        top = moves.shape[0]
        groups = [[k * members + m for m in range(members)] for k in range(top)]
        every = lax.all_gather(weights, "rcv", axis_index_groups=groups)
        me = lax.axis_index("rcv") % members
        zero = jnp.int32(0)
        return [
            [(lax.dynamic_index_in_dim(every, (me + step) % members, 0, keepdims=False), zero)]
            for step in range(1, members)
        ]
    part = 5 * total // 32
    shared = total // 2 - 2 * part

    def cut_at(chip, core):
        return 2 * shared + (chip * 2 + core) * part

    def cut(start, size):
        return lax.dynamic_slice_in_dim(weights, start, size, 0)

    one = moves.other_member(cut(cut_at(chip, core), part))
    both = moves.other_member(cut(core * shared, shared))
    other = moves.next_chip(one, 1)
    return [
        [
            (one, cut_at(chip, core)),
            (moves.other_core(one), cut_at(chip, 1 - core)),
            (both, core * shared),
            (moves.other_core(both), (1 - core) * shared),
            (other, cut_at(1 - chip, core)),
            (moves.other_core(other), cut_at(1 - chip, 1 - core)),
        ]
    ]


def routing_rows(expert_ids, gate_weights, width):
    names = expert_ids.T.astype(F32)
    gate = gate_weights.T
    high = lax.reduce_precision(gate, 8, 7)
    middle = lax.reduce_precision(gate - high, 8, 7)
    low = gate - high - middle
    rows = jnp.concatenate([names, high, middle, low], axis=0).astype(BF16)
    return jnp.pad(rows, ((0, 0), (0, width - rows.shape[1])))


def per_device(
    stream,
    queries,
    keys,
    values,
    out_proj,
    norm_gain,
    expert_weights,
    expert_ids,
    gate_weights,
    out_cotangent,
):
    rows, width = stream.shape
    groups, heads = lax.axis_size("rcv"), lax.axis_size("hd")
    local = expert_weights.shape[1]
    top = expert_ids.shape[1]
    experts = local * groups
    capacity = (5 * rows * top + 4 * experts - 1) // (4 * experts)
    slots = (top * capacity + 15) // 16 * 16
    moves = Moves(groups, heads, top)
    members = groups // top
    choice, member = lax.axis_index("rcv") // members, lax.axis_index("rcv") % members
    chip, core = lax.axis_index("hd") // 2, lax.axis_index("hd") % 2

    kv_blocks = gather_sequence(moves, jnp.concatenate([keys, values], axis=0))
    routed = jnp.concatenate([out_cotangent, routing_rows(expert_ids, gate_weights, width)], axis=0)
    cot_blocks = gather_choices(moves, routed)
    weights = split_experts(expert_weights)
    sets = [[(weights, jnp.int32(0))]] + other_weights(moves, weights, chip, core)
    mix, normed = attention(queries, stream, out_proj, norm_gain, kv_blocks)
    x_blocks = gather_choices(moves, normed)
    where = jnp.stack([choice, member] + [start for pieces in sets for _, start in pieces]).astype(
        jnp.int32
    )
    outs, grads = expert_calls(
        where,
        x_blocks,
        cot_blocks,
        [[piece for piece, _ in pieces] for pieces in sets],
        experts // top,
        slots,
        top,
    )
    outs = scatter_choices(moves, outs)
    grads = scatter_choices(moves, grads)
    return finish(mix, out_cotangent, norm_gain, outs, grads)


def solution(mesh):
    row = P(("rcv", "hd"), None)
    placed = (row, row, row, row, P(), P(), P(None, "rcv", None, None), row, row, row)
    return jax.shard_map(
        per_device, mesh=mesh, in_specs=placed, out_specs=(row, row), check_vma=False
    )
```

time: 228 us -> 145 us (0.64)
  local copies, waits for them, and re-layouts: 52 us -> 4.66 us
  waiting for transfers between devices: 111 us -> 66.5 us
  Pallas kernels: 0 us -> 35.8 us
  other arithmetic: 15.8 us -> 0.18 us
  matrix products: 13.7 us -> 0 us
  starting transfers between devices: 33.4 us -> 36.2 us
    all_to_all x8 -> x0, waiting for transfers between devices: 111 us -> none  [the longest x1 28.7 us: per_device(): lax.all_to_all(pack_rows(normed), 'rcv', split_axis=1, concat_axis=1, til...]
    ppermute x0 -> x21, waiting for transfers between devices: none -> 66.5 us  [send(): return lax.ppermute(array, ('rcv', 'hd'), pairs)]
    ppermute x0 -> x21, starting transfers between devices: none -> 36.2 us  [send(): return lax.ppermute(array, ('rcv', 'hd'), pairs)]
    pallas_call x0 -> x5, Pallas kernels: none -> 35.8 us  [the longest x1 11.4 us: expert_calls(): pl.pallas_call(functools.partial(out_kernel, set_sizes, experts, slots),...]
    all_to_all x8 -> x0, starting transfers between devices: 33.4 us -> none  [the longest x1 6.45 us: per_device(): lax.all_to_all(pack_rows(normed), 'rcv', split_axis=1, concat_axis=1, til...]
    dot_general x7 -> x0, matrix products: 13.7 us -> none  [the longest x1 3.4 us: expert_pass(): jnp.einsum('jmd,djcf->jmcf', arrived_rows, expert_weights[:, :, :2], pref...]
    gather x4 -> x0, local copies, waits for them, and re-layouts: 12.5 us -> none  [the longest x2 6.94 us: pack_rows(): jnp.take(padded, source, axis=0)]
    slice x3 -> x0, local copies, waits for them, and re-layouts: 11.8 us -> none  [the longest x1 7.01 us: expert_pass(): expert_weights[:, :, :2]]
  transfers between devices with their start and end apart: 8 -> 21, of which waited for: 8 -> 11; matrix products, arithmetic and copies ran while one was open for 16% -> 1% of each run, Pallas kernels for 0% -> 10%
where the time goes in v1:
time: 145 us; the launch traced here: 144 us
  waiting for transfers between devices  66.5 us (46%)
  starting transfers between devices  36.2 us (25%)
  Pallas kernels  35.8 us (25%)
  local copies, waits for them, and re-layouts  4.66 us (3%)
    ppermute x21, waiting for transfers between devices, send(): return lax.ppermute(array, ('rcv', 'hd'), pairs)  66.5 us
    ppermute x21, starting transfers between devices, send(): return lax.ppermute(array, ('rcv', 'hd'), pairs)  36.2 us
    pallas_call x1, Pallas kernels, expert_calls(): pl.pallas_call(functools.partial(out_kernel, set_sizes, experts, slots),...  11.4 us
    pallas_call x1, Pallas kernels, expert_calls(): pl.pallas_call(functools.partial(grad_kernel, set_sizes, experts, slots),...  11.1 us
    pallas_call x1, Pallas kernels, split_experts(): pl.pallas_call(split_kernel, grid=(depth // rows,), in_specs=[pl.BlockSpe...  8.36 us
    pallas_call x1, Pallas kernels, attention(): pl.pallas_call(functools.partial(attention_kernel, len(kv_blocks)), in_sp...  3.79 us
  transfers between devices with their start and end apart: 21, of which 11 were waited for; matrix products, arithmetic and copies ran while one was open for 1% of the time, Pallas kernels for 10%

profile of v1, /device:TPU:0, one launch (start us, length us, event | category | flops | bytes accessed | tf_op | source)
XLA Modules:
  0.0 144.2 jit_solution(8913716126894794488)
XLA Ops:
  0.6 8.4 %split_experts.1.refs_8_.refs_10_ = bf16[32,2,3,32,512]{4,3,2,1,0:T(8,128)(2,1)} custom-call(bf16[1024,3,2,512]{3,2,1,0:T(2,128)(2,1)} %bitcast.21), custom_call_target="tpu_custom_call" | custom-call | bytes 12582912 | tf_op jit(solution)/shard_map/split_experts/pallas_call | solution.py:46
  9.0 1.3 constant_dynamic-slice_fusion.1
  10.3 3.0 %collective-permute-start.9 = (bf16[5,2,3,32,512]{4,3,2,1,0:T(8,128)(2,1)S(1)}, bf16[5,2,3,32,512]{4,3,2,1,0:T(8,128)(2,1)S(1)}, u32[]{:S(2)}, u32[]{:S(2)}) collective-permute-start(bf16[5,2,3,32,512]{4,3,2,1,0:T(8,128)(2,1)S(1)} %constant_dynamic-slice_fusion.1), channel_id=1, source_target_pairs={{0,4},{1,5},{2,6},{3,7},{4,0},{5,1},{6,2},{7,3},{8,12},{9,13},{10,... | collective-permute-start | bytes 2949128 | tf_op jit(solution)/shard_map/ppermute | solution.py:322
  13.4 1.5 %constant_dynamic-slice_fusion = bf16[6,2,3,32,512]{4,3,2,1,0:T(8,128)(2,1)S(1)} fusion(bf16[32,2,3,32,512]{4,3,2,1,0:T(8,128)(2,1)} %split_experts.1.refs_8_.refs_10_, s32[]{:T(128)S(6)} %select_n.29), kind=kLoop, calls=%fused_computation.20 | loop fusion | bytes 2359300 | tf_op jit(solution)/shard_map/dynamic_slice | solution.py:379
  15.1 2.0 %collective-permute-start = (bf16[256,1024]{1,0:T(8,128)(2,1)S(1)}, bf16[256,1024]{1,0:T(8,128)(2,1)S(1)}, u32[]{:S(2)}, u32[]{:S(2)}) collective-permute-start(bf16[256,1024]{1,0:T(8,128)(2,1)S(1)} %constant_dynamic-update-slice_fusion.refs_0_), channel_id=1, source_target_pairs={{0,2},{1,3},{2,0},{3,1},{4,6},{5,7},{6,4},{7,5},{8,10},{9,11},{10,... | collective-permute-start | bytes 1572872 | tf_op jit(solution)/shard_map/ppermute | solution.py:322
  17.1 18.8 %collective-permute-done.9.refs_9_.refs_11_ = bf16[5,2,3,32,512]{4,3,2,1,0:T(8,128)(2,1)S(1)} collective-permute-done((bf16[5,2,3,32,512]{4,3,2,1,0:T(8,128)(2,1)S(1)}, bf16[5,2,3,32,512]{4,3,2,1,0:T(8,128)(2,1)S(1)}, u32[]{:S(2)}, u32[]{:S(2)}) %collective-permute-start.9) | collective-permute-done | bytes 983072 | tf_op jit(solution)/shard_map/ppermute | solution.py:322
  35.9 2.0 %collective-permute-start.13 = (bf16[5,2,3,32,512]{4,3,2,1,0:T(8,128)(2,1)S(1)}, bf16[5,2,3,32,512]{4,3,2,1,0:T(8,128)(2,1)S(1)}, u32[]{:S(2)}, u32[]{:S(2)}) collective-permute-start(bf16[5,2,3,32,512]{4,3,2,1,0:T(8,128)(2,1)S(1)} %collective-permute-done.9.refs_9_.refs_11_), channel_id=1, source_target_pairs={{0,2},{1,3},{2,0},{3,1},{4,6},{5,7},{6,4},{7,5},{8,10},{9,11},{10,... | collective-permute-start | bytes 2949128 | tf_op jit(solution)/shard_map/ppermute | solution.py:322
  38.6 3.7 %collective-permute-start.7 = (bf16[144,1024]{1,0:T(8,128)(2,1)S(1)}, bf16[144,1024]{1,0:T(8,128)(2,1)S(1)}, u32[]{:S(2)}, u32[]{:S(2)}) collective-permute-start(bf16[144,1024]{1,0:T(8,128)(2,1)S(1)} %pad_maximum_fusion.refs_4_.refs_0_), channel_id=1, source_target_pairs={{0,24},{1,25},{2,26},{3,27},{4,28},{5,29},{6,30},{7,31},{8,16},{9,... | collective-permute-start | bytes 884744 | tf_op jit(solution)/shard_map/ppermute | solution.py:322
  42.3 7.3 %collective-permute-done.7.refs_6_.refs_2_ = bf16[144,1024]{1,0:T(8,128)(2,1)S(1)} collective-permute-done((bf16[144,1024]{1,0:T(8,128)(2,1)S(1)}, bf16[144,1024]{1,0:T(8,128)(2,1)S(1)}, u32[]{:S(2)}, u32[]{:S(2)}) %collective-permute-start.7) | collective-permute-done | bytes 294944 | tf_op jit(solution)/shard_map/ppermute | solution.py:322
  49.6 5.9 %collective-permute-start.6 = (bf16[144,1024]{1,0:T(8,128)(2,1)S(1)}, bf16[144,1024]{1,0:T(8,128)(2,1)S(1)}, u32[]{:S(2)}, u32[]{:S(2)}) collective-permute-start(bf16[144,1024]{1,0:T(8,128)(2,1)S(1)} %pad_maximum_fusion.refs_4_.refs_0_), channel_id=1, source_target_pairs={{0,8},{1,9},{2,10},{3,11},{4,12},{5,13},{6,14},{7,15},{8,0},{9,1},... | collective-permute-start | bytes 884744 | tf_op jit(solution)/shard_map/ppermute | solution.py:322
  55.6 4.9 %collective-permute-done.11.refs_11_.refs_13_ = bf16[6,2,3,32,512]{4,3,2,1,0:T(8,128)(2,1)} collective-permute-done((bf16[6,2,3,32,512]{4,3,2,1,0:T(8,128)(2,1)S(1)}, bf16[6,2,3,32,512]{4,3,2,1,0:T(8,128)(2,1)}, u32[]{:S(2)}, u32[]{:S(2)}) %collective-permute-start.11) | collective-permute-done | bytes 1179680 | tf_op jit(solution)/shard_map/ppermute | solution.py:322
  61.0 3.8 %attention.1 = (bf16[128,1024]{1,0:T(8,128)(2,1)S(1)}, bf16[128,1024]{1,0:T(8,128)(2,1)}) custom-call(bf16[128,1024]{1,0:T(8,128)(2,1)S(1)} %copy-done.8, bf16[128,1024]{1,0:T(8,128)(2,1)S(1)} %copy-done.9, bf16[1024,1024]{1,0:T(8,128)(2,1)S(1)} %copy-done.2, f32[1,1024]{1,0:T(1,128)S(1)} %bitcast.19, ...), custom_call_target="tpu_custom_call" | custom-call | flops 8000000000 | bytes 4000000 | tf_op jit(solution)/shard_map/attention/pallas_call | solution.py:84
  64.8 3.8 %collective-permute-start.4 = (bf16[128,1024]{1,0:T(8,128)(2,1)}, bf16[128,1024]{1,0:T(8,128)(2,1)}, u32[]{:S(2)}, u32[]{:S(2)}) collective-permute-start(bf16[128,1024]{1,0:T(8,128)(2,1)} %get-tuple-element.15.refs_0_), channel_id=1, source_target_pairs={{0,24},{1,25},{2,26},{3,27},{4,28},{5,29},{6,30},{7,31},{8,16},{9,... | collective-permute-start | bytes 786440 | tf_op jit(solution)/shard_map/ppermute | solution.py:322
  69.4 1.4 collective-permute-start.3
  70.7 6.2 %collective-permute-done.4.refs_2_ = bf16[128,1024]{1,0:T(8,128)(2,1)} collective-permute-done((bf16[128,1024]{1,0:T(8,128)(2,1)}, bf16[128,1024]{1,0:T(8,128)(2,1)}, u32[]{:S(2)}, u32[]{:S(2)}) %collective-permute-start.4) | collective-permute-done | bytes 262176 | tf_op jit(solution)/shard_map/ppermute | solution.py:322
  76.9 3.9 %collective-permute-start.5 = (bf16[128,1024]{1,0:T(8,128)(2,1)}, bf16[128,1024]{1,0:T(8,128)(2,1)}, u32[]{:S(2)}, u32[]{:S(2)}) collective-permute-start(bf16[128,1024]{1,0:T(8,128)(2,1)} %collective-permute-done.4.refs_2_), channel_id=1, source_target_pairs={{0,8},{1,9},{2,10},{3,11},{4,12},{5,13},{6,14},{7,15},{8,0},{9,1},... | collective-permute-start | bytes 786440 | tf_op jit(solution)/shard_map/ppermute | solution.py:322
  80.9 1.1 collective-permute-done.3.refs_1_
  82.0 5.5 %collective-permute-done.5.refs_3_ = bf16[128,1024]{1,0:T(8,128)(2,1)} collective-permute-done((bf16[128,1024]{1,0:T(8,128)(2,1)}, bf16[128,1024]{1,0:T(8,128)(2,1)}, u32[]{:S(2)}, u32[]{:S(2)}) %collective-permute-start.5) | collective-permute-done | bytes 262176 | tf_op jit(solution)/shard_map/ppermute | solution.py:322
  88.5 11.4 %expert_out.1 = (bf16[128,1024]{1,0:T(8,128)(2,1)S(1)}, bf16[128,1024]{1,0:T(8,128)(2,1)S(1)}, bf16[128,1024]{1,0:T(8,128)(2,1)S(1)}, bf16[128,1024]{1,0:T(8,128...) custom-call(s32[9]{0:T(128)S(1)} %stack.35.where_ref, bf16[128,1024]{1,0:T(8,128)(2,1)} %get-tuple-element.15.refs_0_, ...), custom_call_target="tpu_custom_call" | custom-call | flops 6000000000 | bytes 12582912 | tf_op jit(solution)/shard_map/expert_out/pallas_call | solution.py:256
  99.9 1.1 collective-permute-start.16
  101.0 11.1 %expert_grad.1 = (bf16[128,1024]{1,0:T(8,128)(2,1)S(1)}, bf16[128,1024]{1,0:T(8,128)(2,1)S(1)}, bf16[128,1024]{1,0:T(8,128)(2,1)S(1)}, bf16[128,1024]{1,0:T(8,128)(2,1)S(1)}) custom-call(s32[9]{0:T(128)S(1)} %stack.35.where_ref, bf16[144,1024]{1,0:T(8,128)(2,1)S(1)} %pad_maximum_fusion.refs_4_.refs_0_, ...), custom_call_target="tpu_custom_call" | custom-call | flops 6000000000 | bytes 12582912 | tf_op jit(solution)/shard_map/expert_grad/pallas_call | solution.py:267
  112.1 1.0 collective-permute-start.19
  113.2 1.1 collective-permute-start.15
  114.2 1.0 collective-permute-start.18
  115.3 2.4 %collective-permute-start.17 = (bf16[128,1024]{1,0:T(8,128)(2,1)S(1)}, bf16[128,1024]{1,0:T(8,128)(2,1)S(1)}, u32[]{:S(2)}, u32[]{:S(2)}) collective-permute-start(bf16[128,1024]{1,0:T(8,128)(2,1)S(1)} %add_convert_fusion.1), channel_id=1, source_target_pairs={{0,24},{1,25},{2,26},{3,27},{4,28},{5,29},{6,30},{7,31},{8,16},{9,... | collective-permute-start | bytes 786440 | tf_op jit(solution)/shard_map/ppermute | solution.py:322
  117.7 3.8 %collective-permute-done.19 = bf16[128,1024]{1,0:T(8,128)(2,1)S(1)} collective-permute-done((bf16[128,1024]{1,0:T(8,128)(2,1)S(1)}, bf16[128,1024]{1,0:T(8,128)(2,1)S(1)}, u32[]{:S(2)}, u32[]{:S(2)}) %collective-permute-start.19) | collective-permute-done | bytes 262176 | tf_op jit(solution)/shard_map/ppermute | solution.py:322
  121.5 2.5 %collective-permute-start.20 = (bf16[128,1024]{1,0:T(8,128)(2,1)S(1)}, bf16[128,1024]{1,0:T(8,128)(2,1)S(1)}, u32[]{:S(2)}, u32[]{:S(2)}) collective-permute-start(bf16[128,1024]{1,0:T(8,128)(2,1)S(1)} %add_convert_fusion), channel_id=1, source_target_pairs={{0,24},{1,25},{2,26},{3,27},{4,28},{5,29},{6,30},{7,31},{8,16},{9,... | collective-permute-start | bytes 786440 | tf_op jit(solution)/shard_map/ppermute | solution.py:322
  124.1 3.0 %collective-permute-done.15.o1 = bf16[128,1024]{1,0:T(8,128)(2,1)S(1)} collective-permute-done((bf16[128,1024]{1,0:T(8,128)(2,1)S(1)}, bf16[128,1024]{1,0:T(8,128)(2,1)S(1)}, u32[]{:S(2)}, u32[]{:S(2)}) %collective-permute-start.15) | collective-permute-done | bytes 262176 | tf_op jit(solution)/shard_map/ppermute | solution.py:322
  127.1 4.1 %collective-permute-done.18.g1 = bf16[128,1024]{1,0:T(8,128)(2,1)S(1)} collective-permute-done((bf16[128,1024]{1,0:T(8,128)(2,1)S(1)}, bf16[128,1024]{1,0:T(8,128)(2,1)S(1)}, u32[]{:S(2)}, u32[]{:S(2)}) %collective-permute-start.18) | collective-permute-done | bytes 262176 | tf_op jit(solution)/shard_map/ppermute | solution.py:322
  131.2 8.4 %collective-permute-done.17.o2 = bf16[128,1024]{1,0:T(8,128)(2,1)S(1)} collective-permute-done((bf16[128,1024]{1,0:T(8,128)(2,1)S(1)}, bf16[128,1024]{1,0:T(8,128)(2,1)S(1)}, u32[]{:S(2)}, u32[]{:S(2)}) %collective-permute-start.17) | collective-permute-done | bytes 262176 | tf_op jit(solution)/shard_map/ppermute | solution.py:322
  139.6 3.5 %collective-permute-done.20.g2 = bf16[128,1024]{1,0:T(8,128)(2,1)S(1)} collective-permute-done((bf16[128,1024]{1,0:T(8,128)(2,1)S(1)}, bf16[128,1024]{1,0:T(8,128)(2,1)S(1)}, u32[]{:S(2)}, u32[]{:S(2)}) %collective-permute-start.20) | collective-permute-done | bytes 262176 | tf_op jit(solution)/shard_map/ppermute | solution.py:322
  143.1 1.1 finish.1
  (54 shorter events, 3.3 us)
Async XLA Ops:
  10.3 4.8 %copy-start.10 = (bf16[128,1024]{1,0:T(8,128)(2,1)S(1)}, bf16[128,1024]{1,0:T(8,128)(2,1)}, u32[]{:S(2)}) copy-start(bf16[128,1024]{1,0:T(8,128)(2,1)} %param.12) | copy-start | bytes 786436
  10.3 25.6 %collective-permute-start.9 = (bf16[5,2,3,32,512]{4,3,2,1,0:T(8,128)(2,1)S(1)}, bf16[5,2,3,32,512]{4,3,2,1,0:T(8,128)(2,1)S(1)}, u32[]{:S(2)}, u32[]{:S(2)}) collective-permute-start(bf16[5,2,3,32,512]{4,3,2,1,0:T(8,128)(2,1)S(1)} %constant_dynamic-slice_fusion.1), channel_id=1, source_target_pairs={{0,4},{1,5},{2,6},{3,7},{4,0},{5,1},{6,2},{7,3},{8,12},{9,13},{10,... | collective-permute-start | bytes 2949128 | tf_op jit(solution)/shard_map/ppermute | solution.py:322
  13.3 24.6 %copy-start.12 = (s32[128,4]{0,1:T(4,128)S(1)}, s32[128,4]{0,1:T(4,128)}, u32[]{:S(2)}) copy-start(s32[128,4]{0,1:T(4,128)} %param.17) | copy-start | bytes 6148
  13.3 24.6 %copy-start.13 = (f32[128,4]{0,1:T(4,128)S(1)}, f32[128,4]{0,1:T(4,128)}, u32[]{:S(2)}) copy-start(f32[128,4]{0,1:T(4,128)} %param.18) | copy-start | bytes 6148
  13.3 25.2 %copy-start = (bf16[128,1024]{1,0:T(8,128)(2,1)S(1)}, bf16[128,1024]{1,0:T(8,128)(2,1)}, u32[]{:S(2)}) copy-start(bf16[128,1024]{1,0:T(8,128)(2,1)} %cot_ref.1) | copy-start | bytes 786436
  13.3 47.6 %copy-start.2 = (bf16[1024,1024]{1,0:T(8,128)(2,1)S(1)}, bf16[1024,1024]{1,0:T(8,128)(2,1)}, u32[]{:S(2)}) copy-start(bf16[1024,1024]{1,0:T(8,128)(2,1)} %proj_ref.1) | copy-start | bytes 6291460
  14.9 46.1 %copy-start.1 = (f32[1024]{0:T(1024)S(1)}, f32[1024]{0:T(1024)}, u32[]{:S(2)}) copy-start(f32[1024]{0:T(1024)} %param.15) | copy-start | bytes 12292
  14.9 46.1 %copy-start.8 = (bf16[128,1024]{1,0:T(8,128)(2,1)S(1)}, bf16[128,1024]{1,0:T(8,128)(2,1)}, u32[]{:S(2)}) copy-start(bf16[128,1024]{1,0:T(8,128)(2,1)} %q_ref.1) | copy-start | bytes 786436
  14.9 46.1 %copy-start.9 = (bf16[128,1024]{1,0:T(8,128)(2,1)S(1)}, bf16[128,1024]{1,0:T(8,128)(2,1)}, u32[]{:S(2)}) copy-start(bf16[128,1024]{1,0:T(8,128)(2,1)} %stream_ref.1) | copy-start | bytes 786436
  14.9 45.5 %collective-permute-start.11 = (bf16[6,2,3,32,512]{4,3,2,1,0:T(8,128)(2,1)S(1)}, bf16[6,2,3,32,512]{4,3,2,1,0:T(8,128)(2,1)}, u32[]{:S(2)}, u32[]{:S(2)}) collective-permute-start(bf16[6,2,3,32,512]{4,3,2,1,0:T(8,128)(2,1)S(1)} %constant_dynamic-slice_fusion), channel_id=1, source_target_pairs={{0,4},{1,5},{2,6},{3,7},{4,0},{5,1},{6,2},{7,3},{8,12},{9,13},{10,... | collective-permute-start | bytes 3538952 | tf_op jit(solution)/shard_map/ppermute | solution.py:322
  15.1 22.9 %collective-permute-start = (bf16[256,1024]{1,0:T(8,128)(2,1)S(1)}, bf16[256,1024]{1,0:T(8,128)(2,1)S(1)}, u32[]{:S(2)}, u32[]{:S(2)}) collective-permute-start(bf16[256,1024]{1,0:T(8,128)(2,1)S(1)} %constant_dynamic-update-slice_fusion.refs_0_), channel_id=1, source_target_pairs={{0,2},{1,3},{2,0},{3,1},{4,6},{5,7},{6,4},{7,5},{8,10},{9,11},{10,... | collective-permute-start | bytes 1572872 | tf_op jit(solution)/shard_map/ppermute | solution.py:322
  35.9 24.6 %collective-permute-start.13 = (bf16[5,2,3,32,512]{4,3,2,1,0:T(8,128)(2,1)S(1)}, bf16[5,2,3,32,512]{4,3,2,1,0:T(8,128)(2,1)S(1)}, u32[]{:S(2)}, u32[]{:S(2)}) collective-permute-start(bf16[5,2,3,32,512]{4,3,2,1,0:T(8,128)(2,1)S(1)} %collective-permute-done.9.refs_9_.refs_11_), channel_id=1, source_target_pairs={{0,2},{1,3},{2,0},{3,1},{4,6},{5,7},{6,4},{7,5},{8,10},{9,11},{10,... | collective-permute-start | bytes 2949128 | tf_op jit(solution)/shard_map/ppermute | solution.py:322
  37.9 17.6 %collective-permute-start.1 = (bf16[256,1024]{1,0:T(8,128)(2,1)S(1)}, bf16[256,1024]{1,0:T(8,128)(2,1)S(1)}, u32[]{:S(2)}, u32[]{:S(2)}) collective-permute-start(bf16[256,1024]{1,0:T(8,128)(2,1)S(1)} %constant_dynamic-update-slice_fusion.refs_0_), channel_id=1, source_target_pairs={{0,1},{1,0},{2,3},{3,2},{4,5},{5,4},{6,7},{7,6},{8,9},{9,8},{10,11... | collective-permute-start | bytes 1572872 | tf_op jit(solution)/shard_map/ppermute | solution.py:322
  38.0 17.5 %collective-permute-start.2 = (bf16[256,1024]{1,0:T(8,128)(2,1)S(1)}, bf16[256,1024]{1,0:T(8,128)(2,1)S(1)}, u32[]{:S(2)}, u32[]{:S(2)}) collective-permute-start(bf16[256,1024]{1,0:T(8,128)(2,1)S(1)} %collective-permute-done.refs_1_), channel_id=1, source_target_pairs={{0,1},{1,0},{2,3},{3,2},{4,5},{5,4},{6,7},{7,6},{8,9},{9,8},{10,11... | collective-permute-start | bytes 1572872 | tf_op jit(solution)/shard_map/ppermute | solution.py:322
  38.6 11.0 %collective-permute-start.7 = (bf16[144,1024]{1,0:T(8,128)(2,1)S(1)}, bf16[144,1024]{1,0:T(8,128)(2,1)S(1)}, u32[]{:S(2)}, u32[]{:S(2)}) collective-permute-start(bf16[144,1024]{1,0:T(8,128)(2,1)S(1)} %pad_maximum_fusion.refs_4_.refs_0_), channel_id=1, source_target_pairs={{0,24},{1,25},{2,26},{3,27},{4,28},{5,29},{6,30},{7,31},{8,16},{9,... | collective-permute-start | bytes 884744 | tf_op jit(solution)/shard_map/ppermute | solution.py:322
  49.6 15.2 %collective-permute-start.6 = (bf16[144,1024]{1,0:T(8,128)(2,1)S(1)}, bf16[144,1024]{1,0:T(8,128)(2,1)S(1)}, u32[]{:S(2)}, u32[]{:S(2)}) collective-permute-start(bf16[144,1024]{1,0:T(8,128)(2,1)S(1)} %pad_maximum_fusion.refs_4_.refs_0_), channel_id=1, source_target_pairs={{0,8},{1,9},{2,10},{3,11},{4,12},{5,13},{6,14},{7,15},{8,0},{9,1},... | collective-permute-start | bytes 884744 | tf_op jit(solution)/shard_map/ppermute | solution.py:322
  55.5 13.1 %collective-permute-start.8 = (bf16[144,1024]{1,0:T(8,128)(2,1)S(1)}, bf16[144,1024]{1,0:T(8,128)(2,1)S(1)}, u32[]{:S(2)}, u32[]{:S(2)}) collective-permute-start(bf16[144,1024]{1,0:T(8,128)(2,1)S(1)} %collective-permute-done.7.refs_6_.refs_2_), channel_id=1, source_target_pairs={{0,8},{1,9},{2,10},{3,11},{4,12},{5,13},{6,14},{7,15},{8,0},{9,1},... | collective-permute-start | bytes 884744 | tf_op jit(solution)/shard_map/ppermute | solution.py:322
  55.5 32.0 %collective-permute-start.10 = (bf16[5,2,3,32,512]{4,3,2,1,0:T(8,128)(2,1)S(1)}, bf16[5,2,3,32,512]{4,3,2,1,0:T(8,128)(2,1)}, u32[]{:S(2)}, u32[]{:S(2)}) collective-permute-start(bf16[5,2,3,32,512]{4,3,2,1,0:T(8,128)(2,1)S(1)} %collective-permute-done.9.refs_9_.refs_11_), channel_id=1, source_target_pairs={{0,1},{1,0},{2,3},{3,2},{4,5},{5,4},{6,7},{7,6},{8,9},{9,8},{10,11... | collective-permute-start | bytes 2949128 | tf_op jit(solution)/shard_map/ppermute | solution.py:322
  60.5 27.1 %collective-permute-start.12 = (bf16[6,2,3,32,512]{4,3,2,1,0:T(8,128)(2,1)}, bf16[6,2,3,32,512]{4,3,2,1,0:T(8,128)(2,1)}, u32[]{:S(2)}, u32[]{:S(2)}) collective-permute-start(bf16[6,2,3,32,512]{4,3,2,1,0:T(8,128)(2,1)} %collective-permute-done.11.refs_11_.refs_13_), channel_id=1, source_target_pairs={{0,1},{1,0},{2,3},{3,2},{4,5},{5,4},{6,7},{7,6},{8,9},{9,8},{10,11... | collective-permute-start | bytes 3538952 | tf_op jit(solution)/shard_map/ppermute | solution.py:322
  60.5 4.3 %copy-start.3 = (bf16[5,2,3,32,512]{4,3,2,1,0:T(8,128)(2,1)}, bf16[5,2,3,32,512]{4,3,2,1,0:T(8,128)(2,1)S(1)}, u32[]{:S(2)}) copy-start(bf16[5,2,3,32,512]{4,3,2,1,0:T(8,128)(2,1)S(1)} %collective-permute-done.13.refs_13_.refs_15_) | copy-start | bytes 2949124
  60.5 27.0 %collective-permute-start.14 = (bf16[5,2,3,32,512]{4,3,2,1,0:T(8,128)(2,1)S(1)}, bf16[5,2,3,32,512]{4,3,2,1,0:T(8,128)(2,1)}, u32[]{:S(2)}, u32[]{:S(2)}) collective-permute-start(bf16[5,2,3,32,512]{4,3,2,1,0:T(8,128)(2,1)S(1)} %collective-permute-done.13.refs_13_.refs_15_), channel_id=1, source_target_pairs={{0,1},{1,0},{2,3},{3,2},{4,5},{5,4},{6,7},{7,6},{8,9},{9,8},{10,11... | collective-permute-start | bytes 2949128 | tf_op jit(solution)/shard_map/ppermute | solution.py:322
  64.8 12.1 %collective-permute-start.4 = (bf16[128,1024]{1,0:T(8,128)(2,1)}, bf16[128,1024]{1,0:T(8,128)(2,1)}, u32[]{:S(2)}, u32[]{:S(2)}) collective-permute-start(bf16[128,1024]{1,0:T(8,128)(2,1)} %get-tuple-element.15.refs_0_), channel_id=1, source_target_pairs={{0,24},{1,25},{2,26},{3,27},{4,28},{5,29},{6,30},{7,31},{8,16},{9,... | collective-permute-start | bytes 786440 | tf_op jit(solution)/shard_map/ppermute | solution.py:322
  69.4 12.6 %collective-permute-start.3 = (bf16[128,1024]{1,0:T(8,128)(2,1)}, bf16[128,1024]{1,0:T(8,128)(2,1)}, u32[]{:S(2)}, u32[]{:S(2)}) collective-permute-start(bf16[128,1024]{1,0:T(8,128)(2,1)} %get-tuple-element.15.refs_0_), channel_id=1, source_target_pairs={{0,8},{1,9},{2,10},{3,11},{4,12},{5,13},{6,14},{7,15},{8,0},{9,1},... | collective-permute-start | bytes 786440 | tf_op jit(solution)/shard_map/ppermute | solution.py:322
  76.9 10.6 %collective-permute-start.5 = (bf16[128,1024]{1,0:T(8,128)(2,1)}, bf16[128,1024]{1,0:T(8,128)(2,1)}, u32[]{:S(2)}, u32[]{:S(2)}) collective-permute-start(bf16[128,1024]{1,0:T(8,128)(2,1)} %collective-permute-done.4.refs_2_), channel_id=1, source_target_pairs={{0,8},{1,9},{2,10},{3,11},{4,12},{5,13},{6,14},{7,15},{8,0},{9,1},... | collective-permute-start | bytes 786440 | tf_op jit(solution)/shard_map/ppermute | solution.py:322
  80.9 20.1 %copy-start.4 = (bf16[5,2,3,32,512]{4,3,2,1,0:T(8,128)(2,1)S(1)}, bf16[5,2,3,32,512]{4,3,2,1,0:T(8,128)(2,1)}, u32[]{:S(2)}) copy-start(bf16[5,2,3,32,512]{4,3,2,1,0:T(8,128)(2,1)} %copy-done.3) | copy-start | bytes 2949124
  88.5 12.5 %copy-start.7 = (bf16[144,1024]{1,0:T(8,128)(2,1)S(1)}, bf16[144,1024]{1,0:T(8,128)(2,1)}, u32[]{:S(2)}) copy-start(bf16[144,1024]{1,0:T(8,128)(2,1)} %copy-done.5) | copy-start | bytes 884740
  99.9 15.4 %collective-permute-start.16 = (bf16[128,1024]{1,0:T(8,128)(2,1)S(1)}, bf16[128,1024]{1,0:T(8,128)(2,1)S(1)}, u32[]{:S(2)}, u32[]{:S(2)}) collective-permute-start(bf16[128,1024]{1,0:T(8,128)(2,1)S(1)} %get-tuple-element.19), channel_id=1, source_target_pairs={{0,8},{1,9},{2,10},{3,11},{4,12},{5,13},{6,14},{7,15},{8,0},{9,1},... | collective-permute-start | bytes 786440 | tf_op jit(solution)/shard_map/ppermute | solution.py:322
  112.1 9.3 %collective-permute-start.19 = (bf16[128,1024]{1,0:T(8,128)(2,1)S(1)}, bf16[128,1024]{1,0:T(8,128)(2,1)S(1)}, u32[]{:S(2)}, u32[]{:S(2)}) collective-permute-start(bf16[128,1024]{1,0:T(8,128)(2,1)S(1)} %get-tuple-element.25), channel_id=1, source_target_pairs={{0,8},{1,9},{2,10},{3,11},{4,12},{5,13},{6,14},{7,15},{8,0},{9,1},... | collective-permute-start | bytes 786440 | tf_op jit(solution)/shard_map/ppermute | solution.py:322
  113.2 13.9 %collective-permute-start.15 = (bf16[128,1024]{1,0:T(8,128)(2,1)S(1)}, bf16[128,1024]{1,0:T(8,128)(2,1)S(1)}, u32[]{:S(2)}, u32[]{:S(2)}) collective-permute-start(bf16[128,1024]{1,0:T(8,128)(2,1)S(1)} %get-tuple-element.17), channel_id=1, source_target_pairs={{0,8},{1,9},{2,10},{3,11},{4,12},{5,13},{6,14},{7,15},{8,0},{9,1},... | collective-permute-start | bytes 786440 | tf_op jit(solution)/shard_map/ppermute | solution.py:322
  114.2 16.9 %collective-permute-start.18 = (bf16[128,1024]{1,0:T(8,128)(2,1)S(1)}, bf16[128,1024]{1,0:T(8,128)(2,1)S(1)}, u32[]{:S(2)}, u32[]{:S(2)}) collective-permute-start(bf16[128,1024]{1,0:T(8,128)(2,1)S(1)} %get-tuple-element.23), channel_id=1, source_target_pairs={{0,8},{1,9},{2,10},{3,11},{4,12},{5,13},{6,14},{7,15},{8,0},{9,1},... | collective-permute-start | bytes 786440 | tf_op jit(solution)/shard_map/ppermute | solution.py:322
  115.3 24.3 %collective-permute-start.17 = (bf16[128,1024]{1,0:T(8,128)(2,1)S(1)}, bf16[128,1024]{1,0:T(8,128)(2,1)S(1)}, u32[]{:S(2)}, u32[]{:S(2)}) collective-permute-start(bf16[128,1024]{1,0:T(8,128)(2,1)S(1)} %add_convert_fusion.1), channel_id=1, source_target_pairs={{0,24},{1,25},{2,26},{3,27},{4,28},{5,29},{6,30},{7,31},{8,16},{9,... | collective-permute-start | bytes 786440 | tf_op jit(solution)/shard_map/ppermute | solution.py:322
  121.5 21.5 %collective-permute-start.20 = (bf16[128,1024]{1,0:T(8,128)(2,1)S(1)}, bf16[128,1024]{1,0:T(8,128)(2,1)S(1)}, u32[]{:S(2)}, u32[]{:S(2)}) collective-permute-start(bf16[128,1024]{1,0:T(8,128)(2,1)S(1)} %add_convert_fusion), channel_id=1, source_target_pairs={{0,24},{1,25},{2,26},{3,27},{4,28},{5,29},{6,30},{7,31},{8,16},{9,... | collective-permute-start | bytes 786440 | tf_op jit(solution)/shard_map/ppermute | solution.py:322
  (3 other events, 3.4 us)

commit v2 on v0

v2 whole, which is shorter than its diff:
```python
import functools
import math

import jax
import jax.numpy as jnp
from jax import lax
from jax.experimental import pallas as pl
from jax.experimental.pallas import tpu as pltpu
from jax.sharding import PartitionSpec as P

HS = 64
LANES = 128
CHUNK = 32
NORM_EPS = 1e-06
MIB = 1 << 20
OPT = dict(cut=4, kv="first", vm=40, att=60, order=True)
F32, BF16 = jnp.float32, jnp.bfloat16


def dot(a, b, contract=((1,), (0,))):
    return lax.dot_general(a, b, (contract, ((), ())), preferred_element_type=F32)


def params(mebibytes=16):
    return pltpu.CompilerParams(vmem_limit_bytes=mebibytes * MIB)


def vmem_specs(count):
    return [pl.BlockSpec(memory_space=pltpu.VMEM)] * count


COSTS = dict(after=0, split_pieces=0, split_experts=8, attention=0, routing=0, expert_out=0, expert_grad=0, out_sum=20, grad_sum=0)


def cost(name):
    return pl.CostEstimate(flops=int(1e6 + 1e9 * COSTS[name]), bytes_accessed=10000, transcendentals=0)


def split_kernel(rows_ref, _, o_ref, done_ref):
    put_apart(rows_ref, o_ref)
    done_ref[...] = jnp.zeros_like(done_ref)


def put_apart(rows_ref, o_ref):
    for part in range(rows_ref.shape[1]):
        by_expert = jnp.swapaxes(rows_ref[:, part], 0, 1)
        for expert in range(by_expert.shape[0]):
            o_ref[expert, part] = by_expert[expert]


def split_experts(by_part, earlier):
    depth, parts, local, hidden = by_part.shape
    rows = 4 * CHUNK
    return pl.pallas_call(
        split_kernel,
        grid=(depth // rows,),
        in_specs=[
            pl.BlockSpec((rows, parts, local, hidden), lambda i: (i, 0, 0, 0)),
            pl.BlockSpec(memory_space=pl.ANY),
        ],
        out_specs=[
            pl.BlockSpec((local, parts, rows, hidden), lambda i: (0, 0, i, 0)),
            pl.BlockSpec((8, LANES), lambda i: (0, 0)),
        ],
        out_shape=[
            jax.ShapeDtypeStruct((local, parts, depth, hidden), BF16),
            jax.ShapeDtypeStruct((8, LANES), F32),
        ],
        compiler_params=params(60),
        cost_estimate=cost("split_experts"),
        name="split_experts",
    )(by_part, earlier)


def split_pieces_kernel(counts, base, table_ref, w_ref, *refs):
    refs = refs[-2 * len(counts) - 1 :]
    out_refs, scratch, sems = refs[: len(counts)], refs[len(counts) : -1], refs[-1]
    copies = []
    for place, count in enumerate(counts):
        at = pl.multiple_of(table_ref[base + place] * CHUNK, CHUNK)
        copies.append(
            pltpu.make_async_copy(
                w_ref.at[pl.ds(at, count * CHUNK)], scratch[place], sems.at[place]
            )
        )
        copies[-1].start()
    for place, copy in enumerate(copies):
        copy.wait()
        put_apart(scratch[place], out_refs[place])


def split_pieces(by_part, table, base, counts, *earlier):
    _, parts, local, hidden = by_part.shape
    shapes = [(local, parts, count * CHUNK, hidden) for count in counts]
    return pl.pallas_call(
        functools.partial(split_pieces_kernel, counts, base),
        in_specs=[pl.BlockSpec(memory_space=pltpu.SMEM), pl.BlockSpec(memory_space=pltpu.HBM)]
        + [pl.BlockSpec(memory_space=pl.ANY)] * len(earlier),
        out_specs=vmem_specs(len(counts)),
        out_shape=[jax.ShapeDtypeStruct(shape, BF16) for shape in shapes],
        scratch_shapes=[
            pltpu.VMEM((count * CHUNK, parts, local, hidden), BF16) for count in counts
        ]
        + [pltpu.SemaphoreType.DMA((len(counts),))],
        compiler_params=params(60),
        cost_estimate=cost("split_pieces"),
        name="split_pieces",
    )(table, by_part, *earlier)


def attention_kernel(count, gain_ref, meta_ref, q_hbm, stream_hbm, proj_hbm, *refs):
    k_refs, v_refs = refs[:count], refs[count : 2 * count]
    mix_ref, normed_ref, query, stream, proj, attended, all_keys, all_values, sems = refs[2 * count :]
    rows, width = query.shape
    pairs = [(q_hbm, query)] + blocks_of(k_refs, all_keys) + blocks_of(v_refs, all_values)
    copies = load(pairs + [(stream_hbm, stream), (proj_hbm, proj)], sems)
    wait(copies[:-2])
    first = lax.broadcasted_iota(jnp.int32, (rows, LANES), 1) < HS
    for pair in range(width // LANES):
        cols = slice(pair * LANES, (pair + 1) * LANES)
        scaled = query[:, cols] * jnp.asarray(1.0 / math.sqrt(HS), BF16)
        zero = jnp.zeros_like(scaled)
        both = jnp.concatenate([jnp.where(first, scaled, zero), jnp.where(first, zero, scaled)], axis=0)
        scores = dot(both, all_keys[:, cols], ((1,), (1,)))
        raw = jnp.exp(scores - jnp.max(scores, axis=1, keepdims=True))
        total = jnp.sum(raw, axis=1, keepdims=True)
        mixed = dot(raw.astype(BF16), all_values[:, cols]) / total
        attended[:, cols] = jnp.where(first, mixed[:rows], mixed[rows:]).astype(BF16)
    wait(copies[-2:])
    mix = (stream[...].astype(F32) + dot(attended[...], proj[...])).astype(BF16)
    mix_ref[...] = mix
    wide = mix.astype(F32)
    inverse = lax.rsqrt(jnp.mean(wide * wide, axis=1, keepdims=True) + NORM_EPS)
    normed_ref[:rows] = (gain_ref[...] * wide * inverse).astype(BF16)
    normed_ref[rows:] = meta_ref[...]


def attention(queries, stream, out_proj, norm_gain, meta, key_blocks, value_blocks):
    rows, width = stream.shape
    length = len(key_blocks) * rows
    outs = [jax.ShapeDtypeStruct((n, width), BF16) for n in (rows, rows + meta.shape[0])]
    loads = [queries, stream, out_proj, *key_blocks, *value_blocks]
    scratch = [(rows, width), (rows, width), out_proj.shape, (rows, width), (length, width), (length, width)]
    return pl.pallas_call(
        functools.partial(attention_kernel, len(key_blocks)),
        in_specs=vmem_specs(2) + [pl.BlockSpec(memory_space=pl.ANY)] * len(loads),
        out_specs=vmem_specs(2),
        out_shape=outs,
        scratch_shapes=[pltpu.VMEM(shape, BF16) for shape in scratch]
        + [pltpu.SemaphoreType.DMA((len(loads),))],
        compiler_params=params(OPT["att"]),
        cost_estimate=cost("attention"),
        name="attention",
    )(norm_gain[None, :], meta, *loads)


def routing_kernel(experts, local, slots, where_ref, *refs):
    x_refs, (pick_ref, put_ref, gate_ref, meta_refs, sems) = refs[:4], refs[4:]
    lines, rows = meta_refs.shape[1:]
    copies = []
    for place, ref in enumerate(x_refs):
        source = ref.at[pl.ds(ref.shape[0] - lines, lines), pl.ds(0, rows)]
        copies.append(pltpu.make_async_copy(source, meta_refs.at[place], sems.at[place]))
        copies[-1].start()
    wait(copies)
    choice, member = where_ref[0], where_ref[1]
    members = experts // local
    blocks = len(x_refs)
    top = lines // 4
    names = []
    for place in range(blocks):
        meta = meta_refs[place].astype(F32)
        line = lax.broadcasted_iota(jnp.int32, meta.shape, 0)
        names.append(jnp.sum(jnp.where(line == choice, meta, 0.0), axis=0, keepdims=True))
        gate = jnp.where((line >= top) & (lax.rem(line, top) == choice), meta, 0.0)
        gate = jnp.broadcast_to(jnp.sum(gate, axis=0, keepdims=True), (rows, rows))
        gate_ref[place * rows : (place + 1) * rows] = jnp.transpose(gate)
    names = jnp.concatenate(names, axis=1)
    count = blocks * rows
    named = names.astype(jnp.int32) - choice * experts
    chosen = named == lax.broadcasted_iota(jnp.int32, (max(experts, 8), count), 0)
    earlier = lax.broadcasted_iota(jnp.int32, (count, count), 0) < lax.broadcasted_iota(
        jnp.int32, (count, count), 1
    )
    rank = dot(
        jnp.where(chosen, 1.0, 0.0).astype(BF16), jnp.where(earlier, 1.0, 0.0).astype(BF16)
    )
    rank = jnp.sum(jnp.where(chosen, rank, 0.0), axis=0, keepdims=True)
    slot = jnp.zeros_like(rank)
    for expert in range(experts):
        step = lax.rem(expert // local - member + members, members)
        base = ((step * local + expert % local) * slots).astype(F32)
        slot = jnp.where(named == expert, rank + base, slot)
    total = pick_ref.shape[0]
    hit = slot.astype(jnp.int32) == lax.broadcasted_iota(jnp.int32, (total, count), 0)
    pick_ref[...] = jnp.where(hit, 1.0, 0.0).astype(BF16)
    for place in range(blocks):
        part = slice(place * rows, (place + 1) * rows)
        column = jnp.transpose(jnp.broadcast_to(slot[:, part], (rows, rows)))[:, :1]
        hit = column.astype(jnp.int32) == lax.broadcasted_iota(jnp.int32, (rows, total), 1)
        put_ref[part] = jnp.where(hit, 1.0, 0.0).astype(BF16)


def routing(where, routed, rows, top, experts, local, slots):
    blocks = len(routed)
    total = experts * slots
    outs = (
        jax.ShapeDtypeStruct((total, blocks * rows), BF16),
        jax.ShapeDtypeStruct((blocks * rows, total), BF16),
        jax.ShapeDtypeStruct((blocks * rows, rows), F32),
    )

    return pl.pallas_call(
        functools.partial(routing_kernel, experts, local, slots),
        in_specs=[pl.BlockSpec(memory_space=pltpu.SMEM)]
        + [pl.BlockSpec(memory_space=pltpu.HBM)] * blocks,
        out_specs=vmem_specs(3),
        out_shape=outs,
        scratch_shapes=[pltpu.VMEM((blocks, 4 * top, rows), BF16), pltpu.SemaphoreType.DMA((blocks,))],
        compiler_params=params(),
        cost_estimate=cost("routing"),
        name="routing",
    )(where, *routed)


def take_refs(refs, counts):
    taken = []
    for count in counts:
        taken.append(refs[:count])
        refs = refs[count:]
    return taken


def weight_scratch(weight_sets):
    local, parts, _, hidden = weight_sets[0][0].shape
    depth = sum(piece.shape[2] for piece in weight_sets[0])
    most = max(len(each) for each in weight_sets)
    return [
        pltpu.VMEM((2, local, parts, depth, hidden), BF16),
        pltpu.SemaphoreType.DMA((2, local, most)),
    ]


def each_expert(start_ref, w_refs, set_sizes, buffer, sems, prepare, body):
    local = buffer.shape[1]

    def copies(index, expert):
        before, slot = sum(set_sizes[:index]), index % 2
        made = []
        for place in range(set_sizes[index]):
            ref = w_refs[before + place]
            at = pl.multiple_of(start_ref[4 + before + place] * CHUNK, CHUNK)
            target = buffer.at[slot, expert, :, pl.ds(at, ref.shape[2]), :]
            made.append(
                pltpu.make_async_copy(ref.at[expert], target, sems.at[slot, expert, place])
            )
        return made

    def start(index):
        if index < len(set_sizes):
            for expert in range(local):
                for copy in copies(index, expert):
                    copy.start()

    start(0)
    start(1)
    prepare()
    for index in range(len(set_sizes)):
        for expert in range(local):
            for copy in copies(index, expert):
                copy.wait()
            body(index * local + expert, buffer.at[index % 2, expert])
        start(index + 2)


def load(pairs, sems):
    copies = [
        pltpu.make_async_copy(source, target, sems.at[place])
        for place, (source, target) in enumerate(pairs)
    ]
    for copy in copies:
        copy.start()
    return copies


def wait(copies):
    for copy in copies:
        copy.wait()


def blocks_of(refs, every):
    rows = every.shape[0] // len(refs)
    return [
        (ref.at[pl.ds(0, rows)], every.at[pl.ds(place * rows, rows)])
        for place, ref in enumerate(refs)
    ]


def spread_rows(put, gates, made, own_ref, across_ref, *pair_refs):
    total = dot(put[...], made[...])
    rows = own_ref.shape[0]

    def block(place):
        part = slice(place * rows, (place + 1) * rows)
        return (gates[part, :1] * total[part]).astype(BF16)

    own_ref[...] = block(0)
    across_ref[...] = block(2)
    if len(pair_refs) == 1:
        pair_refs[0][:rows] = block(3)
        pair_refs[0][rows:] = block(1)
    else:
        pair_refs[0][...] = block(3)
        pair_refs[1][...] = block(1)


def out_kernel(set_sizes, slots, start_ref, pick_hbm, put_hbm, gate_hbm, *refs):
    x_refs, w_refs, out_refs, kept_refs, rest = take_refs(refs, (4, sum(set_sizes), 3, 2, 10))
    pick, put, gates, every, act, slope, rows, load_sems, buffer, sems = rest
    kept = []

    def prepare():
        wait(first)
        rows[...] = dot(pick[...], every[...]).astype(BF16)

    def body(place, weights):
        part = pl.ds(place * slots, slots)
        gate = dot(rows[part], weights[0])
        up = dot(rows[part], weights[1])
        sigmoid = 1.0 / (1.0 + jnp.exp(-gate))
        active = gate * sigmoid
        act[part] = active.astype(BF16)
        slope[part] = (up * (sigmoid * (1.0 + gate * (1.0 - sigmoid)))).astype(BF16)
        kept.extend(
            load(
                [(act.at[part], kept_refs[0].at[part]), (slope.at[part], kept_refs[1].at[part])],
                load_sems.at[pl.ds(7 + 2 * place, 2)],
            )
        )
        hidden = (active * up).astype(BF16)
        rows[part] = dot(hidden, weights[2], ((1,), (1,))).astype(BF16)

    first = load([(pick_hbm, pick)] + blocks_of(x_refs, every), load_sems)
    later = load([(put_hbm, put), (gate_hbm, gates)], load_sems.at[pl.ds(5, 2)])
    each_expert(start_ref, w_refs, set_sizes, buffer, sems, prepare, body)
    wait(later)
    spread_rows(put, gates, rows, *out_refs)
    wait(kept)


def grad_kernel(set_sizes, slots, start_ref, pick_hbm, put_hbm, gate_hbm, *refs):
    c_refs, kept_refs, w_refs, out_refs, rest = take_refs(refs, (4, 2, sum(set_sizes), 4, 10))
    pick, put, gates, every, act, slope, rows, load_sems, buffer, sems = rest

    def prepare():
        wait(first)
        rows[...] = dot(pick[...], every[...]).astype(BF16)
        wait(kept)

    def body(place, weights):
        part = pl.ds(place * slots, slots)
        back_hidden = dot(rows[part], weights[2])
        gate = (back_hidden * slope[part].astype(F32)).astype(BF16)
        up = (back_hidden * act[part].astype(F32)).astype(BF16)
        result = dot(gate, weights[0], ((1,), (1,))) + dot(up, weights[1], ((1,), (1,)))
        rows[part] = result.astype(BF16)

    first = load([(pick_hbm, pick)] + blocks_of(c_refs, every), load_sems)
    kept = load([(kept_refs[0], act), (kept_refs[1], slope)], load_sems.at[pl.ds(7, 2)])
    later = load([(put_hbm, put), (gate_hbm, gates)], load_sems.at[pl.ds(5, 2)])
    each_expert(start_ref, w_refs, set_sizes, buffer, sems, prepare, body)
    wait(later)
    spread_rows(put, gates, rows, *out_refs)


def whole(array):
    return pl.BlockSpec(array.shape, lambda i: (0,) * array.ndim)


def expert_call(kernel, name, ways, blocks, kept, weight_sets, table, slots, keep):
    pieces = [piece for each in weight_sets for piece in each]
    rows, width = ways[1].shape[0] // len(blocks), blocks[0].shape[1]
    shapes = [jax.ShapeDtypeStruct((n * rows, width), BF16) for n in ((1, 1, 2) if keep else (1, 1, 1, 1))]
    count, hidden = ways[0].shape[0], pieces[0].shape[3]
    keeps = [jax.ShapeDtypeStruct((count, hidden), BF16)] * 2
    anywhere, far_off = pl.BlockSpec(memory_space=pl.ANY), pl.BlockSpec(memory_space=pltpu.HBM)
    return pl.pallas_call(
        functools.partial(kernel, tuple(len(each) for each in weight_sets), slots),
        grid=(1,),
        in_specs=[pl.BlockSpec(memory_space=pltpu.SMEM)]
        + [anywhere] * len(ways)
        + [far_off] * len(blocks)
        + [anywhere] * (len(kept) + len(weight_sets[0]))
        + [far_off] * (len(pieces) - len(weight_sets[0])),
        out_specs=[whole(v) for v in shapes] + [anywhere] * (2 * keep),
        out_shape=shapes + keeps * keep,
        scratch_shapes=[pltpu.VMEM(v.shape, v.dtype) for v in ways]
        + [pltpu.VMEM((len(blocks) * rows, width), BF16)]
        + [pltpu.VMEM(v.shape, v.dtype) for v in keeps]
        + [
            pltpu.VMEM((count, width), BF16),
            pltpu.SemaphoreType.DMA((7 + 2 * (count // slots),)),
        ]
        + weight_scratch(weight_sets),
        compiler_params=params(OPT["vm"]),
        cost_estimate=cost(name),
        name=name,
    )(table, *ways, *blocks, *kept, *pieces)


def out_sum_kernel(mix_ref, own_ref, beside_ref, merged_ref, out_ref):
    rows = mix_ref.shape[0]
    total = own_ref[...].astype(F32) + beside_ref[rows:].astype(F32) + merged_ref[...].astype(F32)
    out_ref[...] = (mix_ref[...].astype(F32) + total).astype(BF16)


def grad_sum_kernel(mix_ref, cot_ref, gain_ref, own_ref, beside_ref, merged_ref, grad_ref):
    wide = mix_ref[...].astype(F32)
    inverse = lax.rsqrt(jnp.mean(wide * wide, axis=1, keepdims=True) + NORM_EPS)
    total = own_ref[...].astype(F32) + beside_ref[...].astype(F32) + merged_ref[...].astype(F32)
    weighted = gain_ref[...] * total
    scaled = wide * inverse
    grad_ref[...] = (
        cot_ref[...].astype(F32)
        + inverse * (weighted - scaled * jnp.mean(weighted * scaled, axis=1, keepdims=True))
    ).astype(BF16)


def finish(kernel, name, *arrays):
    return pl.pallas_call(
        kernel,
        in_specs=vmem_specs(len(arrays)),
        out_specs=vmem_specs(1)[0],
        out_shape=jax.ShapeDtypeStruct(arrays[0].shape, BF16),
        compiler_params=params(),
        cost_estimate=cost(name),
        name=name,
    )(*arrays)


def nothing(*refs):
    pass


def after(arrays, *earlier):
    count = len(arrays)
    return pl.pallas_call(
        nothing,
        in_specs=[pl.BlockSpec(memory_space=pl.ANY)] * (count + len(earlier)),
        out_specs=[pl.BlockSpec(memory_space=pl.ANY)] * count,
        out_shape=[jax.ShapeDtypeStruct(v.shape, v.dtype) for v in arrays],
        input_output_aliases={place: place for place in range(count)},
        compiler_params=params(),
        cost_estimate=cost("after"),
        name="after",
    )(*arrays, *earlier)


class Moves:
    def __init__(self, groups, heads, top):
        self.shape = (top, groups // top, heads // 2, 2)

    def send(self, array, target):
        top, members, chips, cores = self.shape
        pairs = []
        for index in range(math.prod(self.shape)):
            core = index % cores
            chip = index // cores % chips
            member = index // (cores * chips) % members
            choice = index // (cores * chips * members)
            k, m, h, c = target(choice, member, chip, core)
            pairs.append((index, ((k * members + m) * chips + h) * cores + c))
        return lax.ppermute(array, ("rcv", "hd"), pairs)

    def other_core(self, array):
        return self.send(array, lambda k, m, h, c: (k, m, h, 1 - c))

    def next_chip(self, array, step):
        return self.send(array, lambda k, m, h, c: (k, m, (h + step) % self.shape[2], c))

    def other_member(self, array):
        return self.send(array, lambda k, m, h, c: (k, 1 - m, h, c))

    def partner(self, array):
        return self.send(array, lambda k, m, h, c: (k ^ 1, m, h, c))

    def mirror(self, array):
        return self.send(array, lambda k, m, h, c: (3 - k, m, h, c))


def scatter_choices(moves, own, across, *pair):
    rows = own.shape[0]
    pair = [moves.partner(each) for each in pair]
    merged = (across.astype(F32) + pair[0][:rows].astype(F32)).astype(BF16)
    return own, pair[-1], merged


def staged(moves, weights):
    _, members, chips, _ = moves.shape
    return (members, chips) == (2, 2) and weights.shape[0] % (16 * CHUNK) == 0


def piece_plan(depth):
    total = depth // CHUNK
    cut = OPT['cut'] * total // 32
    shared = total // 2 - 2 * cut
    return cut, shared, lambda h, c: 2 * shared + (h * 2 + c) * cut, lambda c: c * shared


def gathered_weights(moves, weights):
    top, members, _, _ = moves.shape
    if members == 1:
        return []
    groups = [[k * members + m for m in range(members)] for k in range(top)]
    every = lax.all_gather(weights, "rcv", axis_index_groups=groups)
    me = lax.axis_index("rcv") % members
    return [
        [lax.dynamic_index_in_dim(every, (me + step) % members, 0, keepdims=False)]
        for step in range(1, members)
    ]


def routing_rows(expert_ids, gate_weights, width):
    names = expert_ids.T.astype(F32)
    gate = gate_weights.T
    high = lax.reduce_precision(gate, 8, 7)
    middle = lax.reduce_precision(gate - high, 8, 7)
    low = gate - high - middle
    rows = jnp.concatenate([names, high, middle, low], axis=0).astype(BF16)
    return jnp.pad(rows, ((0, 0), (0, width - rows.shape[1])))


def per_device(
    stream,
    queries,
    keys,
    values,
    out_proj,
    norm_gain,
    expert_weights,
    expert_ids,
    gate_weights,
    out_cotangent,
):
    rows, width = stream.shape
    groups, heads = lax.axis_size("rcv"), lax.axis_size("hd")
    local = expert_weights.shape[1]
    top = expert_ids.shape[1]
    experts = local * groups
    capacity = (5 * rows * top + 4 * experts - 1) // (4 * experts)
    slots = (top * capacity + 15) // 16 * 16
    moves = Moves(groups, heads, top)
    members = groups // top
    choice, member = lax.axis_index("rcv") // members, lax.axis_index("rcv") % members
    chip, core = lax.axis_index("hd") // 2, lax.axis_index("hd") % 2

    by_part = jnp.transpose(expert_weights, (0, 2, 1, 3))
    in_parts = staged(moves, by_part)
    cut, shared, cut_at, shared_at = piece_plan(width)
    first_cut, first_shared = cut_at(chip, core), shared_at(core)
    places = [0, first_cut, cut_at(chip, 1 - core), first_shared, shared_at(1 - core)]
    places += [cut_at(1 - chip, core), cut_at(1 - chip, 1 - core)]
    if not in_parts:
        places = [0] * members
    table = jnp.stack([choice, member, first_cut, first_shared] + places).astype(jnp.int32)
    if in_parts:
        (one,) = split_pieces(by_part, table, 2, (cut,))
        if OPT["kv"] == "after":
            keys, values, out_cotangent = after([keys, values, out_cotangent], one)
        one = moves.other_member(one)

    hops = range(1, heads // 2)
    far_keys = [moves.next_chip(keys, step) for step in hops]
    far_values = [moves.next_chip(values, step) for step in hops]
    core_keys, core_values = moves.other_core(keys), moves.other_core(values)
    cot = out_cotangent
    cot_across, cot_beside = moves.mirror(cot), moves.partner(cot)
    if in_parts:
        (both,) = split_pieces(by_part, table, 3, (shared,), far_keys[0])
        both = moves.other_member(both)
    far_core_keys = [moves.other_core(each) for each in far_keys]
    far_core_values = [moves.other_core(each) for each in far_values]
    mix, normed = attention(
        queries,
        stream,
        out_proj,
        norm_gain,
        routing_rows(expert_ids, gate_weights, width),
        [keys, core_keys] + far_keys + far_core_keys,
        [values, core_values] + far_values + far_core_values,
    )

    (normed,) = after([normed], cot_across, cot_beside)
    across, beside = moves.mirror(normed), moves.partner(normed)
    if in_parts:
        (one,) = after([one], normed)
        other = moves.next_chip(one, 1)
        one_core = moves.other_core(one)
    weights, done = split_experts(by_part, normed)
    (cot_forward,) = after([cot_across], normed)
    cot_parts = [cot, cot_beside, cot_across, moves.partner(cot_forward)]
    (across,) = after([across], done, cot_parts[3])
    far = moves.partner(across)
    x_parts = [normed, beside, across, far]
    pick, put, gates = routing(table, x_parts, rows, top, experts // top, local, slots)
    sets = [[weights]]
    if in_parts:
        both, other = after([both, other], far, beside)
        sets.append(
            [one, one_core, both, moves.other_core(both), other, moves.other_core(other)]
        )
    else:
        sets += gathered_weights(moves, weights)
    ways = (pick, put, gates)
    *outs, active, slope = expert_call(
        out_kernel, "expert_out", ways, x_parts, (), sets, table, slots, True
    )
    outs = scatter_choices(moves, *outs)
    block_out = finish(out_sum_kernel, "out_sum", mix, *outs[:2], moves.mirror(outs[2]))
    grads = expert_call(
        grad_kernel, "expert_grad", ways, cot_parts, (active, slope), sets, table, slots, False
    )
    if OPT["order"]:
        grads = [*grads[:2], *after(grads[2:], outs[2])]
    grads = scatter_choices(moves, *grads)
    stream_grad = finish(
        grad_sum_kernel, "grad_sum", mix, out_cotangent, norm_gain[None, :], *grads[:2], moves.mirror(grads[2])
    )
    return block_out, stream_grad


def solution(mesh):
    row = P(("rcv", "hd"), None)
    placed = (row, row, row, row, P(), P(), P(None, "rcv", None, None), row, row, row)
    return jax.shard_map(
        per_device, mesh=mesh, in_specs=placed, out_specs=(row, row), check_vma=False
    )
```

time: 228 us -> 121 us (0.53)
  waiting for transfers between devices: 111 us -> 35.8 us
  local copies, waits for them, and re-layouts: 52 us -> 2.84 us
  Pallas kernels: 0 us -> 44.7 us
  other arithmetic: 15.8 us -> 0.76 us
  matrix products: 13.7 us -> 0 us
    all_to_all x8 -> x0, waiting for transfers between devices: 111 us -> none  [the longest x1 28.7 us: per_device(): lax.all_to_all(pack_rows(normed), 'rcv', split_axis=1, concat_axis=1, til...]
    pallas_call x0 -> x15, Pallas kernels: none -> 44.7 us  [the longest x2 19.4 us: expert_call(): pl.pallas_call(functools.partial(kernel, tuple((len(each) for each in wei...]
    ppermute x0 -> x23, waiting for transfers between devices: none -> 35.8 us  [send(): return lax.ppermute(array, ('rcv', 'hd'), pairs)]
    ppermute x0 -> x23, starting transfers between devices: none -> 35.1 us  [send(): return lax.ppermute(array, ('rcv', 'hd'), pairs)]
    all_to_all x8 -> x0, starting transfers between devices: 33.4 us -> none  [the longest x1 6.45 us: per_device(): lax.all_to_all(pack_rows(normed), 'rcv', split_axis=1, concat_axis=1, til...]
    dot_general x7 -> x0, matrix products: 13.7 us -> none  [the longest x1 3.4 us: expert_pass(): jnp.einsum('jmd,djcf->jmcf', arrived_rows, expert_weights[:, :, :2], pref...]
    gather x4 -> x0, local copies, waits for them, and re-layouts: 12.5 us -> none  [the longest x2 6.94 us: pack_rows(): jnp.take(padded, source, axis=0)]
    slice x3 -> x0, local copies, waits for them, and re-layouts: 11.8 us -> none  [the longest x1 7.01 us: expert_pass(): expert_weights[:, :, :2]]
  transfers between devices with their start and end apart: 8 -> 23, of which waited for: 8 -> 10; matrix products, arithmetic and copies ran while one was open for 16% -> 2% of each run, Pallas kernels for 0% -> 28%
where the time goes in v2:
time: 121 us; the launch traced here: 120 us
  Pallas kernels  44.7 us (37%)
  waiting for transfers between devices  35.8 us (30%)
  starting transfers between devices  35.1 us (29%)
  local copies, waits for them, and re-layouts  2.84 us (2%)
    ppermute x23, waiting for transfers between devices, send(): return lax.ppermute(array, ('rcv', 'hd'), pairs)  35.8 us
    ppermute x23, starting transfers between devices, send(): return lax.ppermute(array, ('rcv', 'hd'), pairs)  35.1 us
    pallas_call x2, Pallas kernels, expert_call(): pl.pallas_call(functools.partial(kernel, tuple((len(each) for each in wei...  19.4 us
    pallas_call x1, Pallas kernels, split_experts(): pl.pallas_call(split_kernel, grid=(depth // rows,), in_specs=[pl.BlockSpe...  8.48 us
    pallas_call x2, Pallas kernels, split_pieces(): pl.pallas_call(functools.partial(split_pieces_kernel, counts, base), in_s...  6.77 us
    pallas_call x1, Pallas kernels, attention(): pl.pallas_call(functools.partial(attention_kernel, len(key_blocks)), in_s...  6.34 us
  transfers between devices with their start and end apart: 23, of which 10 were waited for; matrix products, arithmetic and copies ran while one was open for 2% of the time, Pallas kernels for 28%

profile of v2, /device:TPU:0, one launch (start us, length us, event | category | flops | bytes accessed | tf_op | source)
XLA Modules:
  0.0 120.1 jit_solution(12114882294409225528)
XLA Ops:
  0.6 3.0 %collective-permute-start.1 = (bf16[128,1024]{1,0:T(8,128)(2,1)}, bf16[128,1024]{1,0:T(8,128)(2,1)S(1)}, u32[]{:S(2)}, u32[]{:S(2)}) collective-permute-start(bf16[128,1024]{1,0:T(8,128)(2,1)} %refs_0_.2), channel_id=1, source_target_pairs={{0,2},{1,3},{2,0},{3,1},{4,6},{5,7},{6,4},{7,5},{8,10},{9,11},{10,... | collective-permute-start | bytes 786440 | tf_op jit(solution)/shard_map/ppermute | solution.py:473
  3.6 0.7 stack.37.where_ref.table_ref.start_ref
  4.3 3.1 %split_pieces.2 = bf16[2,3,128,512]{3,2,1,0:T(8,128)(2,1)} custom-call(s32[11]{0:T(128)} %stack.37.where_ref.table_ref.start_ref, bf16[1024,3,2,512]{3,2,1,0:T(2,128)(2,1)} %bitcast.21), custom_call_target="tpu_custom_call" | custom-call | flops 1000000 | bytes 10000 | tf_op jit(solution)/shard_map/split_pieces/pallas_call | solution.py:95
  7.4 1.6 %collective-permute-start.12 = (bf16[2,3,128,512]{3,2,1,0:T(8,128)(2,1)}, bf16[2,3,128,512]{3,2,1,0:T(8,128)(2,1)S(1)}, u32[]{:S(2)}, u32[]{:S(2)}) collective-permute-start(bf16[2,3,128,512]{3,2,1,0:T(8,128)(2,1)} %split_pieces.2), channel_id=1, source_target_pairs={{0,4},{1,5},{2,6},{3,7},{4,0},{5,1},{6,2},{7,3},{8,12},{9,13},{10,... | collective-permute-start | bytes 2359304 | tf_op jit(solution)/shard_map/ppermute | solution.py:473
  10.2 3.8 %collective-permute-start.6 = (bf16[128,1024]{1,0:T(8,128)(2,1)S(1)}, bf16[128,1024]{1,0:T(8,128)(2,1)S(1)}, u32[]{:S(2)}, u32[]{:S(2)}) collective-permute-start(bf16[128,1024]{1,0:T(8,128)(2,1)S(1)} %copy-done.2), channel_id=1, source_target_pairs={{0,24},{1,25},{2,26},{3,27},{4,28},{5,29},{6,30},{7,31},{8,16},{9,... | collective-permute-start | bytes 786440 | tf_op jit(solution)/shard_map/ppermute | solution.py:473
  14.0 3.7 %split_pieces.3 = bf16[2,3,256,512]{3,2,1,0:T(8,128)(2,1)} custom-call(s32[11]{0:T(128)} %stack.37.where_ref.table_ref.start_ref, bf16[1024,3,2,512]{3,2,1,0:T(2,128)(2,1)} %bitcast.22, bf16[128,1024]{1,0:T(8,128)(2,1)} %copy-done.8), custom_call_target="tpu_custom_call" | custom-call | flops 1000000 | bytes 10000 | tf_op jit(solution)/shard_map/split_pieces/pallas_call | solution.py:95
  17.8 1.6 %collective-permute-start.14 = (bf16[2,3,256,512]{3,2,1,0:T(8,128)(2,1)}, bf16[2,3,256,512]{3,2,1,0:T(8,128)(2,1)S(1)}, u32[]{:S(2)}, u32[]{:S(2)}) collective-permute-start(bf16[2,3,256,512]{3,2,1,0:T(8,128)(2,1)} %split_pieces.3), channel_id=1, source_target_pairs={{0,4},{1,5},{2,6},{3,7},{4,0},{5,1},{6,2},{7,3},{8,12},{9,13},{10,... | collective-permute-start | bytes 4718600 | tf_op jit(solution)/shard_map/ppermute | solution.py:473
  20.7 0.7 copy.21.refs_0_
  22.6 6.3 %attention.1 = (bf16[128,1024]{1,0:T(8,128)(2,1)}, bf16[144,1024]{1,0:T(8,128)(2,1)}) custom-call(f32[1,1024]{1,0:T(1,128)} %bitcast.19, bf16[16,1024]{1,0:T(8,128)(2,1)} %fusion.6.meta_ref, bf16[128,1024]{1,0:T(8,128)(2,1)} %q_hbm.1, bf16[128,1024]{1,0:T(8,128)(2,1)} %stream_hbm.1, bf16[1024,1024]{1,0:T(8,128)(2,1)} %proj_hbm.1, bf16[128,1024]{1,0:T(8,128)(2,1)} %refs_0_.2, ...), custom_call_target="tpu_custom_call" | custom-call | flops 1000000 | bytes 10000 | tf_op jit(solution)/shard_map/attention/pallas_call | solution.py:144
  28.9 4.4 %collective-permute-start.9 = (bf16[144,1024]{1,0:T(8,128)(2,1)}, bf16[144,1024]{1,0:T(8,128)(2,1)S(1)}, u32[]{:S(2)}, u32[]{:S(2)}) collective-permute-start(bf16[144,1024]{1,0:T(8,128)(2,1)} %after.6._.refs_1_.refs_0_), channel_id=1, source_target_pairs={{0,24},{1,25},{2,26},{3,27},{4,28},{5,29},{6,30},{7,31},{8,16},{9,... | collective-permute-start | bytes 884744 | tf_op jit(solution)/shard_map/ppermute | solution.py:473
  33.3 2.4 %collective-permute-start.8 = (bf16[144,1024]{1,0:T(8,128)(2,1)}, bf16[144,1024]{1,0:T(8,128)(2,1)S(1)}, u32[]{:S(2)}, u32[]{:S(2)}) collective-permute-start(bf16[144,1024]{1,0:T(8,128)(2,1)} %after.6._.refs_1_.refs_0_), channel_id=1, source_target_pairs={{0,8},{1,9},{2,10},{3,11},{4,12},{5,13},{6,14},{7,15},{8,0},{9,1},... | collective-permute-start | bytes 884744 | tf_op jit(solution)/shard_map/ppermute | solution.py:473
  35.8 1.5 %collective-permute-start.15 = (bf16[2,3,128,512]{3,2,1,0:T(8,128)(2,1)S(1)}, bf16[2,3,128,512]{3,2,1,0:T(8,128)(2,1)S(1)}, u32[]{:S(2)}, u32[]{:S(2)}) collective-permute-start(bf16[2,3,128,512]{3,2,1,0:T(8,128)(2,1)S(1)} %after.9.refs_5_.refs_7_), channel_id=1, source_target_pairs={{0,2},{1,3},{2,0},{3,1},{4,6},{5,7},{6,4},{7,5},{8,10},{9,11},{10,... | collective-permute-start | bytes 2359304 | tf_op jit(solution)/shard_map/ppermute | solution.py:473
  37.3 8.5 %split_experts.1 = (bf16[2,3,1024,512]{3,2,1,0:T(8,128)(2,1)}, f32[8,128]{1,0:T(8,128)}) custom-call(bf16[1024,3,2,512]{3,2,1,0:T(2,128)(2,1)} %bitcast.23, bf16[144,1024]{1,0:T(8,128)(2,1)} %after.6._.refs_1_.refs_0_), custom_call_target="tpu_custom_call" | custom-call | flops 8000999936 | bytes 10000 | tf_op jit(solution)/shard_map/split_experts/pallas_call | solution.py:54
  45.8 7.2 %collective-permute-done.10.refs_2_.refs_3_ = bf16[128,1024]{1,0:T(8,128)(2,1)} collective-permute-done((bf16[128,1024]{1,0:T(8,128)(2,1)}, bf16[128,1024]{1,0:T(8,128)(2,1)}, u32[]{:S(2)}, u32[]{:S(2)}) %collective-permute-start.10) | collective-permute-done | bytes 262176 | tf_op jit(solution)/shard_map/ppermute | solution.py:473
  53.0 0.7 copy-done.7
  53.7 1.8 %collective-permute-start.11 = (bf16[144,1024]{1,0:T(8,128)(2,1)S(1)}, bf16[144,1024]{1,0:T(8,128)(2,1)S(1)}, u32[]{:S(2)}, u32[]{:S(2)}) collective-permute-start(bf16[144,1024]{1,0:T(8,128)(2,1)S(1)} %after.8.refs_2_), channel_id=1, source_target_pairs={{0,8},{1,9},{2,10},{3,11},{4,12},{5,13},{6,14},{7,15},{8,0},{9,1},... | collective-permute-start | bytes 884744 | tf_op jit(solution)/shard_map/ppermute | solution.py:473
  55.4 7.1 %collective-permute-done.11.refs_3_.refs_2_ = bf16[144,1024]{1,0:T(8,128)(2,1)S(1)} collective-permute-done((bf16[144,1024]{1,0:T(8,128)(2,1)S(1)}, bf16[144,1024]{1,0:T(8,128)(2,1)S(1)}, u32[]{:S(2)}, u32[]{:S(2)}) %collective-permute-start.11) | collective-permute-done | bytes 294944 | tf_op jit(solution)/shard_map/ppermute | solution.py:473
  63.2 1.9 %routing.1 = (bf16[640,512]{1,0:T(8,128)(2,1)S(1)}, bf16[512,640]{1,0:T(8,128)(2,1)S(1)}, f32[512,128]{1,0:T(8,128)S(1)}) custom-call(s32[11]{0:T(128)S(1)} %copy-done.5, bf16[144,1024]{1,0:T(8,128)(2,1)} %after.6._.refs_1_.refs_0_, bf16[144,1024]{1,0:T(8,128)(2,1)S(1)} %collective-permute-done.8.refs_1_.refs_3_, bf16[144,1024]{1,0:T(8,128)(2,1)S(1)} %after.8.refs_2_, ...), custom_call_target="tpu_custom_call" | custom-call | flops 1000000 | bytes 10000 | tf_op jit(solution)/shard_map/routing/pallas_call | solution.py:213
  65.1 2.0 %collective-permute-done.13.refs_6_.refs_8_ = bf16[2,3,128,512]{3,2,1,0:T(8,128)(2,1)S(1)} collective-permute-done((bf16[2,3,128,512]{3,2,1,0:T(8,128)(2,1)S(1)}, bf16[2,3,128,512]{3,2,1,0:T(8,128)(2,1)S(1)}, u32[]{:S(2)}, u32[]{:S(2)}) %collective-permute-start.13) | collective-permute-done | bytes 786464 | tf_op jit(solution)/shard_map/ppermute | solution.py:473
  67.2 1.1 collective-permute-done.17.refs_10_.refs_12_
  68.3 10.3 %expert_out.1 = (bf16[128,1024]{1,0:T(8,128)(2,1)S(1)}, bf16[128,1024]{1,0:T(8,128)(2,1)S(1)}, bf16[256,1024]{1,0:T(8,128)(2,1)S(1)}, bf16[640,512]{1,0:T(8,128)(2,1)S(1)}, bf16[640,512]{1,0:T(8,128)(2,1)S(1)}) custom-call(s32[11]{0:T(128)S(1)} %copy-done.5, bf16[640,512]{1,0:T(8,128)(2,1)S(1)} %get-tuple-element.25.pick_hbm, ...), custom_call_target="tpu_custom_call" | custom-call | flops 1000000 | bytes 10000 | tf_op jit(solution)/shard_map/expert_out/pallas_call | solution.py:387
  78.6 1.2 %collective-permute-start.18 = (bf16[256,1024]{1,0:T(8,128)(2,1)S(1)}, bf16[256,1024]{1,0:T(8,128)(2,1)S(1)}, u32[]{:S(2)}, u32[]{:S(2)}) collective-permute-start(bf16[256,1024]{1,0:T(8,128)(2,1)S(1)} %get-tuple-element.32), channel_id=1, source_target_pairs={{0,8},{1,9},{2,10},{3,11},{4,12},{5,13},{6,14},{7,15},{8,0},{9,1},... | collective-permute-start | bytes 1572872 | tf_op jit(solution)/shard_map/ppermute | solution.py:473
  79.9 9.1 %expert_grad.1 = (bf16[128,1024]{1,0:T(8,128)(2,1)S(1)}, bf16[128,1024]{1,0:T(8,128)(2,1)S(1)}, bf16[128,1024]{1,0:T(8,128)(2,1)S(1)}, bf16[128,1024]{1,0:T(8,128)(2,1)S(1)}) custom-call(s32[11]{0:T(128)S(1)} %copy-done.5, bf16[640,512]{1,0:T(8,128)(2,1)S(1)} %get-tuple-element.25.pick_hbm, bf16[512,640]{1,0:T(8,128)(2,1)S(1)} %get-tuple-element.26.put_hbm, ...), custom_call_target="tpu_custom_call" | custom-call | flops 1000000 | bytes 10000 | tf_op jit(solution)/shard_map/expert_grad/pallas_call | solution.py:387
  88.9 3.7 %collective-permute-done.18.beside_ref = bf16[256,1024]{1,0:T(8,128)(2,1)S(1)} collective-permute-done((bf16[256,1024]{1,0:T(8,128)(2,1)S(1)}, bf16[256,1024]{1,0:T(8,128)(2,1)S(1)}, u32[]{:S(2)}, u32[]{:S(2)}) %collective-permute-start.18) | collective-permute-done | bytes 524320 | tf_op jit(solution)/shard_map/ppermute | solution.py:473
  92.7 1.2 %collective-permute-start.21 = (bf16[128,1024]{1,0:T(8,128)(2,1)S(1)}, bf16[128,1024]{1,0:T(8,128)(2,1)S(1)}, u32[]{:S(2)}, u32[]{:S(2)}) collective-permute-start(bf16[128,1024]{1,0:T(8,128)(2,1)S(1)} %get-tuple-element.41), channel_id=1, source_target_pairs={{0,8},{1,9},{2,10},{3,11},{4,12},{5,13},{6,14},{7,15},{8,0},{9,1},... | collective-permute-start | bytes 786440 | tf_op jit(solution)/shard_map/ppermute | solution.py:473
  94.0 2.6 %collective-permute-start.19 = (bf16[128,1024]{1,0:T(8,128)(2,1)S(1)}, bf16[128,1024]{1,0:T(8,128)(2,1)S(1)}, u32[]{:S(2)}, u32[]{:S(2)}) collective-permute-start(bf16[128,1024]{1,0:T(8,128)(2,1)S(1)} %add_convert_fusion.1.refs_2_), channel_id=1, source_target_pairs={{0,24},{1,25},{2,26},{3,27},{4,28},{5,29},{6,30},{7,31},{8,16},{9,... | collective-permute-start | bytes 786440 | tf_op jit(solution)/shard_map/ppermute | solution.py:473
  96.6 0.8 collective-permute-start.20
  97.4 6.3 %collective-permute-done.21 = bf16[128,1024]{1,0:T(8,128)(2,1)S(1)} collective-permute-done((bf16[128,1024]{1,0:T(8,128)(2,1)S(1)}, bf16[128,1024]{1,0:T(8,128)(2,1)S(1)}, u32[]{:S(2)}, u32[]{:S(2)}) %collective-permute-start.21) | collective-permute-done | bytes 262176 | tf_op jit(solution)/shard_map/ppermute | solution.py:473
  103.8 7.5 %collective-permute-start.22 = (bf16[128,1024]{1,0:T(8,128)(2,1)S(1)}, bf16[128,1024]{1,0:T(8,128)(2,1)S(1)}, u32[]{:S(2)}, u32[]{:S(2)}) collective-permute-start(bf16[128,1024]{1,0:T(8,128)(2,1)S(1)} %add_convert_fusion), channel_id=1, source_target_pairs={{0,24},{1,25},{2,26},{3,27},{4,28},{5,29},{6,30},{7,31},{8,16},{9,... | collective-permute-start | bytes 786440 | tf_op jit(solution)/shard_map/ppermute | solution.py:473
  111.3 0.8 out_sum.1
  112.1 6.9 %collective-permute-done.22.merged_ref = bf16[128,1024]{1,0:T(8,128)(2,1)S(1)} collective-permute-done((bf16[128,1024]{1,0:T(8,128)(2,1)S(1)}, bf16[128,1024]{1,0:T(8,128)(2,1)S(1)}, u32[]{:S(2)}, u32[]{:S(2)}) %collective-permute-start.22) | collective-permute-done | bytes 262176 | tf_op jit(solution)/shard_map/ppermute | solution.py:473
  119.0 1.0 grad_sum.1
  (66 shorter events, 4.5 us)
Async XLA Ops:
  0.6 9.5 %collective-permute-start.1 = (bf16[128,1024]{1,0:T(8,128)(2,1)}, bf16[128,1024]{1,0:T(8,128)(2,1)S(1)}, u32[]{:S(2)}, u32[]{:S(2)}) collective-permute-start(bf16[128,1024]{1,0:T(8,128)(2,1)} %refs_0_.2), channel_id=1, source_target_pairs={{0,2},{1,3},{2,0},{3,1},{4,6},{5,7},{6,4},{7,5},{8,10},{9,11},{10,... | collective-permute-start | bytes 786440 | tf_op jit(solution)/shard_map/ppermute | solution.py:473
  3.6 14.1 %collective-permute-start = (bf16[128,1024]{1,0:T(8,128)(2,1)}, bf16[128,1024]{1,0:T(8,128)(2,1)S(1)}, u32[]{:S(2)}, u32[]{:S(2)}) collective-permute-start(bf16[128,1024]{1,0:T(8,128)(2,1)} %refs_0_.2), channel_id=1, source_target_pairs={{0,1},{1,0},{2,3},{3,2},{4,5},{5,4},{6,7},{7,6},{8,9},{9,8},{10,11... | collective-permute-start | bytes 786440 | tf_op jit(solution)/shard_map/ppermute | solution.py:473
  4.3 5.8 %copy-start.2 = (bf16[128,1024]{1,0:T(8,128)(2,1)S(1)}, bf16[128,1024]{1,0:T(8,128)(2,1)}, u32[]{:S(2)}) copy-start(bf16[128,1024]{1,0:T(8,128)(2,1)} %cot_ref.1) | copy-start | bytes 786436
  7.4 12.0 %copy-start.14 = (f32[128,4]{0,1:T(4,128)S(1)}, f32[128,4]{0,1:T(4,128)}, u32[]{:S(2)}) copy-start(f32[128,4]{0,1:T(4,128)} %param.18) | copy-start | bytes 6148
  7.4 12.7 %copy-start.13 = (s32[128,4]{0,1:T(4,128)S(1)}, s32[128,4]{0,1:T(4,128)}, u32[]{:S(2)}) copy-start(s32[128,4]{0,1:T(4,128)} %param.17) | copy-start | bytes 6148
  7.4 28.3 %collective-permute-start.12 = (bf16[2,3,128,512]{3,2,1,0:T(8,128)(2,1)}, bf16[2,3,128,512]{3,2,1,0:T(8,128)(2,1)S(1)}, u32[]{:S(2)}, u32[]{:S(2)}) collective-permute-start(bf16[2,3,128,512]{3,2,1,0:T(8,128)(2,1)} %split_pieces.2), channel_id=1, source_target_pairs={{0,4},{1,5},{2,6},{3,7},{4,0},{5,1},{6,2},{7,3},{8,12},{9,13},{10,... | collective-permute-start | bytes 2359304 | tf_op jit(solution)/shard_map/ppermute | solution.py:473
  9.0 10.4 %collective-permute-start.3 = (bf16[128,1024]{1,0:T(8,128)(2,1)S(1)}, bf16[128,1024]{1,0:T(8,128)(2,1)}, u32[]{:S(2)}, u32[]{:S(2)}) collective-permute-start(bf16[128,1024]{1,0:T(8,128)(2,1)S(1)} %copy-done.9), channel_id=1, source_target_pairs={{0,1},{1,0},{2,3},{3,2},{4,5},{5,4},{6,7},{7,6},{8,9},{9,8},{10,11... | collective-permute-start | bytes 786440 | tf_op jit(solution)/shard_map/ppermute | solution.py:473
  9.2 10.2 %collective-permute-start.4 = (bf16[128,1024]{1,0:T(8,128)(2,1)S(1)}, bf16[128,1024]{1,0:T(8,128)(2,1)}, u32[]{:S(2)}, u32[]{:S(2)}) collective-permute-start(bf16[128,1024]{1,0:T(8,128)(2,1)S(1)} %copy-done.9), channel_id=1, source_target_pairs={{0,2},{1,3},{2,0},{3,1},{4,6},{5,7},{6,4},{7,5},{8,10},{9,11},{10,... | collective-permute-start | bytes 786440 | tf_op jit(solution)/shard_map/ppermute | solution.py:473
  10.2 10.0 %collective-permute-start.6 = (bf16[128,1024]{1,0:T(8,128)(2,1)S(1)}, bf16[128,1024]{1,0:T(8,128)(2,1)S(1)}, u32[]{:S(2)}, u32[]{:S(2)}) collective-permute-start(bf16[128,1024]{1,0:T(8,128)(2,1)S(1)} %copy-done.2), channel_id=1, source_target_pairs={{0,24},{1,25},{2,26},{3,27},{4,28},{5,29},{6,30},{7,31},{8,16},{9,... | collective-permute-start | bytes 786440 | tf_op jit(solution)/shard_map/ppermute | solution.py:473
  17.8 44.8 %collective-permute-start.14 = (bf16[2,3,256,512]{3,2,1,0:T(8,128)(2,1)}, bf16[2,3,256,512]{3,2,1,0:T(8,128)(2,1)S(1)}, u32[]{:S(2)}, u32[]{:S(2)}) collective-permute-start(bf16[2,3,256,512]{3,2,1,0:T(8,128)(2,1)} %split_pieces.3), channel_id=1, source_target_pairs={{0,4},{1,5},{2,6},{3,7},{4,0},{5,1},{6,2},{7,3},{8,12},{9,13},{10,... | collective-permute-start | bytes 4718600 | tf_op jit(solution)/shard_map/ppermute | solution.py:473
  19.4 9.6 %collective-permute-start.7 = (bf16[128,1024]{1,0:T(8,128)(2,1)S(1)}, bf16[128,1024]{1,0:T(8,128)(2,1)S(1)}, u32[]{:S(2)}, u32[]{:S(2)}) collective-permute-start(bf16[128,1024]{1,0:T(8,128)(2,1)S(1)} %copy-done.2), channel_id=1, source_target_pairs={{0,8},{1,9},{2,10},{3,11},{4,12},{5,13},{6,14},{7,15},{8,0},{9,1},... | collective-permute-start | bytes 786440 | tf_op jit(solution)/shard_map/ppermute | solution.py:473
  19.5 2.0 %collective-permute-start.2 = (bf16[128,1024]{1,0:T(8,128)(2,1)}, bf16[128,1024]{1,0:T(8,128)(2,1)S(1)}, u32[]{:S(2)}, u32[]{:S(2)}) collective-permute-start(bf16[128,1024]{1,0:T(8,128)(2,1)} %copy-done.8), channel_id=1, source_target_pairs={{0,1},{1,0},{2,3},{3,2},{4,5},{5,4},{6,7},{7,6},{8,9},{9,8},{10,11... | collective-permute-start | bytes 786440 | tf_op jit(solution)/shard_map/ppermute | solution.py:473
  20.1 1.7 %collective-permute-start.5 = (bf16[128,1024]{1,0:T(8,128)(2,1)}, bf16[128,1024]{1,0:T(8,128)(2,1)S(1)}, u32[]{:S(2)}, u32[]{:S(2)}) collective-permute-start(bf16[128,1024]{1,0:T(8,128)(2,1)} %collective-permute-done.4.refs_6_), channel_id=1, source_target_pairs={{0,1},{1,0},{2,3},{3,2},{4,5},{5,4},{6,7},{7,6},{8,9},{9,8},{10,11... | collective-permute-start | bytes 786440 | tf_op jit(solution)/shard_map/ppermute | solution.py:473
  28.9 6.8 %copy-start = (bf16[128,1024]{1,0:T(8,128)(2,1)}, bf16[128,1024]{1,0:T(8,128)(2,1)S(1)}, u32[]{:S(2)}) copy-start(bf16[128,1024]{1,0:T(8,128)(2,1)S(1)} %collective-permute-done.7.refs_2_.refs_1_) | copy-start | bytes 786436
  28.9 24.0 %collective-permute-start.9 = (bf16[144,1024]{1,0:T(8,128)(2,1)}, bf16[144,1024]{1,0:T(8,128)(2,1)S(1)}, u32[]{:S(2)}, u32[]{:S(2)}) collective-permute-start(bf16[144,1024]{1,0:T(8,128)(2,1)} %after.6._.refs_1_.refs_0_), channel_id=1, source_target_pairs={{0,24},{1,25},{2,26},{3,27},{4,28},{5,29},{6,30},{7,31},{8,16},{9,... | collective-permute-start | bytes 884744 | tf_op jit(solution)/shard_map/ppermute | solution.py:473
  33.3 22.1 %collective-permute-start.8 = (bf16[144,1024]{1,0:T(8,128)(2,1)}, bf16[144,1024]{1,0:T(8,128)(2,1)S(1)}, u32[]{:S(2)}, u32[]{:S(2)}) collective-permute-start(bf16[144,1024]{1,0:T(8,128)(2,1)} %after.6._.refs_1_.refs_0_), channel_id=1, source_target_pairs={{0,8},{1,9},{2,10},{3,11},{4,12},{5,13},{6,14},{7,15},{8,0},{9,1},... | collective-permute-start | bytes 884744 | tf_op jit(solution)/shard_map/ppermute | solution.py:473
  35.7 17.2 %collective-permute-start.10 = (bf16[128,1024]{1,0:T(8,128)(2,1)}, bf16[128,1024]{1,0:T(8,128)(2,1)}, u32[]{:S(2)}, u32[]{:S(2)}) collective-permute-start(bf16[128,1024]{1,0:T(8,128)(2,1)} %after.7), channel_id=1, source_target_pairs={{0,8},{1,9},{2,10},{3,11},{4,12},{5,13},{6,14},{7,15},{8,0},{9,1},... | collective-permute-start | bytes 786440 | tf_op jit(solution)/shard_map/ppermute | solution.py:473
  35.8 26.8 %collective-permute-start.15 = (bf16[2,3,128,512]{3,2,1,0:T(8,128)(2,1)S(1)}, bf16[2,3,128,512]{3,2,1,0:T(8,128)(2,1)S(1)}, u32[]{:S(2)}, u32[]{:S(2)}) collective-permute-start(bf16[2,3,128,512]{3,2,1,0:T(8,128)(2,1)S(1)} %after.9.refs_5_.refs_7_), channel_id=1, source_target_pairs={{0,2},{1,3},{2,0},{3,1},{4,6},{5,7},{6,4},{7,5},{8,10},{9,11},{10,... | collective-permute-start | bytes 2359304 | tf_op jit(solution)/shard_map/ppermute | solution.py:473
  53.7 9.6 %copy-start.5 = (s32[11]{0:T(128)S(1)}, s32[11]{0:T(128)}, u32[]{:S(2)}) copy-start(s32[11]{0:T(128)} %stack.37.where_ref.table_ref.start_ref) | copy-start | bytes 136
  53.7 8.9 %collective-permute-start.11 = (bf16[144,1024]{1,0:T(8,128)(2,1)S(1)}, bf16[144,1024]{1,0:T(8,128)(2,1)S(1)}, u32[]{:S(2)}, u32[]{:S(2)}) collective-permute-start(bf16[144,1024]{1,0:T(8,128)(2,1)S(1)} %after.8.refs_2_), channel_id=1, source_target_pairs={{0,8},{1,9},{2,10},{3,11},{4,12},{5,13},{6,14},{7,15},{8,0},{9,1},... | collective-permute-start | bytes 884744 | tf_op jit(solution)/shard_map/ppermute | solution.py:473
  62.6 5.7 %collective-permute-start.16 = (bf16[2,3,256,512]{3,2,1,0:T(8,128)(2,1)S(1)}, bf16[2,3,256,512]{3,2,1,0:T(8,128)(2,1)S(1)}, u32[]{:S(2)}, u32[]{:S(2)}) collective-permute-start(bf16[2,3,256,512]{3,2,1,0:T(8,128)(2,1)S(1)} %get-tuple-element.29.refs_7_.refs_9_), channel_id=1, source_target_pairs={{0,1},{1,0},{2,3},{3,2},{4,5},{5,4},{6,7},{7,6},{8,9},{9,8},{10,11... | collective-permute-start | bytes 4718600 | tf_op jit(solution)/shard_map/ppermute | solution.py:473
  62.6 4.5 %collective-permute-start.13 = (bf16[2,3,128,512]{3,2,1,0:T(8,128)(2,1)S(1)}, bf16[2,3,128,512]{3,2,1,0:T(8,128)(2,1)S(1)}, u32[]{:S(2)}, u32[]{:S(2)}) collective-permute-start(bf16[2,3,128,512]{3,2,1,0:T(8,128)(2,1)S(1)} %after.9.refs_5_.refs_7_), channel_id=1, source_target_pairs={{0,1},{1,0},{2,3},{3,2},{4,5},{5,4},{6,7},{7,6},{8,9},{9,8},{10,11... | collective-permute-start | bytes 2359304 | tf_op jit(solution)/shard_map/ppermute | solution.py:473
  63.1 5.1 %collective-permute-start.17 = (bf16[2,3,128,512]{3,2,1,0:T(8,128)(2,1)S(1)}, bf16[2,3,128,512]{3,2,1,0:T(8,128)(2,1)S(1)}, u32[]{:S(2)}, u32[]{:S(2)}) collective-permute-start(bf16[2,3,128,512]{3,2,1,0:T(8,128)(2,1)S(1)} %get-tuple-element.30.refs_9_.refs_11_), channel_id=1, source_target_pairs={{0,1},{1,0},{2,3},{3,2},{4,5},{5,4},{6,7},{7,6},{8,9},{9,8},{10,11... | collective-permute-start | bytes 2359304 | tf_op jit(solution)/shard_map/ppermute | solution.py:473
  68.3 11.6 %copy-start.1 = (bf16[128,1024]{1,0:T(8,128)(2,1)S(1)}, bf16[128,1024]{1,0:T(8,128)(2,1)}, u32[]{:S(2)}) copy-start(bf16[128,1024]{1,0:T(8,128)(2,1)} %copy-done) | copy-start | bytes 786436
  68.3 11.6 %copy-start.3 = (bf16[128,1024]{1,0:T(8,128)(2,1)S(1)}, bf16[128,1024]{1,0:T(8,128)(2,1)}, u32[]{:S(2)}) copy-start(bf16[128,1024]{1,0:T(8,128)(2,1)} %cot_ref.1) | copy-start | bytes 786436
  78.6 14.0 %collective-permute-start.18 = (bf16[256,1024]{1,0:T(8,128)(2,1)S(1)}, bf16[256,1024]{1,0:T(8,128)(2,1)S(1)}, u32[]{:S(2)}, u32[]{:S(2)}) collective-permute-start(bf16[256,1024]{1,0:T(8,128)(2,1)S(1)} %get-tuple-element.32), channel_id=1, source_target_pairs={{0,8},{1,9},{2,10},{3,11},{4,12},{5,13},{6,14},{7,15},{8,0},{9,1},... | collective-permute-start | bytes 1572872 | tf_op jit(solution)/shard_map/ppermute | solution.py:473
  88.9 22.3 %copy-start.4 = (bf16[128,1024]{1,0:T(8,128)(2,1)S(1)}, bf16[128,1024]{1,0:T(8,128)(2,1)}, u32[]{:S(2)}) copy-start(bf16[128,1024]{1,0:T(8,128)(2,1)} %get-tuple-element.22.mix_ref) | copy-start | bytes 786436
  92.7 11.0 %collective-permute-start.21 = (bf16[128,1024]{1,0:T(8,128)(2,1)S(1)}, bf16[128,1024]{1,0:T(8,128)(2,1)S(1)}, u32[]{:S(2)}, u32[]{:S(2)}) collective-permute-start(bf16[128,1024]{1,0:T(8,128)(2,1)S(1)} %get-tuple-element.41), channel_id=1, source_target_pairs={{0,8},{1,9},{2,10},{3,11},{4,12},{5,13},{6,14},{7,15},{8,0},{9,1},... | collective-permute-start | bytes 786440 | tf_op jit(solution)/shard_map/ppermute | solution.py:473
  94.0 17.3 %collective-permute-start.19 = (bf16[128,1024]{1,0:T(8,128)(2,1)S(1)}, bf16[128,1024]{1,0:T(8,128)(2,1)S(1)}, u32[]{:S(2)}, u32[]{:S(2)}) collective-permute-start(bf16[128,1024]{1,0:T(8,128)(2,1)S(1)} %add_convert_fusion.1.refs_2_), channel_id=1, source_target_pairs={{0,24},{1,25},{2,26},{3,27},{4,28},{5,29},{6,30},{7,31},{8,16},{9,... | collective-permute-start | bytes 786440 | tf_op jit(solution)/shard_map/ppermute | solution.py:473
  96.6 15.6 %collective-permute-start.20 = (bf16[128,1024]{1,0:T(8,128)(2,1)S(1)}, bf16[128,1024]{1,0:T(8,128)(2,1)S(1)}, u32[]{:S(2)}, u32[]{:S(2)}) collective-permute-start(bf16[128,1024]{1,0:T(8,128)(2,1)S(1)} %get-tuple-element.39), channel_id=1, source_target_pairs={{0,8},{1,9},{2,10},{3,11},{4,12},{5,13},{6,14},{7,15},{8,0},{9,1},... | collective-permute-start | bytes 786440 | tf_op jit(solution)/shard_map/ppermute | solution.py:473
  103.8 15.2 %collective-permute-start.22 = (bf16[128,1024]{1,0:T(8,128)(2,1)S(1)}, bf16[128,1024]{1,0:T(8,128)(2,1)S(1)}, u32[]{:S(2)}, u32[]{:S(2)}) collective-permute-start(bf16[128,1024]{1,0:T(8,128)(2,1)S(1)} %add_convert_fusion), channel_id=1, source_target_pairs={{0,24},{1,25},{2,26},{3,27},{4,28},{5,29},{6,30},{7,31},{8,16},{9,... | collective-permute-start | bytes 786440 | tf_op jit(solution)/shard_map/ppermute | solution.py:473
  111.3 7.8 %copy-start.6 = (f32[1024]{0:T(1024)S(1)}, f32[1024]{0:T(1024)}, u32[]{:S(2)}) copy-start(f32[1024]{0:T(1024)} %param.15) | copy-start | bytes 12292
  (6 other events, 14.8 us)

commit v3 on v2

--- a/solution.py
+++ b/solution.py
@@ -13,7 +13,6 @@
 CHUNK = 32
 NORM_EPS = 1e-06
 MIB = 1 << 20
-OPT = dict(cut=4, kv="first", vm=40, att=60, order=True)
 F32, BF16 = jnp.float32, jnp.bfloat16
 
 
@@ -29,7 +28,7 @@
     return [pl.BlockSpec(memory_space=pltpu.VMEM)] * count
 
 
-COSTS = dict(after=0, split_pieces=0, split_experts=8, attention=0, routing=0, expert_out=0, expert_grad=0, out_sum=20, grad_sum=0)
+COSTS = {'after': 0, 'split_pieces': 3, 'split_experts': 8, 'attention': 0, 'routing': 0, 'own_out': 0, 'own_grad': 5, 'other_out': 0, 'other_grad': 6, 'out_sum': 20, 'grad_sum': 0}
 
 
 def cost(name):
@@ -148,7 +147,7 @@
         out_shape=outs,
         scratch_shapes=[pltpu.VMEM(shape, BF16) for shape in scratch]
         + [pltpu.SemaphoreType.DMA((len(loads),))],
-        compiler_params=params(OPT["att"]),
+        compiler_params=params(60),
         cost_estimate=cost("attention"),
         name="attention",
     )(norm_gain[None, :], meta, *loads)
@@ -236,12 +235,12 @@
     depth = sum(piece.shape[2] for piece in weight_sets[0])
     most = max(len(each) for each in weight_sets)
     return [
-        pltpu.VMEM((2, local, parts, depth, hidden), BF16),
+        pltpu.VMEM((min(2, len(weight_sets)), local, parts, depth, hidden), BF16),
         pltpu.SemaphoreType.DMA((2, local, most)),
     ]
 
 
-def each_expert(start_ref, w_refs, set_sizes, buffer, sems, prepare, body):
+def each_expert(start_ref, base, w_refs, set_sizes, buffer, sems, prepare, body):
     local = buffer.shape[1]
 
     def copies(index, expert):
@@ -249,7 +248,7 @@
         made = []
         for place in range(set_sizes[index]):
             ref = w_refs[before + place]
-            at = pl.multiple_of(start_ref[4 + before + place] * CHUNK, CHUNK)
+            at = pl.multiple_of(start_ref[4 + base + before + place] * CHUNK, CHUNK)
             target = buffer.at[slot, expert, :, pl.ds(at, ref.shape[2]), :]
             made.append(
                 pltpu.make_async_copy(ref.at[expert], target, sems.at[slot, expert, place])
@@ -296,37 +295,36 @@
     ]
 
 
-def spread_rows(put, gates, made, own_ref, across_ref, *pair_refs):
+def spread_rows(put, gates, made, own_ref, across_ref, far_ref, beside_ref):
     total = dot(put[...], made[...])
     rows = own_ref.shape[0]
-
-    def block(place):
+    more = beside_ref.shape[0] - rows
+    for place, ref in enumerate((own_ref, beside_ref, across_ref, far_ref)):
         part = slice(place * rows, (place + 1) * rows)
-        return (gates[part, :1] * total[part]).astype(BF16)
-
-    own_ref[...] = block(0)
-    across_ref[...] = block(2)
-    if len(pair_refs) == 1:
-        pair_refs[0][:rows] = block(3)
-        pair_refs[0][rows:] = block(1)
-    else:
-        pair_refs[0][...] = block(3)
-        pair_refs[1][...] = block(1)
-
-
-def out_kernel(set_sizes, slots, start_ref, pick_hbm, put_hbm, gate_hbm, *refs):
-    x_refs, w_refs, out_refs, kept_refs, rest = take_refs(refs, (4, sum(set_sizes), 3, 2, 10))
+        block = (gates[part, :1] * total[part]).astype(BF16)
+        if place == 1:
+            ref[more:] = block
+        else:
+            ref[...] = block
+
+
+def out_kernel(plan, start_ref, pick_hbm, put_hbm, gate_hbm, *refs):
+    base, lead, slots, set_sizes, ignored = plan
+    x_refs, w_refs, prior, _, out_refs, kept_refs, rest = take_refs(
+        refs, (4, sum(set_sizes), bool(lead), ignored, 4 if lead else 1, 2, 10)
+    )
     pick, put, gates, every, act, slope, rows, load_sems, buffer, sems = rest
+    count = pick.shape[0]
     kept = []
 
     def prepare():
         wait(first)
-        rows[...] = dot(pick[...], every[...]).astype(BF16)
+        rows[pl.ds(lead, count)] = dot(pick[...], every[...]).astype(BF16)
 
     def body(place, weights):
-        part = pl.ds(place * slots, slots)
-        gate = dot(rows[part], weights[0])
-        up = dot(rows[part], weights[1])
+        part, mine = pl.ds(place * slots, slots), pl.ds(lead + place * slots, slots)
+        gate = dot(rows[mine], weights[0])
+        up = dot(rows[mine], weights[1])
         sigmoid = 1.0 / (1.0 + jnp.exp(-gate))
         active = gate * sigmoid
         act[part] = active.astype(BF16)
@@ -334,90 +332,111 @@
         kept.extend(
             load(
                 [(act.at[part], kept_refs[0].at[part]), (slope.at[part], kept_refs[1].at[part])],
-                load_sems.at[pl.ds(7 + 2 * place, 2)],
+                load_sems.at[pl.ds(8 + 2 * place, 2)],
             )
         )
         hidden = (active * up).astype(BF16)
-        rows[part] = dot(hidden, weights[2], ((1,), (1,))).astype(BF16)
-
-    first = load([(pick_hbm, pick)] + blocks_of(x_refs, every), load_sems)
-    later = load([(put_hbm, put), (gate_hbm, gates)], load_sems.at[pl.ds(5, 2)])
-    each_expert(start_ref, w_refs, set_sizes, buffer, sems, prepare, body)
-    wait(later)
-    spread_rows(put, gates, rows, *out_refs)
+        rows[mine] = dot(hidden, weights[2], ((1,), (1,))).astype(BF16)
+
+    first = load([(pick_hbm.at[pl.ds(lead, count)], pick)] + blocks_of(x_refs, every), load_sems)
+    if lead:
+        pairs = [(put_hbm, put), (gate_hbm, gates), (prior[0], rows.at[pl.ds(0, lead)])]
+        later = load(pairs, load_sems.at[pl.ds(5, 3)])
+    each_expert(start_ref, base, w_refs, set_sizes, buffer, sems, prepare, body)
+    if lead:
+        wait(later)
+        spread_rows(put, gates, rows, *out_refs)
+    else:
+        out_refs[0][...] = rows[...]
     wait(kept)
 
 
-def grad_kernel(set_sizes, slots, start_ref, pick_hbm, put_hbm, gate_hbm, *refs):
-    c_refs, kept_refs, w_refs, out_refs, rest = take_refs(refs, (4, 2, sum(set_sizes), 4, 10))
+def grad_kernel(plan, start_ref, pick_hbm, put_hbm, gate_hbm, *refs):
+    base, lead, slots, set_sizes, ignored = plan
+    c_refs, w_refs, prior, _, kept_refs, out_refs, rest = take_refs(
+        refs, (4, sum(set_sizes), 2 * bool(lead), ignored, 2, 4 if lead else 1, 10)
+    )
     pick, put, gates, every, act, slope, rows, load_sems, buffer, sems = rest
+    count = pick.shape[0]
 
     def prepare():
         wait(first)
-        rows[...] = dot(pick[...], every[...]).astype(BF16)
+        rows[pl.ds(lead, count)] = dot(pick[...], every[...]).astype(BF16)
         wait(kept)
 
     def body(place, weights):
-        part = pl.ds(place * slots, slots)
-        back_hidden = dot(rows[part], weights[2])
+        part, mine = pl.ds(place * slots, slots), pl.ds(lead + place * slots, slots)
+        back_hidden = dot(rows[mine], weights[2])
         gate = (back_hidden * slope[part].astype(F32)).astype(BF16)
         up = (back_hidden * act[part].astype(F32)).astype(BF16)
         result = dot(gate, weights[0], ((1,), (1,))) + dot(up, weights[1], ((1,), (1,)))
-        rows[part] = result.astype(BF16)
-
-    first = load([(pick_hbm, pick)] + blocks_of(c_refs, every), load_sems)
-    kept = load([(kept_refs[0], act), (kept_refs[1], slope)], load_sems.at[pl.ds(7, 2)])
-    later = load([(put_hbm, put), (gate_hbm, gates)], load_sems.at[pl.ds(5, 2)])
-    each_expert(start_ref, w_refs, set_sizes, buffer, sems, prepare, body)
-    wait(later)
-    spread_rows(put, gates, rows, *out_refs)
+        rows[mine] = result.astype(BF16)
+
+    first = load([(pick_hbm.at[pl.ds(lead, count)], pick)] + blocks_of(c_refs, every), load_sems)
+    kept = load([(kept_refs[0], act), (kept_refs[1], slope)], load_sems.at[pl.ds(8, 2)])
+    if lead:
+        pairs = [(put_hbm, put), (gate_hbm, gates), (prior[0], rows.at[pl.ds(0, lead)])]
+        pairs.append((prior[1], out_refs[3].at[pl.ds(0, prior[1].shape[0])]))
+        later = load(pairs[:3], load_sems.at[pl.ds(5, 3)])
+        later += load(pairs[3:], load_sems.at[pl.ds(10, 1)])
+    each_expert(start_ref, base, w_refs, set_sizes, buffer, sems, prepare, body)
+    if lead:
+        wait(later)
+        spread_rows(put, gates, rows, *out_refs)
+    else:
+        out_refs[0][...] = rows[...]
 
 
 def whole(array):
     return pl.BlockSpec(array.shape, lambda i: (0,) * array.ndim)
 
 
-def expert_call(kernel, name, ways, blocks, kept, weight_sets, table, slots, keep):
-    pieces = [piece for each in weight_sets for piece in each]
-    rows, width = ways[1].shape[0] // len(blocks), blocks[0].shape[1]
-    shapes = [jax.ShapeDtypeStruct((n * rows, width), BF16) for n in ((1, 1, 2) if keep else (1, 1, 1, 1))]
-    count, hidden = ways[0].shape[0], pieces[0].shape[3]
+def expert_call(kernel, name, ways, blocks, sets, base, table, slots, prior=(), earlier=(), kept=()):
+    pieces = [piece for each in sets for piece in each]
+    width, hidden = blocks[0].shape[1], pieces[0].shape[3]
+    rows = ways[1].shape[0] // len(blocks)
+    count = len(sets) * pieces[0].shape[0] * slots
+    lead = prior[0].shape[0] if prior else 0
+    tall = [rows, rows, rows, rows * len(prior)] if prior else [count]
+    shapes = [jax.ShapeDtypeStruct((n, width), BF16) for n in tall]
     keeps = [jax.ShapeDtypeStruct((count, hidden), BF16)] * 2
-    anywhere, far_off = pl.BlockSpec(memory_space=pl.ANY), pl.BlockSpec(memory_space=pltpu.HBM)
+    keep = [] if kept else keeps
+    anywhere = pl.BlockSpec(memory_space=pl.ANY)
+    plan = (base, lead, slots, tuple(len(each) for each in sets), len(earlier))
+    operands = [*ways, *blocks, *pieces, *prior, *earlier, *kept]
     return pl.pallas_call(
-        functools.partial(kernel, tuple(len(each) for each in weight_sets), slots),
+        functools.partial(kernel, plan),
         grid=(1,),
-        in_specs=[pl.BlockSpec(memory_space=pltpu.SMEM)]
-        + [anywhere] * len(ways)
-        + [far_off] * len(blocks)
-        + [anywhere] * (len(kept) + len(weight_sets[0]))
-        + [far_off] * (len(pieces) - len(weight_sets[0])),
-        out_specs=[whole(v) for v in shapes] + [anywhere] * (2 * keep),
-        out_shape=shapes + keeps * keep,
-        scratch_shapes=[pltpu.VMEM(v.shape, v.dtype) for v in ways]
+        in_specs=[pl.BlockSpec(memory_space=pltpu.SMEM)] + [anywhere] * len(operands),
+        out_specs=[whole(v) for v in shapes] + [anywhere] * len(keep),
+        out_shape=shapes + keep,
+        scratch_shapes=[pltpu.VMEM((count, ways[0].shape[1]), BF16)]
+        + [pltpu.VMEM(v.shape, v.dtype) for v in ways[1:]]
         + [pltpu.VMEM((len(blocks) * rows, width), BF16)]
         + [pltpu.VMEM(v.shape, v.dtype) for v in keeps]
         + [
-            pltpu.VMEM((count, width), BF16),
-            pltpu.SemaphoreType.DMA((7 + 2 * (count // slots),)),
+            pltpu.VMEM((lead + count, width), BF16),
+            pltpu.SemaphoreType.DMA((11 + 2 * (count // slots),)),
         ]
-        + weight_scratch(weight_sets),
-        compiler_params=params(OPT["vm"]),
+        + weight_scratch(sets),
+        compiler_params=params(45 if name == "own_out" else 40),
         cost_estimate=cost(name),
         name=name,
-    )(table, *ways, *blocks, *kept, *pieces)
+    )(table, *operands)
 
 
 def out_sum_kernel(mix_ref, own_ref, beside_ref, merged_ref, out_ref):
     rows = mix_ref.shape[0]
-    total = own_ref[...].astype(F32) + beside_ref[rows:].astype(F32) + merged_ref[...].astype(F32)
+    total = own_ref[...].astype(F32) + beside_ref[:rows].astype(F32) + merged_ref[...].astype(F32)
     out_ref[...] = (mix_ref[...].astype(F32) + total).astype(BF16)
 
 
-def grad_sum_kernel(mix_ref, cot_ref, gain_ref, own_ref, beside_ref, merged_ref, grad_ref):
+def grad_sum_kernel(mix_ref, cot_ref, gain_ref, own_ref, beside_ref, merged_ref, *refs):
+    grad_ref = refs[-1]
     wide = mix_ref[...].astype(F32)
     inverse = lax.rsqrt(jnp.mean(wide * wide, axis=1, keepdims=True) + NORM_EPS)
-    total = own_ref[...].astype(F32) + beside_ref[...].astype(F32) + merged_ref[...].astype(F32)
+    rows = mix_ref.shape[0]
+    total = own_ref[...].astype(F32) + beside_ref[rows:].astype(F32) + merged_ref[...].astype(F32)
     weighted = gain_ref[...] * total
     scaled = wide * inverse
     grad_ref[...] = (
@@ -426,16 +445,16 @@
     ).astype(BF16)
 
 
-def finish(kernel, name, *arrays):
+def finish(kernel, name, *arrays, earlier=()):
     return pl.pallas_call(
         kernel,
-        in_specs=vmem_specs(len(arrays)),
+        in_specs=vmem_specs(len(arrays)) + [pl.BlockSpec(memory_space=pl.ANY)] * len(earlier),
         out_specs=vmem_specs(1)[0],
         out_shape=jax.ShapeDtypeStruct(arrays[0].shape, BF16),
         compiler_params=params(),
         cost_estimate=cost(name),
         name=name,
-    )(*arrays)
+    )(*arrays, *earlier)
 
 
 def nothing(*refs):
@@ -488,11 +507,8 @@
         return self.send(array, lambda k, m, h, c: (3 - k, m, h, c))
 
 
-def scatter_choices(moves, own, across, *pair):
-    rows = own.shape[0]
-    pair = [moves.partner(each) for each in pair]
-    merged = (across.astype(F32) + pair[0][:rows].astype(F32)).astype(BF16)
-    return own, pair[-1], merged
+def merge(across, far):
+    return (across.astype(F32) + far.astype(F32)).astype(BF16)
 
 
 def staged(moves, weights):
@@ -502,7 +518,7 @@
 
 def piece_plan(depth):
     total = depth // CHUNK
-    cut = OPT['cut'] * total // 32
+    cut = 4 * total // 32
     shared = total // 2 - 2 * cut
     return cut, shared, lambda h, c: 2 * shared + (h * 2 + c) * cut, lambda c: c * shared
 
@@ -563,16 +579,14 @@
     if not in_parts:
         places = [0] * members
     table = jnp.stack([choice, member, first_cut, first_shared] + places).astype(jnp.int32)
-    if in_parts:
-        (one,) = split_pieces(by_part, table, 2, (cut,))
-        if OPT["kv"] == "after":
-            keys, values, out_cotangent = after([keys, values, out_cotangent], one)
-        one = moves.other_member(one)
-
     hops = range(1, heads // 2)
     far_keys = [moves.next_chip(keys, step) for step in hops]
     far_values = [moves.next_chip(values, step) for step in hops]
     core_keys, core_values = moves.other_core(keys), moves.other_core(values)
+    if in_parts:
+        (one,) = split_pieces(by_part, table, 2, (cut,))
+        one = moves.other_member(one)
+
     cot = out_cotangent
     cot_across, cot_beside = moves.mirror(cot), moves.partner(cot)
     if in_parts:
@@ -603,28 +617,48 @@
     far = moves.partner(across)
     x_parts = [normed, beside, across, far]
     pick, put, gates = routing(table, x_parts, rows, top, experts // top, local, slots)
-    sets = [[weights]]
+    ways, sets = (pick, put, gates), [[weights]]
+    own_outs, *own_kept = expert_call(
+        out_kernel, "own_out", ways, x_parts, sets, 0, table, slots, earlier=[cot_parts[3]]
+    )
+    (own_grads,) = expert_call(
+        grad_kernel, "own_grad", ways, cot_parts, sets, 0, table, slots, kept=own_kept
+    )
     if in_parts:
-        both, other = after([both, other], far, beside)
-        sets.append(
-            [one, one_core, both, moves.other_core(both), other, moves.other_core(other)]
-        )
+        both, other = after([both, other], own_outs)
+        sets = [[one, one_core, both, moves.other_core(both), other, moves.other_core(other)]]
     else:
-        sets += gathered_weights(moves, weights)
-    ways = (pick, put, gates)
+        sets = gathered_weights(moves, weights)
     *outs, active, slope = expert_call(
-        out_kernel, "expert_out", ways, x_parts, (), sets, table, slots, True
-    )
-    outs = scatter_choices(moves, *outs)
-    block_out = finish(out_sum_kernel, "out_sum", mix, *outs[:2], moves.mirror(outs[2]))
-    grads = expert_call(
-        grad_kernel, "expert_grad", ways, cot_parts, (active, slope), sets, table, slots, False
-    )
-    if OPT["order"]:
-        grads = [*grads[:2], *after(grads[2:], outs[2])]
-    grads = scatter_choices(moves, *grads)
+        out_kernel, "other_out", ways, x_parts, sets, 1, table, slots, [own_outs], [own_grads]
+    )
+    far_out = moves.partner(outs[2])
+    merged_out = merge(outs[1], far_out)
+    own_grad, across_grad, far_grad, beside = expert_call(
+        grad_kernel,
+        "other_grad",
+        ways,
+        cot_parts,
+        sets,
+        1,
+        table,
+        slots,
+        [own_grads, outs[3]],
+        kept=[active, slope],
+    )
+    (far_grad,) = after([moves.partner(far_grad)], merged_out)
+    merged_grad = merge(across_grad, far_grad)
+    beside = moves.partner(beside)
+    block_out = finish(out_sum_kernel, "out_sum", mix, outs[0], beside, moves.mirror(merged_out))
     stream_grad = finish(
-        grad_sum_kernel, "grad_sum", mix, out_cotangent, norm_gain[None, :], *grads[:2], moves.mirror(grads[2])
+        grad_sum_kernel,
+        "grad_sum",
+        mix,
+        out_cotangent,
+        norm_gain[None, :],
+        own_grad,
+        beside,
+        moves.mirror(merged_grad),
     )
     return block_out, stream_grad
 

time: 121 us -> 119 us (0.983)
  starting transfers between devices: 35.1 us -> 26.3 us
  Pallas kernels: 44.7 us -> 49.2 us
  waiting for transfers between devices: 35.8 us -> 38.1 us
    ppermute x23, starting transfers between devices: 35.1 us -> 26.3 us  [send(): return lax.ppermute(array, ('rcv', 'hd'), pairs)]
    pallas_call x4 -> x6, Pallas kernels: 21.2 us -> 25.7 us  [the longest x4 23.9 us: expert_call(): pl.pallas_call(functools.partial(kernel, plan), grid=(1,), in_specs=[pl.B...]
    ppermute x23, waiting for transfers between devices: 35.8 us -> 38.1 us  [send(): return lax.ppermute(array, ('rcv', 'hd'), pairs)]
    unnamed x31 -> x35, local copies, waits for them, and re-layouts: 2.16 us -> 2.55 us
  transfers between devices with their start and end apart: 23 -> 23, of which waited for: 10 -> 9; matrix products, arithmetic and copies ran while one was open for 2% -> 2% of each run, Pallas kernels for 28% -> 35%
where the time goes in v3:
time: 119 us; the launch traced here: 118 us
  Pallas kernels  49.2 us (41%)
  waiting for transfers between devices  38.1 us (32%)
  starting transfers between devices  26.3 us (22%)
  local copies, waits for them, and re-layouts  3.21 us (3%)
    ppermute x23, waiting for transfers between devices, send(): return lax.ppermute(array, ('rcv', 'hd'), pairs)  38.1 us
    ppermute x23, starting transfers between devices, send(): return lax.ppermute(array, ('rcv', 'hd'), pairs)  26.3 us
    pallas_call x4, Pallas kernels, expert_call(): pl.pallas_call(functools.partial(kernel, plan), grid=(1,), in_specs=[pl.B...  23.9 us
    pallas_call x1, Pallas kernels, split_experts(): pl.pallas_call(split_kernel, grid=(depth // rows,), in_specs=[pl.BlockSpe...  8.52 us
    pallas_call x2, Pallas kernels, split_pieces(): pl.pallas_call(functools.partial(split_pieces_kernel, counts, base), in_s...  6.66 us
    pallas_call x1, Pallas kernels, attention(): pl.pallas_call(functools.partial(attention_kernel, len(key_blocks)), in_s...  6.33 us
    unnamed x35, local copies, waits for them, and re-layouts  2.55 us
  transfers between devices with their start and end apart: 23, of which 9 were waited for; matrix products, arithmetic and copies ran while one was open for 2% of the time, Pallas kernels for 35%

profile of v3, /device:TPU:0, one launch (start us, length us, event | category | flops | bytes accessed | tf_op | source)
XLA Modules:
  0.0 118.5 jit_solution(1213548963283679151)
XLA Ops:
  0.6 3.0 %collective-permute-start.1 = (bf16[128,1024]{1,0:T(8,128)(2,1)}, bf16[128,1024]{1,0:T(8,128)(2,1)S(1)}, u32[]{:S(2)}, u32[]{:S(2)}) collective-permute-start(bf16[128,1024]{1,0:T(8,128)(2,1)} %refs_0_.3), channel_id=1, source_target_pairs={{0,2},{1,3},{2,0},{3,1},{4,6},{5,7},{6,4},{7,5},{8,10},{9,11},{10,... | collective-permute-start | bytes 786440 | tf_op jit(solution)/shard_map/ppermute | solution.py:492
  4.1 3.9 %collective-permute-start.6 = (bf16[128,1024]{1,0:T(8,128)(2,1)}, bf16[128,1024]{1,0:T(8,128)(2,1)S(1)}, u32[]{:S(2)}, u32[]{:S(2)}) collective-permute-start(bf16[128,1024]{1,0:T(8,128)(2,1)} %cot_ref.1), channel_id=1, source_target_pairs={{0,24},{1,25},{2,26},{3,27},{4,28},{5,29},{6,30},{7,31},{8,16},{9,... | collective-permute-start | bytes 786440 | tf_op jit(solution)/shard_map/ppermute | solution.py:492
  8.7 2.9 %split_pieces.2 = bf16[2,3,128,512]{3,2,1,0:T(8,128)(2,1)} custom-call(s32[11]{0:T(128)} %stack.37.where_ref.table_ref.start_ref, bf16[1024,3,2,512]{3,2,1,0:T(2,128)(2,1)} %bitcast.23), custom_call_target="tpu_custom_call" | custom-call | flops 3000999936 | bytes 10000 | tf_op jit(solution)/shard_map/split_pieces/pallas_call | solution.py:94
  11.6 1.6 %collective-permute-start.12 = (bf16[2,3,128,512]{3,2,1,0:T(8,128)(2,1)}, bf16[2,3,128,512]{3,2,1,0:T(8,128)(2,1)S(1)}, u32[]{:S(2)}, u32[]{:S(2)}) collective-permute-start(bf16[2,3,128,512]{3,2,1,0:T(8,128)(2,1)} %split_pieces.2), channel_id=1, source_target_pairs={{0,4},{1,5},{2,6},{3,7},{4,0},{5,1},{6,2},{7,3},{8,12},{9,13},{10,... | collective-permute-start | bytes 2359304 | tf_op jit(solution)/shard_map/ppermute | solution.py:492
  13.2 3.7 %split_pieces.3 = bf16[2,3,256,512]{3,2,1,0:T(8,128)(2,1)} custom-call(s32[11]{0:T(128)} %stack.37.where_ref.table_ref.start_ref, bf16[1024,3,2,512]{3,2,1,0:T(2,128)(2,1)} %bitcast.24, bf16[128,1024]{1,0:T(8,128)(2,1)} %copy-done.8), custom_call_target="tpu_custom_call" | custom-call | flops 3000999936 | bytes 10000 | tf_op jit(solution)/shard_map/split_pieces/pallas_call | solution.py:94
  17.7 1.6 %collective-permute-start.7 = (bf16[128,1024]{1,0:T(8,128)(2,1)S(1)}, bf16[128,1024]{1,0:T(8,128)(2,1)S(1)}, u32[]{:S(2)}, u32[]{:S(2)}) collective-permute-start(bf16[128,1024]{1,0:T(8,128)(2,1)S(1)} %copy-done), channel_id=1, source_target_pairs={{0,8},{1,9},{2,10},{3,11},{4,12},{5,13},{6,14},{7,15},{8,0},{9,1},... | collective-permute-start | bytes 786440 | tf_op jit(solution)/shard_map/ppermute | solution.py:492
  20.4 0.7 copy.20.refs_0_
  21.2 0.7 copy-done.12
  22.0 6.3 %attention.1 = (bf16[128,1024]{1,0:T(8,128)(2,1)}, bf16[144,1024]{1,0:T(8,128)(2,1)}) custom-call(f32[1,1024]{1,0:T(1,128)} %bitcast.21, bf16[16,1024]{1,0:T(8,128)(2,1)} %fusion.6.meta_ref, bf16[128,1024]{1,0:T(8,128)(2,1)} %q_hbm.1, bf16[128,1024]{1,0:T(8,128)(2,1)} %stream_hbm.1, bf16[1024,1024]{1,0:T(8,128)(2,1)} %proj_hbm.1, bf16[128,1024]{1,0:T(8,128)(2,1)} %refs_0_.3, ...), custom_call_target="tpu_custom_call" | custom-call | flops 1000000 | bytes 10000 | tf_op jit(solution)/shard_map/attention/pallas_call | solution.py:143
  28.3 2.6 %collective-permute-start.9 = (bf16[144,1024]{1,0:T(8,128)(2,1)}, bf16[144,1024]{1,0:T(8,128)(2,1)S(1)}, u32[]{:S(2)}, u32[]{:S(2)}) collective-permute-start(bf16[144,1024]{1,0:T(8,128)(2,1)} %after.6._.refs_1_.refs_0_), channel_id=1, source_target_pairs={{0,24},{1,25},{2,26},{3,27},{4,28},{5,29},{6,30},{7,31},{8,16},{9,... | collective-permute-start | bytes 884744 | tf_op jit(solution)/shard_map/ppermute | solution.py:492
  31.5 0.8 collective-permute-done.12.refs_0_
  32.3 1.5 %collective-permute-start.15 = (bf16[2,3,128,512]{3,2,1,0:T(8,128)(2,1)S(1)}, bf16[2,3,128,512]{3,2,1,0:T(8,128)(2,1)S(1)}, u32[]{:S(2)}, u32[]{:S(2)}) collective-permute-start(bf16[2,3,128,512]{3,2,1,0:T(8,128)(2,1)S(1)} %after.9.refs_4_), channel_id=1, source_target_pairs={{0,2},{1,3},{2,0},{3,1},{4,6},{5,7},{6,4},{7,5},{8,10},{9,11},{10,... | collective-permute-start | bytes 2359304 | tf_op jit(solution)/shard_map/ppermute | solution.py:492
  33.8 8.5 %split_experts.1 = (bf16[2,3,1024,512]{3,2,1,0:T(8,128)(2,1)}, f32[8,128]{1,0:T(8,128)}) custom-call(bf16[1024,3,2,512]{3,2,1,0:T(2,128)(2,1)} %bitcast.25, bf16[144,1024]{1,0:T(8,128)(2,1)} %after.6._.refs_1_.refs_0_), custom_call_target="tpu_custom_call" | custom-call | flops 8000999936 | bytes 10000 | tf_op jit(solution)/shard_map/split_experts/pallas_call | solution.py:53
  42.4 1.5 %collective-permute-start.8 = (bf16[144,1024]{1,0:T(8,128)(2,1)}, bf16[144,1024]{1,0:T(8,128)(2,1)S(1)}, u32[]{:S(2)}, u32[]{:S(2)}) collective-permute-start(bf16[144,1024]{1,0:T(8,128)(2,1)} %after.6._.refs_1_.refs_0_), channel_id=1, source_target_pairs={{0,8},{1,9},{2,10},{3,11},{4,12},{5,13},{6,14},{7,15},{8,0},{9,1},... | collective-permute-start | bytes 884744 | tf_op jit(solution)/shard_map/ppermute | solution.py:492
  43.8 1.4 %collective-permute-done.10.refs_2_.refs_5_.refs_3_ = bf16[128,1024]{1,0:T(8,128)(2,1)S(1)} collective-permute-done((bf16[128,1024]{1,0:T(8,128)(2,1)}, bf16[128,1024]{1,0:T(8,128)(2,1)S(1)}, u32[]{:S(2)}, u32[]{:S(2)}) %collective-permute-start.10) | collective-permute-done | bytes 262176 | tf_op jit(solution)/shard_map/ppermute | solution.py:492
  45.9 1.1 collective-permute-start.11
  47.1 5.4 %collective-permute-done.8.refs_1_ = bf16[144,1024]{1,0:T(8,128)(2,1)S(1)} collective-permute-done((bf16[144,1024]{1,0:T(8,128)(2,1)}, bf16[144,1024]{1,0:T(8,128)(2,1)S(1)}, u32[]{:S(2)}, u32[]{:S(2)}) %collective-permute-start.8) | collective-permute-done | bytes 294944 | tf_op jit(solution)/shard_map/ppermute | solution.py:492
  52.5 5.3 %collective-permute-done.11.refs_3_ = bf16[144,1024]{1,0:T(8,128)(2,1)S(1)} collective-permute-done((bf16[144,1024]{1,0:T(8,128)(2,1)S(1)}, bf16[144,1024]{1,0:T(8,128)(2,1)S(1)}, u32[]{:S(2)}, u32[]{:S(2)}) %collective-permute-start.11) | collective-permute-done | bytes 294944 | tf_op jit(solution)/shard_map/ppermute | solution.py:492
  57.8 1.9 %routing.1 = (bf16[640,512]{1,0:T(8,128)(2,1)S(1)}, bf16[512,640]{1,0:T(8,128)(2,1)S(1)}, f32[512,128]{1,0:T(8,128)S(1)}) custom-call(s32[11]{0:T(128)S(1)} %copy-done.6, bf16[144,1024]{1,0:T(8,128)(2,1)} %after.6._.refs_1_.refs_0_, bf16[144,1024]{1,0:T(8,128)(2,1)S(1)} %collective-permute-done.8.refs_1_, bf16[144,1024]{1,0:T(8,128)(2,1)S(1)} %after.8.refs_2_, ...), custom_call_target="tpu_custom_call" | custom-call | flops 1000000 | bytes 10000 | tf_op jit(solution)/shard_map/routing/pallas_call | solution.py:212
  59.7 6.2 %own_out.1 = (bf16[320,1024]{1,0:T(8,128)(2,1)S(1)}, bf16[320,512]{1,0:T(8,128)(2,1)S(1)}, bf16[320,512]{1,0:T(8,128)(2,1)S(1)}) custom-call(s32[11]{0:T(128)S(1)} %copy-done.6, bf16[640,512]{1,0:T(8,128)(2,1)S(1)} %get-tuple-element.27.pick_hbm, bf16[512,640]{1,0:T(8,128)(2,1)S(1)} %get-tuple-element.28.put_hbm, f32[512,128]{1,0:T(8,128)S(1)} %get-tuple-element.29.gate_hbm, ...), custom_call_target="tpu_custom_call" | custom-call | flops 1000000 | bytes 10000 | tf_op jit(solution)/shard_map/own_out/pallas_call | solution.py:407
  67.0 4.2 %own_grad.1.refs_11_.refs_10_ = bf16[320,1024]{1,0:T(8,128)(2,1)S(1)} custom-call(s32[11]{0:T(128)S(1)} %copy-done.6, bf16[640,512]{1,0:T(8,128)(2,1)S(1)} %get-tuple-element.27.pick_hbm, bf16[512,640]{1,0:T(8,128)(2,1)S(1)} %get-tuple-element.28.put_hbm, f32[512,128]{1,0:T(8,128)S(1)} %get-tuple-element.29.gate_hbm, bf16[128,1024]{1,0:T(8,128)(2,1)S(1)} %copy-done.1, ...), custom_call_target="tpu_custom_call" | custom-call | flops 5000999936 | bytes 10000 | tf_op jit(solution)/shard_map/own_grad/pallas_call | solution.py:407
  71.8 7.0 %other_out.1 = (bf16[128,1024]{1,0:T(8,128)(2,1)S(1)}, bf16[128,1024]{1,0:T(8,128)(2,1)S(1)}, bf16[128,1024]{1,0:T(8,128)(2,1)S(1)}, bf16[128,1024]{1,0:T(8,128)...) custom-call(s32[11]{0:T(128)S(1)} %copy-done.6, bf16[640,512]{1,0:T(8,128)(2,1)S(1)} %get-tuple-element.27.pick_hbm, ...), custom_call_target="tpu_custom_call" | custom-call | flops 1000000 | bytes 10000 | tf_op jit(solution)/shard_map/other_out/pallas_call | solution.py:407
  79.4 6.5 %other_grad.1 = (bf16[128,1024]{1,0:T(8,128)(2,1)S(1)}, bf16[128,1024]{1,0:T(8,128)(2,1)S(1)}, bf16[128,1024]{1,0:T(8,128)(2,1)S(1)}, bf16[256,1024]{1,0:T(8,128)(2,1)S(1)}) custom-call(s32[11]{0:T(128)S(1)} %copy-done.6, bf16[640,512]{1,0:T(8,128)(2,1)S(1)} %get-tuple-element.27.pick_hbm, bf16[512,640]{1,0:T(8,128)(2,1)S(1)} %get-tuple-element.28.put_hbm, ...), custom_call_target="tpu_custom_call" | custom-call | flops 6000999936 | bytes 10000 | tf_op jit(solution)/shard_map/other_grad/pallas_call | solution.py:407
  85.9 1.5 %collective-permute-start.21 = (bf16[128,1024]{1,0:T(8,128)(2,1)S(1)}, bf16[128,1024]{1,0:T(8,128)(2,1)S(1)}, u32[]{:S(2)}, u32[]{:S(2)}) collective-permute-start(bf16[128,1024]{1,0:T(8,128)(2,1)S(1)} %get-tuple-element.45), channel_id=1, source_target_pairs={{0,8},{1,9},{2,10},{3,11},{4,12},{5,13},{6,14},{7,15},{8,0},{9,1},... | collective-permute-start | bytes 786440 | tf_op jit(solution)/shard_map/ppermute | solution.py:492
  88.1 7.1 %collective-permute-done.21.refs_0_ = bf16[128,1024]{1,0:T(8,128)(2,1)S(1)} collective-permute-done((bf16[128,1024]{1,0:T(8,128)(2,1)S(1)}, bf16[128,1024]{1,0:T(8,128)(2,1)S(1)}, u32[]{:S(2)}, u32[]{:S(2)}) %collective-permute-start.21) | collective-permute-done | bytes 262176 | tf_op jit(solution)/shard_map/ppermute | solution.py:492
  95.2 1.5 %collective-permute-start.22 = (bf16[128,1024]{1,0:T(8,128)(2,1)S(1)}, bf16[128,1024]{1,0:T(8,128)(2,1)S(1)}, u32[]{:S(2)}, u32[]{:S(2)}) collective-permute-start(bf16[128,1024]{1,0:T(8,128)(2,1)S(1)} %add_convert_fusion), channel_id=1, source_target_pairs={{0,24},{1,25},{2,26},{3,27},{4,28},{5,29},{6,30},{7,31},{8,16},{9,... | collective-permute-start | bytes 786440 | tf_op jit(solution)/shard_map/ppermute | solution.py:492
  96.7 2.4 %collective-permute-start.20 = (bf16[128,1024]{1,0:T(8,128)(2,1)S(1)}, bf16[128,1024]{1,0:T(8,128)(2,1)S(1)}, u32[]{:S(2)}, u32[]{:S(2)}) collective-permute-start(bf16[128,1024]{1,0:T(8,128)(2,1)S(1)} %add_convert_fusion.1.refs_1_), channel_id=1, source_target_pairs={{0,24},{1,25},{2,26},{3,27},{4,28},{5,29},{6,30},{7,31},{8,16},{9,... | collective-permute-start | bytes 786440 | tf_op jit(solution)/shard_map/ppermute | solution.py:492
  99.1 6.2 %collective-permute-done.18.beside_ref = bf16[256,1024]{1,0:T(8,128)(2,1)S(1)} collective-permute-done((bf16[256,1024]{1,0:T(8,128)(2,1)S(1)}, bf16[256,1024]{1,0:T(8,128)(2,1)S(1)}, u32[]{:S(2)}, u32[]{:S(2)}) %collective-permute-start.18) | collective-permute-done | bytes 524320 | tf_op jit(solution)/shard_map/ppermute | solution.py:492
  105.3 7.8 %collective-permute-done.22.merged_ref = bf16[128,1024]{1,0:T(8,128)(2,1)S(1)} collective-permute-done((bf16[128,1024]{1,0:T(8,128)(2,1)S(1)}, bf16[128,1024]{1,0:T(8,128)(2,1)S(1)}, u32[]{:S(2)}, u32[]{:S(2)}) %collective-permute-start.22) | collective-permute-done | bytes 262176 | tf_op jit(solution)/shard_map/ppermute | solution.py:492
  113.1 1.0 grad_sum.1
  114.2 3.5 %collective-permute-done.20.merged_ref = bf16[128,1024]{1,0:T(8,128)(2,1)S(1)} collective-permute-done((bf16[128,1024]{1,0:T(8,128)(2,1)S(1)}, bf16[128,1024]{1,0:T(8,128)(2,1)S(1)}, u32[]{:S(2)}, u32[]{:S(2)}) %collective-permute-start.20) | collective-permute-done | bytes 262176 | tf_op jit(solution)/shard_map/ppermute | solution.py:492
  117.6 0.8 out_sum.1
  (73 shorter events, 7.4 us)
Async XLA Ops:
  0.6 11.0 %collective-permute-start.1 = (bf16[128,1024]{1,0:T(8,128)(2,1)}, bf16[128,1024]{1,0:T(8,128)(2,1)S(1)}, u32[]{:S(2)}, u32[]{:S(2)}) collective-permute-start(bf16[128,1024]{1,0:T(8,128)(2,1)} %refs_0_.3), channel_id=1, source_target_pairs={{0,2},{1,3},{2,0},{3,1},{4,6},{5,7},{6,4},{7,5},{8,10},{9,11},{10,... | collective-permute-start | bytes 786440 | tf_op jit(solution)/shard_map/ppermute | solution.py:492
  3.6 14.1 %collective-permute-start = (bf16[128,1024]{1,0:T(8,128)(2,1)}, bf16[128,1024]{1,0:T(8,128)(2,1)S(1)}, u32[]{:S(2)}, u32[]{:S(2)}) collective-permute-start(bf16[128,1024]{1,0:T(8,128)(2,1)} %refs_0_.3), channel_id=1, source_target_pairs={{0,1},{1,0},{2,3},{3,2},{4,5},{5,4},{6,7},{7,6},{8,9},{9,8},{10,11... | collective-permute-start | bytes 786440 | tf_op jit(solution)/shard_map/ppermute | solution.py:492
  3.6 13.4 %collective-permute-start.4 = (bf16[128,1024]{1,0:T(8,128)(2,1)}, bf16[128,1024]{1,0:T(8,128)(2,1)S(1)}, u32[]{:S(2)}, u32[]{:S(2)}) collective-permute-start(bf16[128,1024]{1,0:T(8,128)(2,1)} %refs_4_.1), channel_id=1, source_target_pairs={{0,2},{1,3},{2,0},{3,1},{4,6},{5,7},{6,4},{7,5},{8,10},{9,11},{10,... | collective-permute-start | bytes 786440 | tf_op jit(solution)/shard_map/ppermute | solution.py:492
  3.8 15.5 %collective-permute-start.3 = (bf16[128,1024]{1,0:T(8,128)(2,1)}, bf16[128,1024]{1,0:T(8,128)(2,1)}, u32[]{:S(2)}, u32[]{:S(2)}) collective-permute-start(bf16[128,1024]{1,0:T(8,128)(2,1)} %refs_4_.1), channel_id=1, source_target_pairs={{0,1},{1,0},{2,3},{3,2},{4,5},{5,4},{6,7},{7,6},{8,9},{9,8},{10,11... | collective-permute-start | bytes 786440 | tf_op jit(solution)/shard_map/ppermute | solution.py:492
  4.1 15.1 %collective-permute-start.6 = (bf16[128,1024]{1,0:T(8,128)(2,1)}, bf16[128,1024]{1,0:T(8,128)(2,1)S(1)}, u32[]{:S(2)}, u32[]{:S(2)}) collective-permute-start(bf16[128,1024]{1,0:T(8,128)(2,1)} %cot_ref.1), channel_id=1, source_target_pairs={{0,24},{1,25},{2,26},{3,27},{4,28},{5,29},{6,30},{7,31},{8,16},{9,... | collective-permute-start | bytes 786440 | tf_op jit(solution)/shard_map/ppermute | solution.py:492
  11.6 6.1 %copy-start.14 = (f32[128,4]{0,1:T(4,128)S(1)}, f32[128,4]{0,1:T(4,128)}, u32[]{:S(2)}) copy-start(f32[128,4]{0,1:T(4,128)} %param.18) | copy-start | bytes 6148
  11.6 6.1 %copy-start = (bf16[128,1024]{1,0:T(8,128)(2,1)S(1)}, bf16[128,1024]{1,0:T(8,128)(2,1)}, u32[]{:S(2)}) copy-start(bf16[128,1024]{1,0:T(8,128)(2,1)} %cot_ref.1) | copy-start | bytes 786436
  11.6 8.2 %copy-start.13 = (s32[128,4]{0,1:T(4,128)S(1)}, s32[128,4]{0,1:T(4,128)}, u32[]{:S(2)}) copy-start(s32[128,4]{0,1:T(4,128)} %param.17) | copy-start | bytes 6148
  11.6 20.7 %collective-permute-start.12 = (bf16[2,3,128,512]{3,2,1,0:T(8,128)(2,1)}, bf16[2,3,128,512]{3,2,1,0:T(8,128)(2,1)S(1)}, u32[]{:S(2)}, u32[]{:S(2)}) collective-permute-start(bf16[2,3,128,512]{3,2,1,0:T(8,128)(2,1)} %split_pieces.2), channel_id=1, source_target_pairs={{0,4},{1,5},{2,6},{3,7},{4,0},{5,1},{6,2},{7,3},{8,12},{9,13},{10,... | collective-permute-start | bytes 2359304 | tf_op jit(solution)/shard_map/ppermute | solution.py:492
  17.0 5.0 %copy-start.10 = (bf16[128,1024]{1,0:T(8,128)(2,1)}, bf16[128,1024]{1,0:T(8,128)(2,1)S(1)}, u32[]{:S(2)}) copy-start(bf16[128,1024]{1,0:T(8,128)(2,1)S(1)} %collective-permute-done.4.refs_6_) | copy-start | bytes 786436
  17.0 49.0 %collective-permute-start.14 = (bf16[2,3,256,512]{3,2,1,0:T(8,128)(2,1)}, bf16[2,3,256,512]{3,2,1,0:T(8,128)(2,1)S(1)}, u32[]{:S(2)}, u32[]{:S(2)}) collective-permute-start(bf16[2,3,256,512]{3,2,1,0:T(8,128)(2,1)} %split_pieces.3), channel_id=1, source_target_pairs={{0,4},{1,5},{2,6},{3,7},{4,0},{5,1},{6,2},{7,3},{8,12},{9,13},{10,... | collective-permute-start | bytes 4718600 | tf_op jit(solution)/shard_map/ppermute | solution.py:492
  17.7 10.6 %collective-permute-start.7 = (bf16[128,1024]{1,0:T(8,128)(2,1)S(1)}, bf16[128,1024]{1,0:T(8,128)(2,1)S(1)}, u32[]{:S(2)}, u32[]{:S(2)}) collective-permute-start(bf16[128,1024]{1,0:T(8,128)(2,1)S(1)} %copy-done), channel_id=1, source_target_pairs={{0,8},{1,9},{2,10},{3,11},{4,12},{5,13},{6,14},{7,15},{8,0},{9,1},... | collective-permute-start | bytes 786440 | tf_op jit(solution)/shard_map/ppermute | solution.py:492
  19.3 1.9 %collective-permute-start.2 = (bf16[128,1024]{1,0:T(8,128)(2,1)}, bf16[128,1024]{1,0:T(8,128)(2,1)S(1)}, u32[]{:S(2)}, u32[]{:S(2)}) collective-permute-start(bf16[128,1024]{1,0:T(8,128)(2,1)} %copy-done.8), channel_id=1, source_target_pairs={{0,1},{1,0},{2,3},{3,2},{4,5},{5,4},{6,7},{7,6},{8,9},{9,8},{10,11... | collective-permute-start | bytes 786440 | tf_op jit(solution)/shard_map/ppermute | solution.py:492
  19.3 1.9 %collective-permute-start.5 = (bf16[128,1024]{1,0:T(8,128)(2,1)S(1)}, bf16[128,1024]{1,0:T(8,128)(2,1)S(1)}, u32[]{:S(2)}, u32[]{:S(2)}) collective-permute-start(bf16[128,1024]{1,0:T(8,128)(2,1)S(1)} %collective-permute-done.4.refs_6_), channel_id=1, source_target_pairs={{0,1},{1,0},{2,3},{3,2},{4,5},{5,4},{6,7},{7,6},{8,9},{9,8},{10,11... | collective-permute-start | bytes 786440 | tf_op jit(solution)/shard_map/ppermute | solution.py:492
  28.3 16.9 %collective-permute-start.9 = (bf16[144,1024]{1,0:T(8,128)(2,1)}, bf16[144,1024]{1,0:T(8,128)(2,1)S(1)}, u32[]{:S(2)}, u32[]{:S(2)}) collective-permute-start(bf16[144,1024]{1,0:T(8,128)(2,1)} %after.6._.refs_1_.refs_0_), channel_id=1, source_target_pairs={{0,24},{1,25},{2,26},{3,27},{4,28},{5,29},{6,30},{7,31},{8,16},{9,... | collective-permute-start | bytes 884744 | tf_op jit(solution)/shard_map/ppermute | solution.py:492
  30.9 14.4 %collective-permute-start.10 = (bf16[128,1024]{1,0:T(8,128)(2,1)}, bf16[128,1024]{1,0:T(8,128)(2,1)S(1)}, u32[]{:S(2)}, u32[]{:S(2)}) collective-permute-start(bf16[128,1024]{1,0:T(8,128)(2,1)} %after.7), channel_id=1, source_target_pairs={{0,8},{1,9},{2,10},{3,11},{4,12},{5,13},{6,14},{7,15},{8,0},{9,1},... | collective-permute-start | bytes 786440 | tf_op jit(solution)/shard_map/ppermute | solution.py:492
  32.3 25.5 %copy-start.6 = (s32[11]{0:T(128)S(1)}, s32[11]{0:T(128)}, u32[]{:S(2)}) copy-start(s32[11]{0:T(128)} %stack.37.where_ref.table_ref.start_ref) | copy-start | bytes 136
  32.3 33.7 %collective-permute-start.15 = (bf16[2,3,128,512]{3,2,1,0:T(8,128)(2,1)S(1)}, bf16[2,3,128,512]{3,2,1,0:T(8,128)(2,1)S(1)}, u32[]{:S(2)}, u32[]{:S(2)}) collective-permute-start(bf16[2,3,128,512]{3,2,1,0:T(8,128)(2,1)S(1)} %after.9.refs_4_), channel_id=1, source_target_pairs={{0,2},{1,3},{2,0},{3,1},{4,6},{5,7},{6,4},{7,5},{8,10},{9,11},{10,... | collective-permute-start | bytes 2359304 | tf_op jit(solution)/shard_map/ppermute | solution.py:492
  42.4 10.2 %collective-permute-start.8 = (bf16[144,1024]{1,0:T(8,128)(2,1)}, bf16[144,1024]{1,0:T(8,128)(2,1)S(1)}, u32[]{:S(2)}, u32[]{:S(2)}) collective-permute-start(bf16[144,1024]{1,0:T(8,128)(2,1)} %after.6._.refs_1_.refs_0_), channel_id=1, source_target_pairs={{0,8},{1,9},{2,10},{3,11},{4,12},{5,13},{6,14},{7,15},{8,0},{9,1},... | collective-permute-start | bytes 884744 | tf_op jit(solution)/shard_map/ppermute | solution.py:492
  45.9 11.9 %collective-permute-start.11 = (bf16[144,1024]{1,0:T(8,128)(2,1)S(1)}, bf16[144,1024]{1,0:T(8,128)(2,1)S(1)}, u32[]{:S(2)}, u32[]{:S(2)}) collective-permute-start(bf16[144,1024]{1,0:T(8,128)(2,1)S(1)} %after.8.refs_2_), channel_id=1, source_target_pairs={{0,8},{1,9},{2,10},{3,11},{4,12},{5,13},{6,14},{7,15},{8,0},{9,1},... | collective-permute-start | bytes 884744 | tf_op jit(solution)/shard_map/ppermute | solution.py:492
  59.7 7.0 %slice-start = ((s8[6291456]{0:T(1024)(128)(4,1)}), s8[4194304]{0:T(1024)(128)(4,1)S(1)}, s32[]{:S(2)}) async-start(s8[6291456]{0:T(1024)(128)(4,1)} %bitcast.19), calls=%async_computation | async-start | bytes 8388608
  59.7 7.0 %slice-start.1 = ((s8[6291456]{0:T(1024)(128)(4,1)}), s8[2097152]{0:T(1024)(128)(4,1)S(1)}, s32[]{:S(2)}) async-start(s8[6291456]{0:T(1024)(128)(4,1)} %bitcast.19), calls=%async_computation.1 | async-start | bytes 4194304
  66.0 5.7 %collective-permute-start.16 = (bf16[2,3,256,512]{3,2,1,0:T(8,128)(2,1)S(1)}, bf16[2,3,256,512]{3,2,1,0:T(8,128)(2,1)S(1)}, u32[]{:S(2)}, u32[]{:S(2)}) collective-permute-start(bf16[2,3,256,512]{3,2,1,0:T(8,128)(2,1)S(1)} %get-tuple-element.32.refs_6_), channel_id=1, source_target_pairs={{0,1},{1,0},{2,3},{3,2},{4,5},{5,4},{6,7},{7,6},{8,9},{9,8},{10,11... | collective-permute-start | bytes 4718600 | tf_op jit(solution)/shard_map/ppermute | solution.py:492
  66.1 5.1 %collective-permute-start.13 = (bf16[2,3,128,512]{3,2,1,0:T(8,128)(2,1)S(1)}, bf16[2,3,128,512]{3,2,1,0:T(8,128)(2,1)S(1)}, u32[]{:S(2)}, u32[]{:S(2)}) collective-permute-start(bf16[2,3,128,512]{3,2,1,0:T(8,128)(2,1)S(1)} %after.9.refs_4_), channel_id=1, source_target_pairs={{0,1},{1,0},{2,3},{3,2},{4,5},{5,4},{6,7},{7,6},{8,9},{9,8},{10,11... | collective-permute-start | bytes 2359304 | tf_op jit(solution)/shard_map/ppermute | solution.py:492
  66.6 5.1 %collective-permute-start.17 = (bf16[2,3,128,512]{3,2,1,0:T(8,128)(2,1)S(1)}, bf16[2,3,128,512]{3,2,1,0:T(8,128)(2,1)S(1)}, u32[]{:S(2)}, u32[]{:S(2)}) collective-permute-start(bf16[2,3,128,512]{3,2,1,0:T(8,128)(2,1)S(1)} %get-tuple-element.33.refs_8_), channel_id=1, source_target_pairs={{0,1},{1,0},{2,3},{3,2},{4,5},{5,4},{6,7},{7,6},{8,9},{9,8},{10,11... | collective-permute-start | bytes 2359304 | tf_op jit(solution)/shard_map/ppermute | solution.py:492
  78.7 9.3 %collective-permute-start.19 = (bf16[128,1024]{1,0:T(8,128)(2,1)S(1)}, bf16[128,1024]{1,0:T(8,128)(2,1)S(1)}, u32[]{:S(2)}, u32[]{:S(2)}) collective-permute-start(bf16[128,1024]{1,0:T(8,128)(2,1)S(1)} %get-tuple-element.42), channel_id=1, source_target_pairs={{0,8},{1,9},{2,10},{3,11},{4,12},{5,13},{6,14},{7,15},{8,0},{9,1},... | collective-permute-start | bytes 786440 | tf_op jit(solution)/shard_map/ppermute | solution.py:492
  85.9 27.3 %copy-start.2 = (bf16[128,1024]{1,0:T(8,128)(2,1)S(1)}, bf16[128,1024]{1,0:T(8,128)(2,1)}, u32[]{:S(2)}) copy-start(bf16[128,1024]{1,0:T(8,128)(2,1)} %get-tuple-element.24.mix_ref) | copy-start | bytes 786436
  85.9 27.3 %copy-start.5 = (f32[1024]{0:T(1024)S(1)}, f32[1024]{0:T(1024)}, u32[]{:S(2)}) copy-start(f32[1024]{0:T(1024)} %param.15) | copy-start | bytes 12292
  85.9 9.3 %collective-permute-start.21 = (bf16[128,1024]{1,0:T(8,128)(2,1)S(1)}, bf16[128,1024]{1,0:T(8,128)(2,1)S(1)}, u32[]{:S(2)}, u32[]{:S(2)}) collective-permute-start(bf16[128,1024]{1,0:T(8,128)(2,1)S(1)} %get-tuple-element.45), channel_id=1, source_target_pairs={{0,8},{1,9},{2,10},{3,11},{4,12},{5,13},{6,14},{7,15},{8,0},{9,1},... | collective-permute-start | bytes 786440 | tf_op jit(solution)/shard_map/ppermute | solution.py:492
  87.4 18.0 %collective-permute-start.18 = (bf16[256,1024]{1,0:T(8,128)(2,1)S(1)}, bf16[256,1024]{1,0:T(8,128)(2,1)S(1)}, u32[]{:S(2)}, u32[]{:S(2)}) collective-permute-start(bf16[256,1024]{1,0:T(8,128)(2,1)S(1)} %get-tuple-element.40), channel_id=1, source_target_pairs={{0,8},{1,9},{2,10},{3,11},{4,12},{5,13},{6,14},{7,15},{8,0},{9,1},... | collective-permute-start | bytes 1572872 | tf_op jit(solution)/shard_map/ppermute | solution.py:492
  95.2 17.9 %collective-permute-start.22 = (bf16[128,1024]{1,0:T(8,128)(2,1)S(1)}, bf16[128,1024]{1,0:T(8,128)(2,1)S(1)}, u32[]{:S(2)}, u32[]{:S(2)}) collective-permute-start(bf16[128,1024]{1,0:T(8,128)(2,1)S(1)} %add_convert_fusion), channel_id=1, source_target_pairs={{0,24},{1,25},{2,26},{3,27},{4,28},{5,29},{6,30},{7,31},{8,16},{9,... | collective-permute-start | bytes 786440 | tf_op jit(solution)/shard_map/ppermute | solution.py:492
  96.7 20.9 %collective-permute-start.20 = (bf16[128,1024]{1,0:T(8,128)(2,1)S(1)}, bf16[128,1024]{1,0:T(8,128)(2,1)S(1)}, u32[]{:S(2)}, u32[]{:S(2)}) collective-permute-start(bf16[128,1024]{1,0:T(8,128)(2,1)S(1)} %add_convert_fusion.1.refs_1_), channel_id=1, source_target_pairs={{0,24},{1,25},{2,26},{3,27},{4,28},{5,29},{6,30},{7,31},{8,16},{9,... | collective-permute-start | bytes 786440 | tf_op jit(solution)/shard_map/ppermute | solution.py:492
  (8 other events, 14.1 us)

commit v4 on v3

--- a/solution.py
+++ b/solution.py
@@ -612,7 +612,7 @@
         one_core = moves.other_core(one)
     weights, done = split_experts(by_part, normed)
     (cot_forward,) = after([cot_across], normed)
-    cot_parts = [cot, cot_beside, cot_across, moves.partner(cot_forward)]
+    cot_parts = [cot, cot_beside, cot_forward, moves.partner(cot_forward)]
     (across,) = after([across], done, cot_parts[3])
     far = moves.partner(across)
     x_parts = [normed, beside, across, far]

time: 119 us -> 122 us (1.025)
  waiting for transfers between devices: 38.1 us -> 43.7 us
  starting transfers between devices: 26.3 us -> 23.9 us
    ppermute x23, waiting for transfers between devices: 38.1 us -> 43.7 us  [send(): return lax.ppermute(array, ('rcv', 'hd'), pairs)]
    ppermute x23, starting transfers between devices: 26.3 us -> 23.9 us  [send(): return lax.ppermute(array, ('rcv', 'hd'), pairs)]
    unnamed x35 -> x32, local copies, waits for them, and re-layouts: 2.55 us -> 2.48 us
  transfers between devices with their start and end apart: 23 -> 23, of which waited for: 9 -> 12; matrix products, arithmetic and copies ran while one was open for 2% -> 1% of each run, Pallas kernels for 35% -> 34%
where the time goes in v4:
time: 122 us; the launch traced here: 121 us
  Pallas kernels  49.1 us (40%)
  waiting for transfers between devices  43.7 us (36%)
  starting transfers between devices  23.9 us (20%)
  local copies, waits for them, and re-layouts  3.09 us (3%)
    ppermute x23, waiting for transfers between devices, send(): return lax.ppermute(array, ('rcv', 'hd'), pairs)  43.7 us
    pallas_call x4, Pallas kernels, expert_call(): pl.pallas_call(functools.partial(kernel, plan), grid=(1,), in_specs=[pl.B...  23.9 us
    ppermute x23, starting transfers between devices, send(): return lax.ppermute(array, ('rcv', 'hd'), pairs)  23.9 us
    pallas_call x1, Pallas kernels, split_experts(): pl.pallas_call(split_kernel, grid=(depth // rows,), in_specs=[pl.BlockSpe...  8.51 us
    pallas_call x2, Pallas kernels, split_pieces(): pl.pallas_call(functools.partial(split_pieces_kernel, counts, base), in_s...  6.67 us
    pallas_call x1, Pallas kernels, attention(): pl.pallas_call(functools.partial(attention_kernel, len(key_blocks)), in_s...  6.34 us
    unnamed x32, local copies, waits for them, and re-layouts  2.48 us
  transfers between devices with their start and end apart: 23, of which 12 were waited for; matrix products, arithmetic and copies ran while one was open for 1% of the time, Pallas kernels for 34%

profile of v4, /device:TPU:0, one launch (start us, length us, event | category | flops | bytes accessed | tf_op | source)
XLA Modules:
  0.0 121.4 jit_solution(1046888591444483800)
XLA Ops:
  0.6 3.0 %collective-permute-start.1 = (bf16[128,1024]{1,0:T(8,128)(2,1)}, bf16[128,1024]{1,0:T(8,128)(2,1)S(1)}, u32[]{:S(2)}, u32[]{:S(2)}) collective-permute-start(bf16[128,1024]{1,0:T(8,128)(2,1)} %refs_0_.3), channel_id=1, source_target_pairs={{0,2},{1,3},{2,0},{3,1},{4,6},{5,7},{6,4},{7,5},{8,10},{9,11},{10,... | collective-permute-start | bytes 786440 | tf_op jit(solution)/shard_map/ppermute | solution.py:492
  4.8 2.9 %split_pieces.2 = bf16[2,3,128,512]{3,2,1,0:T(8,128)(2,1)} custom-call(s32[11]{0:T(128)} %stack.37.where_ref.table_ref.start_ref, bf16[1024,3,2,512]{3,2,1,0:T(2,128)(2,1)} %bitcast.23), custom_call_target="tpu_custom_call" | custom-call | flops 3000999936 | bytes 10000 | tf_op jit(solution)/shard_map/split_pieces/pallas_call | solution.py:94
  7.7 1.8 %collective-permute-start.12 = (bf16[2,3,128,512]{3,2,1,0:T(8,128)(2,1)}, bf16[2,3,128,512]{3,2,1,0:T(8,128)(2,1)S(1)}, u32[]{:S(2)}, u32[]{:S(2)}) collective-permute-start(bf16[2,3,128,512]{3,2,1,0:T(8,128)(2,1)} %split_pieces.2), channel_id=1, source_target_pairs={{0,4},{1,5},{2,6},{3,7},{4,0},{5,1},{6,2},{7,3},{8,12},{9,13},{10,... | collective-permute-start | bytes 2359304 | tf_op jit(solution)/shard_map/ppermute | solution.py:492
  9.6 1.4 %collective-permute-done.1.refs_2_.refs_0_ = bf16[128,1024]{1,0:T(8,128)(2,1)S(1)} collective-permute-done((bf16[128,1024]{1,0:T(8,128)(2,1)}, bf16[128,1024]{1,0:T(8,128)(2,1)S(1)}, u32[]{:S(2)}, u32[]{:S(2)}) %collective-permute-start.1) | collective-permute-done | bytes 262176 | tf_op jit(solution)/shard_map/ppermute | solution.py:492
  11.7 3.7 %split_pieces.3 = bf16[2,3,256,512]{3,2,1,0:T(8,128)(2,1)} custom-call(s32[11]{0:T(128)} %stack.37.where_ref.table_ref.start_ref, bf16[1024,3,2,512]{3,2,1,0:T(2,128)(2,1)} %bitcast.24, bf16[128,1024]{1,0:T(8,128)(2,1)} %copy-done.8), custom_call_target="tpu_custom_call" | custom-call | flops 3000999936 | bytes 10000 | tf_op jit(solution)/shard_map/split_pieces/pallas_call | solution.py:94
  15.8 1.8 %collective-permute-start.14 = (bf16[2,3,256,512]{3,2,1,0:T(8,128)(2,1)}, bf16[2,3,256,512]{3,2,1,0:T(8,128)(2,1)S(1)}, u32[]{:S(2)}, u32[]{:S(2)}) collective-permute-start(bf16[2,3,256,512]{3,2,1,0:T(8,128)(2,1)} %split_pieces.3), channel_id=1, source_target_pairs={{0,4},{1,5},{2,6},{3,7},{4,0},{5,1},{6,2},{7,3},{8,12},{9,13},{10,... | collective-permute-start | bytes 4718600 | tf_op jit(solution)/shard_map/ppermute | solution.py:492
  17.6 1.6 %collective-permute-start.7 = (bf16[128,1024]{1,0:T(8,128)(2,1)S(1)}, bf16[128,1024]{1,0:T(8,128)(2,1)S(1)}, u32[]{:S(2)}, u32[]{:S(2)}) collective-permute-start(bf16[128,1024]{1,0:T(8,128)(2,1)S(1)} %copy-done), channel_id=1, source_target_pairs={{0,8},{1,9},{2,10},{3,11},{4,12},{5,13},{6,14},{7,15},{8,0},{9,1},... | collective-permute-start | bytes 786440 | tf_op jit(solution)/shard_map/ppermute | solution.py:492
  19.3 2.5 %collective-permute-start.6 = (bf16[128,1024]{1,0:T(8,128)(2,1)S(1)}, bf16[128,1024]{1,0:T(8,128)(2,1)S(1)}, u32[]{:S(2)}, u32[]{:S(2)}) collective-permute-start(bf16[128,1024]{1,0:T(8,128)(2,1)S(1)} %copy-done), channel_id=1, source_target_pairs={{0,24},{1,25},{2,26},{3,27},{4,28},{5,29},{6,30},{7,31},{8,16},{9,... | collective-permute-start | bytes 786440 | tf_op jit(solution)/shard_map/ppermute | solution.py:492
  22.4 0.9 collective-permute-done.5.refs_7_
  24.0 6.3 %attention.1 = (bf16[128,1024]{1,0:T(8,128)(2,1)}, bf16[144,1024]{1,0:T(8,128)(2,1)}) custom-call(f32[1,1024]{1,0:T(1,128)} %bitcast.21, bf16[16,1024]{1,0:T(8,128)(2,1)} %fusion.6.meta_ref, bf16[128,1024]{1,0:T(8,128)(2,1)} %q_hbm.1, bf16[128,1024]{1,0:T(8,128)(2,1)} %stream_hbm.1, bf16[1024,1024]{1,0:T(8,128)(2,1)} %proj_hbm.1, bf16[128,1024]{1,0:T(8,128)(2,1)} %refs_0_.3, ...), custom_call_target="tpu_custom_call" | custom-call | flops 1000000 | bytes 10000 | tf_op jit(solution)/shard_map/attention/pallas_call | solution.py:143
  30.4 2.8 %collective-permute-done.6.refs_1_.refs_0_ = bf16[128,1024]{1,0:T(8,128)(2,1)S(1)} collective-permute-done((bf16[128,1024]{1,0:T(8,128)(2,1)S(1)}, bf16[128,1024]{1,0:T(8,128)(2,1)S(1)}, u32[]{:S(2)}, u32[]{:S(2)}) %collective-permute-start.6) | collective-permute-done | bytes 262176 | tf_op jit(solution)/shard_map/ppermute | solution.py:492
  33.2 1.5 %collective-permute-start.9 = (bf16[144,1024]{1,0:T(8,128)(2,1)}, bf16[144,1024]{1,0:T(8,128)(2,1)S(1)}, u32[]{:S(2)}, u32[]{:S(2)}) collective-permute-start(bf16[144,1024]{1,0:T(8,128)(2,1)} %after.6._.refs_1_.refs_0_), channel_id=1, source_target_pairs={{0,24},{1,25},{2,26},{3,27},{4,28},{5,29},{6,30},{7,31},{8,16},{9,... | collective-permute-start | bytes 884744 | tf_op jit(solution)/shard_map/ppermute | solution.py:492
  34.7 1.9 %collective-permute-start.10 = (bf16[128,1024]{1,0:T(8,128)(2,1)S(1)}, bf16[128,1024]{1,0:T(8,128)(2,1)S(1)}, u32[]{:S(2)}, u32[]{:S(2)}) collective-permute-start(bf16[128,1024]{1,0:T(8,128)(2,1)S(1)} %after.7.refs_2_), channel_id=1, source_target_pairs={{0,8},{1,9},{2,10},{3,11},{4,12},{5,13},{6,14},{7,15},{8,0},{9,1},... | collective-permute-start | bytes 786440 | tf_op jit(solution)/shard_map/ppermute | solution.py:492
  36.6 1.6 %collective-permute-start.15 = (bf16[2,3,128,512]{3,2,1,0:T(8,128)(2,1)S(1)}, bf16[2,3,128,512]{3,2,1,0:T(8,128)(2,1)S(1)}, u32[]{:S(2)}, u32[]{:S(2)}) collective-permute-start(bf16[2,3,128,512]{3,2,1,0:T(8,128)(2,1)S(1)} %after.9.refs_4_), channel_id=1, source_target_pairs={{0,2},{1,3},{2,0},{3,1},{4,6},{5,7},{6,4},{7,5},{8,10},{9,11},{10,... | collective-permute-start | bytes 2359304 | tf_op jit(solution)/shard_map/ppermute | solution.py:492
  38.2 8.5 %split_experts.1 = (bf16[2,3,1024,512]{3,2,1,0:T(8,128)(2,1)}, f32[8,128]{1,0:T(8,128)}) custom-call(bf16[1024,3,2,512]{3,2,1,0:T(2,128)(2,1)} %bitcast.25, bf16[144,1024]{1,0:T(8,128)(2,1)} %after.6._.refs_1_.refs_0_), custom_call_target="tpu_custom_call" | custom-call | flops 8000999936 | bytes 10000 | tf_op jit(solution)/shard_map/split_experts/pallas_call | solution.py:53
  46.8 1.7 %collective-permute-done.10.refs_2_.refs_5_.refs_3_ = bf16[128,1024]{1,0:T(8,128)(2,1)S(1)} collective-permute-done((bf16[128,1024]{1,0:T(8,128)(2,1)S(1)}, bf16[128,1024]{1,0:T(8,128)(2,1)S(1)}, u32[]{:S(2)}, u32[]{:S(2)}) %collective-permute-start.10) | collective-permute-done | bytes 262176 | tf_op jit(solution)/shard_map/ppermute | solution.py:492
  49.4 7.4 %collective-permute-done.8.refs_1_ = bf16[144,1024]{1,0:T(8,128)(2,1)S(1)} collective-permute-done((bf16[144,1024]{1,0:T(8,128)(2,1)}, bf16[144,1024]{1,0:T(8,128)(2,1)S(1)}, u32[]{:S(2)}, u32[]{:S(2)}) %collective-permute-start.8) | collective-permute-done | bytes 294944 | tf_op jit(solution)/shard_map/ppermute | solution.py:492
  56.8 3.2 %collective-permute-done.11.refs_3_ = bf16[144,1024]{1,0:T(8,128)(2,1)S(1)} collective-permute-done((bf16[144,1024]{1,0:T(8,128)(2,1)S(1)}, bf16[144,1024]{1,0:T(8,128)(2,1)S(1)}, u32[]{:S(2)}, u32[]{:S(2)}) %collective-permute-start.11) | collective-permute-done | bytes 294944 | tf_op jit(solution)/shard_map/ppermute | solution.py:492
  60.0 1.9 %routing.1 = (bf16[640,512]{1,0:T(8,128)(2,1)S(1)}, bf16[512,640]{1,0:T(8,128)(2,1)S(1)}, f32[512,128]{1,0:T(8,128)S(1)}) custom-call(s32[11]{0:T(128)S(1)} %copy-done.6, bf16[144,1024]{1,0:T(8,128)(2,1)} %after.6._.refs_1_.refs_0_, bf16[144,1024]{1,0:T(8,128)(2,1)S(1)} %collective-permute-done.8.refs_1_, bf16[144,1024]{1,0:T(8,128)(2,1)S(1)} %after.8.refs_2_, ...), custom_call_target="tpu_custom_call" | custom-call | flops 1000000 | bytes 10000 | tf_op jit(solution)/shard_map/routing/pallas_call | solution.py:212
  61.9 6.2 %own_out.1 = (bf16[320,1024]{1,0:T(8,128)(2,1)S(1)}, bf16[320,512]{1,0:T(8,128)(2,1)S(1)}, bf16[320,512]{1,0:T(8,128)(2,1)S(1)}) custom-call(s32[11]{0:T(128)S(1)} %copy-done.6, bf16[640,512]{1,0:T(8,128)(2,1)S(1)} %get-tuple-element.27.pick_hbm, bf16[512,640]{1,0:T(8,128)(2,1)S(1)} %get-tuple-element.28.put_hbm, f32[512,128]{1,0:T(8,128)S(1)} %get-tuple-element.29.gate_hbm, ...), custom_call_target="tpu_custom_call" | custom-call | flops 1000000 | bytes 10000 | tf_op jit(solution)/shard_map/own_out/pallas_call | solution.py:407
  69.2 4.2 %own_grad.1.refs_11_.refs_10_ = bf16[320,1024]{1,0:T(8,128)(2,1)S(1)} custom-call(s32[11]{0:T(128)S(1)} %copy-done.6, bf16[640,512]{1,0:T(8,128)(2,1)S(1)} %get-tuple-element.27.pick_hbm, bf16[512,640]{1,0:T(8,128)(2,1)S(1)} %get-tuple-element.28.put_hbm, f32[512,128]{1,0:T(8,128)S(1)} %get-tuple-element.29.gate_hbm, bf16[128,1024]{1,0:T(8,128)(2,1)S(1)} %copy-done.1, ...), custom_call_target="tpu_custom_call" | custom-call | flops 5000999936 | bytes 10000 | tf_op jit(solution)/shard_map/own_grad/pallas_call | solution.py:407
  73.9 7.0 %other_out.1 = (bf16[128,1024]{1,0:T(8,128)(2,1)S(1)}, bf16[128,1024]{1,0:T(8,128)(2,1)S(1)}, bf16[128,1024]{1,0:T(8,128)(2,1)S(1)}, bf16[128,1024]{1,0:T(8,128)...) custom-call(s32[11]{0:T(128)S(1)} %copy-done.6, bf16[640,512]{1,0:T(8,128)(2,1)S(1)} %get-tuple-element.27.pick_hbm, ...), custom_call_target="tpu_custom_call" | custom-call | flops 1000000 | bytes 10000 | tf_op jit(solution)/shard_map/other_out/pallas_call | solution.py:407
  81.6 6.5 %other_grad.1 = (bf16[128,1024]{1,0:T(8,128)(2,1)S(1)}, bf16[128,1024]{1,0:T(8,128)(2,1)S(1)}, bf16[128,1024]{1,0:T(8,128)(2,1)S(1)}, bf16[256,1024]{1,0:T(8,128)(2,1)S(1)}) custom-call(s32[11]{0:T(128)S(1)} %copy-done.6, bf16[640,512]{1,0:T(8,128)(2,1)S(1)} %get-tuple-element.27.pick_hbm, bf16[512,640]{1,0:T(8,128)(2,1)S(1)} %get-tuple-element.28.put_hbm, ...), custom_call_target="tpu_custom_call" | custom-call | flops 6000999936 | bytes 10000 | tf_op jit(solution)/shard_map/other_grad/pallas_call | solution.py:407
  88.1 1.5 %collective-permute-start.21 = (bf16[128,1024]{1,0:T(8,128)(2,1)S(1)}, bf16[128,1024]{1,0:T(8,128)(2,1)S(1)}, u32[]{:S(2)}, u32[]{:S(2)}) collective-permute-start(bf16[128,1024]{1,0:T(8,128)(2,1)S(1)} %get-tuple-element.45), channel_id=1, source_target_pairs={{0,8},{1,9},{2,10},{3,11},{4,12},{5,13},{6,14},{7,15},{8,0},{9,1},... | collective-permute-start | bytes 786440 | tf_op jit(solution)/shard_map/ppermute | solution.py:492
  90.2 7.1 %collective-permute-done.21.refs_0_ = bf16[128,1024]{1,0:T(8,128)(2,1)S(1)} collective-permute-done((bf16[128,1024]{1,0:T(8,128)(2,1)S(1)}, bf16[128,1024]{1,0:T(8,128)(2,1)S(1)}, u32[]{:S(2)}, u32[]{:S(2)}) %collective-permute-start.21) | collective-permute-done | bytes 262176 | tf_op jit(solution)/shard_map/ppermute | solution.py:492
  97.4 2.5 %collective-permute-start.22 = (bf16[128,1024]{1,0:T(8,128)(2,1)S(1)}, bf16[128,1024]{1,0:T(8,128)(2,1)S(1)}, u32[]{:S(2)}, u32[]{:S(2)}) collective-permute-start(bf16[128,1024]{1,0:T(8,128)(2,1)S(1)} %add_convert_fusion), channel_id=1, source_target_pairs={{0,24},{1,25},{2,26},{3,27},{4,28},{5,29},{6,30},{7,31},{8,16},{9,... | collective-permute-start | bytes 786440 | tf_op jit(solution)/shard_map/ppermute | solution.py:492
  99.9 1.4 %collective-permute-start.20 = (bf16[128,1024]{1,0:T(8,128)(2,1)S(1)}, bf16[128,1024]{1,0:T(8,128)(2,1)S(1)}, u32[]{:S(2)}, u32[]{:S(2)}) collective-permute-start(bf16[128,1024]{1,0:T(8,128)(2,1)S(1)} %add_convert_fusion.1.refs_1_), channel_id=1, source_target_pairs={{0,24},{1,25},{2,26},{3,27},{4,28},{5,29},{6,30},{7,31},{8,16},{9,... | collective-permute-start | bytes 786440 | tf_op jit(solution)/shard_map/ppermute | solution.py:492
  101.3 6.2 %collective-permute-done.18.beside_ref = bf16[256,1024]{1,0:T(8,128)(2,1)S(1)} collective-permute-done((bf16[256,1024]{1,0:T(8,128)(2,1)S(1)}, bf16[256,1024]{1,0:T(8,128)(2,1)S(1)}, u32[]{:S(2)}, u32[]{:S(2)}) %collective-permute-start.18) | collective-permute-done | bytes 524320 | tf_op jit(solution)/shard_map/ppermute | solution.py:492
  107.5 8.6 %collective-permute-done.22.merged_ref = bf16[128,1024]{1,0:T(8,128)(2,1)S(1)} collective-permute-done((bf16[128,1024]{1,0:T(8,128)(2,1)S(1)}, bf16[128,1024]{1,0:T(8,128)(2,1)S(1)}, u32[]{:S(2)}, u32[]{:S(2)}) %collective-permute-start.22) | collective-permute-done | bytes 262176 | tf_op jit(solution)/shard_map/ppermute | solution.py:492
  116.1 1.0 grad_sum.1
  117.1 3.5 %collective-permute-done.20.merged_ref = bf16[128,1024]{1,0:T(8,128)(2,1)S(1)} collective-permute-done((bf16[128,1024]{1,0:T(8,128)(2,1)S(1)}, bf16[128,1024]{1,0:T(8,128)(2,1)S(1)}, u32[]{:S(2)}, u32[]{:S(2)}) %collective-permute-start.20) | collective-permute-done | bytes 262176 | tf_op jit(solution)/shard_map/ppermute | solution.py:492
  120.6 0.8 out_sum.1
  (70 shorter events, 7.4 us)
Async XLA Ops:
  0.6 10.4 %collective-permute-start.1 = (bf16[128,1024]{1,0:T(8,128)(2,1)}, bf16[128,1024]{1,0:T(8,128)(2,1)S(1)}, u32[]{:S(2)}, u32[]{:S(2)}) collective-permute-start(bf16[128,1024]{1,0:T(8,128)(2,1)} %refs_0_.3), channel_id=1, source_target_pairs={{0,2},{1,3},{2,0},{3,1},{4,6},{5,7},{6,4},{7,5},{8,10},{9,11},{10,... | collective-permute-start | bytes 786440 | tf_op jit(solution)/shard_map/ppermute | solution.py:492
  3.6 14.0 %collective-permute-start = (bf16[128,1024]{1,0:T(8,128)(2,1)}, bf16[128,1024]{1,0:T(8,128)(2,1)S(1)}, u32[]{:S(2)}, u32[]{:S(2)}) collective-permute-start(bf16[128,1024]{1,0:T(8,128)(2,1)} %refs_0_.3), channel_id=1, source_target_pairs={{0,1},{1,0},{2,3},{3,2},{4,5},{5,4},{6,7},{7,6},{8,9},{9,8},{10,11... | collective-permute-start | bytes 786440 | tf_op jit(solution)/shard_map/ppermute | solution.py:492
  3.6 12.1 %collective-permute-start.4 = (bf16[128,1024]{1,0:T(8,128)(2,1)}, bf16[128,1024]{1,0:T(8,128)(2,1)S(1)}, u32[]{:S(2)}, u32[]{:S(2)}) collective-permute-start(bf16[128,1024]{1,0:T(8,128)(2,1)} %refs_4_.1), channel_id=1, source_target_pairs={{0,2},{1,3},{2,0},{3,1},{4,6},{5,7},{6,4},{7,5},{8,10},{9,11},{10,... | collective-permute-start | bytes 786440 | tf_op jit(solution)/shard_map/ppermute | solution.py:492
  3.8 15.5 %collective-permute-start.3 = (bf16[128,1024]{1,0:T(8,128)(2,1)}, bf16[128,1024]{1,0:T(8,128)(2,1)}, u32[]{:S(2)}, u32[]{:S(2)}) collective-permute-start(bf16[128,1024]{1,0:T(8,128)(2,1)} %refs_4_.1), channel_id=1, source_target_pairs={{0,1},{1,0},{2,3},{3,2},{4,5},{5,4},{6,7},{7,6},{8,9},{9,8},{10,11... | collective-permute-start | bytes 786440 | tf_op jit(solution)/shard_map/ppermute | solution.py:492
  7.7 9.9 %copy-start.13 = (f32[128,4]{0,1:T(4,128)S(1)}, f32[128,4]{0,1:T(4,128)}, u32[]{:S(2)}) copy-start(f32[128,4]{0,1:T(4,128)} %param.18) | copy-start | bytes 6148
  7.7 9.9 %copy-start = (bf16[128,1024]{1,0:T(8,128)(2,1)S(1)}, bf16[128,1024]{1,0:T(8,128)(2,1)}, u32[]{:S(2)}) copy-start(bf16[128,1024]{1,0:T(8,128)(2,1)} %cot_ref.1) | copy-start | bytes 786436
  7.7 14.1 %copy-start.12 = (s32[128,4]{0,1:T(4,128)S(1)}, s32[128,4]{0,1:T(4,128)}, u32[]{:S(2)}) copy-start(s32[128,4]{0,1:T(4,128)} %param.17) | copy-start | bytes 6148
  7.7 28.9 %collective-permute-start.12 = (bf16[2,3,128,512]{3,2,1,0:T(8,128)(2,1)}, bf16[2,3,128,512]{3,2,1,0:T(8,128)(2,1)S(1)}, u32[]{:S(2)}, u32[]{:S(2)}) collective-permute-start(bf16[2,3,128,512]{3,2,1,0:T(8,128)(2,1)} %split_pieces.2), channel_id=1, source_target_pairs={{0,4},{1,5},{2,6},{3,7},{4,0},{5,1},{6,2},{7,3},{8,12},{9,13},{10,... | collective-permute-start | bytes 2359304 | tf_op jit(solution)/shard_map/ppermute | solution.py:492
  11.0 10.8 %collective-permute-start.2 = (bf16[128,1024]{1,0:T(8,128)(2,1)S(1)}, bf16[128,1024]{1,0:T(8,128)(2,1)}, u32[]{:S(2)}, u32[]{:S(2)}) collective-permute-start(bf16[128,1024]{1,0:T(8,128)(2,1)S(1)} %collective-permute-done.1.refs_2_.refs_0_), channel_id=1, source_target_pairs={{0,1},{1,0},{2,3},{3,2},{4,5},{5,4},{6,7},{7,6},{8,9},{9,8},{10,11... | collective-permute-start | bytes 786440 | tf_op jit(solution)/shard_map/ppermute | solution.py:492
  15.8 7.5 %copy-start.10 = (bf16[128,1024]{1,0:T(8,128)(2,1)}, bf16[128,1024]{1,0:T(8,128)(2,1)S(1)}, u32[]{:S(2)}) copy-start(bf16[128,1024]{1,0:T(8,128)(2,1)S(1)} %collective-permute-done.4.refs_6_) | copy-start | bytes 786436
  15.8 52.4 %collective-permute-start.14 = (bf16[2,3,256,512]{3,2,1,0:T(8,128)(2,1)}, bf16[2,3,256,512]{3,2,1,0:T(8,128)(2,1)S(1)}, u32[]{:S(2)}, u32[]{:S(2)}) collective-permute-start(bf16[2,3,256,512]{3,2,1,0:T(8,128)(2,1)} %split_pieces.3), channel_id=1, source_target_pairs={{0,4},{1,5},{2,6},{3,7},{4,0},{5,1},{6,2},{7,3},{8,12},{9,13},{10,... | collective-permute-start | bytes 4718600 | tf_op jit(solution)/shard_map/ppermute | solution.py:492
  17.6 12.7 %collective-permute-start.7 = (bf16[128,1024]{1,0:T(8,128)(2,1)S(1)}, bf16[128,1024]{1,0:T(8,128)(2,1)S(1)}, u32[]{:S(2)}, u32[]{:S(2)}) collective-permute-start(bf16[128,1024]{1,0:T(8,128)(2,1)S(1)} %copy-done), channel_id=1, source_target_pairs={{0,8},{1,9},{2,10},{3,11},{4,12},{5,13},{6,14},{7,15},{8,0},{9,1},... | collective-permute-start | bytes 786440 | tf_op jit(solution)/shard_map/ppermute | solution.py:492
  19.3 13.9 %collective-permute-start.6 = (bf16[128,1024]{1,0:T(8,128)(2,1)S(1)}, bf16[128,1024]{1,0:T(8,128)(2,1)S(1)}, u32[]{:S(2)}, u32[]{:S(2)}) collective-permute-start(bf16[128,1024]{1,0:T(8,128)(2,1)S(1)} %copy-done), channel_id=1, source_target_pairs={{0,24},{1,25},{2,26},{3,27},{4,28},{5,29},{6,30},{7,31},{8,16},{9,... | collective-permute-start | bytes 786440 | tf_op jit(solution)/shard_map/ppermute | solution.py:492
  21.8 1.5 %collective-permute-start.5 = (bf16[128,1024]{1,0:T(8,128)(2,1)S(1)}, bf16[128,1024]{1,0:T(8,128)(2,1)S(1)}, u32[]{:S(2)}, u32[]{:S(2)}) collective-permute-start(bf16[128,1024]{1,0:T(8,128)(2,1)S(1)} %collective-permute-done.4.refs_6_), channel_id=1, source_target_pairs={{0,1},{1,0},{2,3},{3,2},{4,5},{5,4},{6,7},{7,6},{8,9},{9,8},{10,11... | collective-permute-start | bytes 786440 | tf_op jit(solution)/shard_map/ppermute | solution.py:492
  33.2 15.3 %collective-permute-start.9 = (bf16[144,1024]{1,0:T(8,128)(2,1)}, bf16[144,1024]{1,0:T(8,128)(2,1)S(1)}, u32[]{:S(2)}, u32[]{:S(2)}) collective-permute-start(bf16[144,1024]{1,0:T(8,128)(2,1)} %after.6._.refs_1_.refs_0_), channel_id=1, source_target_pairs={{0,24},{1,25},{2,26},{3,27},{4,28},{5,29},{6,30},{7,31},{8,16},{9,... | collective-permute-start | bytes 884744 | tf_op jit(solution)/shard_map/ppermute | solution.py:492
  34.7 13.8 %collective-permute-start.10 = (bf16[128,1024]{1,0:T(8,128)(2,1)S(1)}, bf16[128,1024]{1,0:T(8,128)(2,1)S(1)}, u32[]{:S(2)}, u32[]{:S(2)}) collective-permute-start(bf16[128,1024]{1,0:T(8,128)(2,1)S(1)} %after.7.refs_2_), channel_id=1, source_target_pairs={{0,8},{1,9},{2,10},{3,11},{4,12},{5,13},{6,14},{7,15},{8,0},{9,1},... | collective-permute-start | bytes 786440 | tf_op jit(solution)/shard_map/ppermute | solution.py:492
  36.6 23.4 %copy-start.6 = (s32[11]{0:T(128)S(1)}, s32[11]{0:T(128)}, u32[]{:S(2)}) copy-start(s32[11]{0:T(128)} %stack.37.where_ref.table_ref.start_ref) | copy-start | bytes 136
  36.6 31.6 %collective-permute-start.15 = (bf16[2,3,128,512]{3,2,1,0:T(8,128)(2,1)S(1)}, bf16[2,3,128,512]{3,2,1,0:T(8,128)(2,1)S(1)}, u32[]{:S(2)}, u32[]{:S(2)}) collective-permute-start(bf16[2,3,128,512]{3,2,1,0:T(8,128)(2,1)S(1)} %after.9.refs_4_), channel_id=1, source_target_pairs={{0,2},{1,3},{2,0},{3,1},{4,6},{5,7},{6,4},{7,5},{8,10},{9,11},{10,... | collective-permute-start | bytes 2359304 | tf_op jit(solution)/shard_map/ppermute | solution.py:492
  46.7 10.2 %collective-permute-start.8 = (bf16[144,1024]{1,0:T(8,128)(2,1)}, bf16[144,1024]{1,0:T(8,128)(2,1)S(1)}, u32[]{:S(2)}, u32[]{:S(2)}) collective-permute-start(bf16[144,1024]{1,0:T(8,128)(2,1)} %after.6._.refs_1_.refs_0_), channel_id=1, source_target_pairs={{0,8},{1,9},{2,10},{3,11},{4,12},{5,13},{6,14},{7,15},{8,0},{9,1},... | collective-permute-start | bytes 884744 | tf_op jit(solution)/shard_map/ppermute | solution.py:492
  49.2 10.8 %collective-permute-start.11 = (bf16[144,1024]{1,0:T(8,128)(2,1)S(1)}, bf16[144,1024]{1,0:T(8,128)(2,1)S(1)}, u32[]{:S(2)}, u32[]{:S(2)}) collective-permute-start(bf16[144,1024]{1,0:T(8,128)(2,1)S(1)} %after.8.refs_2_), channel_id=1, source_target_pairs={{0,8},{1,9},{2,10},{3,11},{4,12},{5,13},{6,14},{7,15},{8,0},{9,1},... | collective-permute-start | bytes 884744 | tf_op jit(solution)/shard_map/ppermute | solution.py:492
  61.9 7.0 %slice-start = ((s8[6291456]{0:T(1024)(128)(4,1)}), s8[4194304]{0:T(1024)(128)(4,1)S(1)}, s32[]{:S(2)}) async-start(s8[6291456]{0:T(1024)(128)(4,1)} %bitcast.19), calls=%async_computation | async-start | bytes 8388608
  61.9 7.0 %slice-start.1 = ((s8[6291456]{0:T(1024)(128)(4,1)}), s8[2097152]{0:T(1024)(128)(4,1)S(1)}, s32[]{:S(2)}) async-start(s8[6291456]{0:T(1024)(128)(4,1)} %bitcast.19), calls=%async_computation.1 | async-start | bytes 4194304
  68.2 5.7 %collective-permute-start.16 = (bf16[2,3,256,512]{3,2,1,0:T(8,128)(2,1)S(1)}, bf16[2,3,256,512]{3,2,1,0:T(8,128)(2,1)S(1)}, u32[]{:S(2)}, u32[]{:S(2)}) collective-permute-start(bf16[2,3,256,512]{3,2,1,0:T(8,128)(2,1)S(1)} %get-tuple-element.32.refs_6_), channel_id=1, source_target_pairs={{0,1},{1,0},{2,3},{3,2},{4,5},{5,4},{6,7},{7,6},{8,9},{9,8},{10,11... | collective-permute-start | bytes 4718600 | tf_op jit(solution)/shard_map/ppermute | solution.py:492
  68.3 5.1 %collective-permute-start.13 = (bf16[2,3,128,512]{3,2,1,0:T(8,128)(2,1)S(1)}, bf16[2,3,128,512]{3,2,1,0:T(8,128)(2,1)S(1)}, u32[]{:S(2)}, u32[]{:S(2)}) collective-permute-start(bf16[2,3,128,512]{3,2,1,0:T(8,128)(2,1)S(1)} %after.9.refs_4_), channel_id=1, source_target_pairs={{0,1},{1,0},{2,3},{3,2},{4,5},{5,4},{6,7},{7,6},{8,9},{9,8},{10,11... | collective-permute-start | bytes 2359304 | tf_op jit(solution)/shard_map/ppermute | solution.py:492
  68.8 5.1 %collective-permute-start.17 = (bf16[2,3,128,512]{3,2,1,0:T(8,128)(2,1)S(1)}, bf16[2,3,128,512]{3,2,1,0:T(8,128)(2,1)S(1)}, u32[]{:S(2)}, u32[]{:S(2)}) collective-permute-start(bf16[2,3,128,512]{3,2,1,0:T(8,128)(2,1)S(1)} %get-tuple-element.33.refs_8_), channel_id=1, source_target_pairs={{0,1},{1,0},{2,3},{3,2},{4,5},{5,4},{6,7},{7,6},{8,9},{9,8},{10,11... | collective-permute-start | bytes 2359304 | tf_op jit(solution)/shard_map/ppermute | solution.py:492
  80.9 9.2 %collective-permute-start.19 = (bf16[128,1024]{1,0:T(8,128)(2,1)S(1)}, bf16[128,1024]{1,0:T(8,128)(2,1)S(1)}, u32[]{:S(2)}, u32[]{:S(2)}) collective-permute-start(bf16[128,1024]{1,0:T(8,128)(2,1)S(1)} %get-tuple-element.42), channel_id=1, source_target_pairs={{0,8},{1,9},{2,10},{3,11},{4,12},{5,13},{6,14},{7,15},{8,0},{9,1},... | collective-permute-start | bytes 786440 | tf_op jit(solution)/shard_map/ppermute | solution.py:492
  88.0 28.0 %copy-start.2 = (bf16[128,1024]{1,0:T(8,128)(2,1)S(1)}, bf16[128,1024]{1,0:T(8,128)(2,1)}, u32[]{:S(2)}) copy-start(bf16[128,1024]{1,0:T(8,128)(2,1)} %get-tuple-element.24.mix_ref) | copy-start | bytes 786436
  88.0 28.0 %copy-start.5 = (f32[1024]{0:T(1024)S(1)}, f32[1024]{0:T(1024)}, u32[]{:S(2)}) copy-start(f32[1024]{0:T(1024)} %param.15) | copy-start | bytes 12292
  88.1 9.3 %collective-permute-start.21 = (bf16[128,1024]{1,0:T(8,128)(2,1)S(1)}, bf16[128,1024]{1,0:T(8,128)(2,1)S(1)}, u32[]{:S(2)}, u32[]{:S(2)}) collective-permute-start(bf16[128,1024]{1,0:T(8,128)(2,1)S(1)} %get-tuple-element.45), channel_id=1, source_target_pairs={{0,8},{1,9},{2,10},{3,11},{4,12},{5,13},{6,14},{7,15},{8,0},{9,1},... | collective-permute-start | bytes 786440 | tf_op jit(solution)/shard_map/ppermute | solution.py:492
  89.6 17.9 %collective-permute-start.18 = (bf16[256,1024]{1,0:T(8,128)(2,1)S(1)}, bf16[256,1024]{1,0:T(8,128)(2,1)S(1)}, u32[]{:S(2)}, u32[]{:S(2)}) collective-permute-start(bf16[256,1024]{1,0:T(8,128)(2,1)S(1)} %get-tuple-element.40), channel_id=1, source_target_pairs={{0,8},{1,9},{2,10},{3,11},{4,12},{5,13},{6,14},{7,15},{8,0},{9,1},... | collective-permute-start | bytes 1572872 | tf_op jit(solution)/shard_map/ppermute | solution.py:492
  97.4 18.7 %collective-permute-start.22 = (bf16[128,1024]{1,0:T(8,128)(2,1)S(1)}, bf16[128,1024]{1,0:T(8,128)(2,1)S(1)}, u32[]{:S(2)}, u32[]{:S(2)}) collective-permute-start(bf16[128,1024]{1,0:T(8,128)(2,1)S(1)} %add_convert_fusion), channel_id=1, source_target_pairs={{0,24},{1,25},{2,26},{3,27},{4,28},{5,29},{6,30},{7,31},{8,16},{9,... | collective-permute-start | bytes 786440 | tf_op jit(solution)/shard_map/ppermute | solution.py:492
  99.9 20.7 %collective-permute-start.20 = (bf16[128,1024]{1,0:T(8,128)(2,1)S(1)}, bf16[128,1024]{1,0:T(8,128)(2,1)S(1)}, u32[]{:S(2)}, u32[]{:S(2)}) collective-permute-start(bf16[128,1024]{1,0:T(8,128)(2,1)S(1)} %add_convert_fusion.1.refs_1_), channel_id=1, source_target_pairs={{0,24},{1,25},{2,26},{3,27},{4,28},{5,29},{6,30},{7,31},{8,16},{9,... | collective-permute-start | bytes 786440 | tf_op jit(solution)/shard_map/ppermute | solution.py:492
  (7 other events, 16.0 us)
